TPU v7x, 512 devices: a whole 4x8x8 slice. The times are simulated.
512 devices in a mesh: space: 32 (over y_hi, x, core), chan: 16 (over y_lo, z).
Axes of the slice: x: 4, y: 8 (y_hi: 4, y_lo: 2; y = y_hi * 2 + y_lo), z: 8, core: 2. Of those that a mesh axis runs over, the one named last changes fastest.
Arguments:
- field: bfloat16 [256, 64, 4, 128], P('chan', 'space'), may hold values from -6 to 6
- filters: bfloat16 [27, 256, 256], P(None, 'chan'), may hold values from -0.078125 to 0.078125
- cotangent: bfloat16 [256, 64, 4, 128], P('chan', 'space'), may hold values from -6 to 6
Outputs:
- out_field: bfloat16 [256, 64, 4, 128], P('chan', 'space')
- input_grad: bfloat16 [256, 64, 4, 128], P('chan', 'space')
- weight_grad: float32 [27, 256, 256], P(None, 'chan')
All inputs are finite; a program needn't handle non-finite values.
Results may differ from a plain program's by a relative error of at most 0.001.
Values may be sent and summed in bfloat16 or wider, within the bound.
No kernel may reach another device: no remote copies, remote signals or barrier semaphores. Data moves between devices by JAX's collectives and lax.ppermute only.
A program may use at most 128 MiB of HBM per device.

v0:
```python
import math

import jax
import jax.numpy as jnp
from jax import lax
from jax.sharding import PartitionSpec as P


def padded_2(cells, sides, width):
    for axis, dim in sides:
        count = lax.axis_size(axis)
        ends = count - 1
        head = lax.slice_in_dim(cells, 0, width, axis=dim)
        tail = lax.slice_in_dim(cells, cells.shape[dim] - width, cells.shape[dim], axis=dim)
        cells = jnp.concatenate(
            [
                lax.ppermute(tail, axis, [(i, (i + 1) % count) for i in range(ends)]),
                cells,
                lax.ppermute(head, axis, [((i + 1) % count, i) for i in range(ends)]),
            ],
            axis=dim,
        )
    return cells


def per_device(field, filters, cotangent):
    local_ch, local_rows, planes, extent = field.shape
    total_ch = filters.shape[2]
    cell_count = local_rows * planes * extent
    scale = 1.0 / math.sqrt(local_rows * lax.axis_size("space") * planes * extent)
    side_pads = ((0, 0), (0, 0), (2, 2), (2, 2))
    flat_cot = cotangent.reshape(local_ch, cell_count)
    rimmed_field = padded_2(field, (("space", 1),), 2)
    piece = lax.all_gather(rimmed_field, "chan", axis=0, tiled=True)
    output_sum = jnp.zeros((local_ch, cell_count), jnp.float32)
    piece_ch = piece.shape[0]
    padded = jnp.pad(piece, side_pads)
    blocks = []
    for forward_k in range(27):
        a, b, c = (forward_k // 9, forward_k // 3 % 3, forward_k % 3)
        window = padded[
            :, 2 * a : 2 * a + local_rows, 2 * b : 2 * b + planes, 2 * c : 2 * c + extent
        ].reshape(piece_ch, cell_count)
        weights_now = filters[forward_k]
        output_sum = output_sum + jnp.dot(weights_now, window, preferred_element_type=jnp.float32)
        blocks.append(
            lax.dot_general(
                flat_cot, window, (((1,), (1,)), ((), ())), preferred_element_type=jnp.float32
            )
        )
    filter_sum = jnp.stack(blocks)
    output_sum, filter_sum = (output_sum, filter_sum)
    weight_grad = lax.psum(filter_sum, "space") * scale

    def adjoint_window(padded, k):
        a, b, c = (k // 9, k // 3 % 3, k % 3)
        return padded[
            :,
            4 - 2 * a : 4 - 2 * a + local_rows,
            4 - 2 * b : 4 - 2 * b + planes,
            4 - 2 * c : 4 - 2 * c + extent,
        ].reshape(padded.shape[0], cell_count)

    rimmed_cot = padded_2(cotangent, (("space", 1),), 2)
    padded_cot = jnp.pad(rimmed_cot, side_pads)
    columns = jnp.concatenate([adjoint_window(padded_cot, k) for k in range(27)], axis=0)
    stacked = filters.reshape(27 * local_ch, total_ch)
    adjoint_sum = lax.psum_scatter(
        lax.dot_general(
            stacked, columns, (((0,), (0,)), ((), ())), preferred_element_type=jnp.float32
        ),
        "chan",
        scatter_dimension=0,
        tiled=True,
    )
    out_field = output_sum.astype(jnp.bfloat16).reshape(local_ch, local_rows, planes, extent)
    input_grad = adjoint_sum.astype(jnp.bfloat16).reshape(local_ch, local_rows, planes, extent)
    return (out_field, input_grad, weight_grad)


def solution(mesh):
    placed = (P("chan", "space", None, None), P(None, "chan", None), P("chan", "space", None, None))
    return jax.shard_map(
        per_device,
        mesh=mesh,
        in_specs=placed,
        out_specs=(
            P("chan", "space", None, None),
            P("chan", "space", None, None),
            P(None, "chan", None),
        ),
        check_vma=False,
    )
```

profile of v0, /device:TPU:1, one launch (start us, length us, event | category | flops | bytes accessed | tf_op | source)
XLA Modules:
  0.0 554.9 jit_solution(4969142857759135054)
XLA Ops:
  7.2 8.8 %collective-permute-start.3 = (bf16[16,2,4,128]{3,2,1,0:T(4,128)(2,1)}, bf16[16,2,4,128]{3,2,1,0:T(4,128)(2,1)S(1)}, u32[]{:S(2)}, u32[]{:S(2)}) collective-permute-start(bf16[16,2,4,128]{3,2,1,0:T(4,128)(2,1)} %param.5), channel_id=1, source_target_pairs={{16,0},{32,16},{48,32},{64,48},{80,64},{96,80},{112,96},{128,112},... | collective-permute-start | bytes 98312 | tf_op jit(solution)/shard_map/ppermute | solution.py:19
  16.0 1.9 collective-permute-start.2
  19.3 1.0 select_maximum_fusion
  22.4 1.3 copy.180
  23.9 2.1 collective-permute-start.1
  25.9 3.9 collective-permute-start
  29.9 1.0 collective-permute-done
  31.6 61.1 %reduce-scatter.4.cloned.1.call-done = f32[16,1024]{1,0:T(8,128)} async-done(((f32[256,1024]{1,0:T(8,128)}), f32[16,1024]{1,0:T(8,128)}) %reduce-scatter.4.cloned.1.call-update) | async-done | bytes 65552
  92.7 1.0 copy.181
  94.5 69.6 %all-gather.2.cloned.1.call-done = bf16[256,6,4,128]{3,0,2,1:T(8,128)(2,1)} async-done(((bf16[16,6,4,128]{3,0,2,1:T(8,128)(2,1)}), bf16[256,6,4,128]{3,0,2,1:T(8,128)(2,1)}) %all-gather.2.cloned.1.call-update) | async-done | bytes 1572880 | tf_op jit(solution)/shard_map/all_gather | solution.py:34
  164.0 4.2 pad_slice_fusion.1
  168.2 2.1 copy.98
  170.3 1.9 fusion.38
  172.2 1.3 fusion.71
  173.5 4.9 pad_slice_fusion
  178.4 2.1 copy.99
  180.5 2.1 copy.100
  182.5 2.0 copy.101
  184.6 2.0 copy.102
  186.6 2.1 copy.103
  188.7 2.1 copy.104
  190.7 2.1 copy.105
  192.8 2.1 copy.106
  194.8 2.1 copy.107
  196.9 2.0 copy.108
  198.9 2.0 copy.109
  201.0 2.1 copy.110
  203.1 2.1 copy.111
  205.2 2.0 copy.112
  207.2 2.1 copy.113
  209.3 2.0 copy.114
  211.3 2.1 copy.115
  213.4 2.0 copy.116
  215.4 2.0 copy.117
  217.4 2.1 copy.118
  219.5 2.0 copy.119
  221.5 2.1 copy.120
  223.6 1.0 copy.121
  224.6 1.0 copy.122
  225.6 1.0 copy.123
  226.6 2.0 copy.124
  228.7 2.0 fusion.37
  230.7 2.0 fusion.36
  232.6 2.0 fusion.35
  235.5 0.9 fusion.34
  236.3 0.9 fusion.33
  237.2 0.9 fusion.32
  238.0 0.9 fusion.31
  238.9 0.9 fusion.30
  239.8 0.9 fusion.29
  240.6 0.9 fusion.28
  241.5 0.9 fusion.27
  243.2 0.9 fusion.26
  244.1 0.9 fusion.25
  244.9 0.9 fusion.24
  245.8 0.9 fusion.23
  246.7 0.9 fusion.22
  247.5 0.9 fusion.21
  248.4 0.9 fusion.20
  249.2 0.9 fusion.19
  251.8 0.9 fusion.17
  253.5 0.9 fusion.15
  261.8 284.8 %all-reduce.4.cloned.1.call-done = f32[27,16,256]{2,1,0:T(8,128)} async-done(((f32[27,16,256]{2,1,0:T(8,128)}), f32[27,16,256]{2,1,0:T(8,128)}) %all-reduce.4.cloned.1.call-update) | async-done | bytes 442384 | tf_op jit(solution)/shard_map/psum | solution.py:53
  546.6 1.8 broadcast_multiply_fusion
  (195 shorter events, 16.3 us)
Async XLA Ops:
  7.2 85.5 %reduce-scatter.4.cloned.1.call-start = ((), (), s32[]{:S(2)}) async-start(), calls=%async_computation.3 | async-start | bytes 1114112
  7.2 11.5 %collective-permute-start.3 = (bf16[16,2,4,128]{3,2,1,0:T(4,128)(2,1)}, bf16[16,2,4,128]{3,2,1,0:T(4,128)(2,1)S(1)}, u32[]{:S(2)}, u32[]{:S(2)}) collective-permute-start(bf16[16,2,4,128]{3,2,1,0:T(4,128)(2,1)} %param.5), channel_id=1, source_target_pairs={{16,0},{32,16},{48,32},{64,48},{80,64},{96,80},{112,96},{128,112},... | collective-permute-start | bytes 98312 | tf_op jit(solution)/shard_map/ppermute | solution.py:19
  16.0 3.3 collective-permute-start.2
  21.0 0.9 copy-start.45
  22.4 1.4 copy-start.46
  23.8 140.2 %all-gather.2.cloned.1.call-start = ((), (), s32[]{:S(2)}) async-start(), calls=%async_computation.1 | async-start | bytes 1671168 | tf_op jit(solution)/shard_map/all_gather | solution.py:34
  23.9 6.0 %collective-permute-start.1 = (bf16[16,2,4,128]{3,0,2,1:T(8,128)(2,1)S(1)}, bf16[16,2,4,128]{3,0,2,1:T(8,128)(2,1)S(1)}, u32[]{:S(2)}, u32[]{:S(2)}) collective-permute-start(bf16[16,2,4,128]{3,0,2,1:T(8,128)(2,1)S(1)} %copy.95), channel_id=1, source_target_pairs={{16,0},{32,16},{48,32},{64,48},{80,64},{96,80},{112,96},{128,112},... | collective-permute-start | bytes 98312 | tf_op jit(solution)/shard_map/ppermute | solution.py:19
  25.9 4.9 collective-permute-start
  31.5 515.1 %all-reduce.4.cloned.1.call-start = ((), (), s32[]{:S(2)}) async-start(), calls=%async_computation.2 | async-start | bytes 884736 | tf_op jit(solution)/shard_map/psum | solution.py:53
  94.5 75.9 %copy-start.1 = (bf16[16,2,4,128]{3,2,1,0:T(4,128)(2,1)S(1)}, bf16[16,2,4,128]{3,2,1,0:T(4,128)(2,1)}, u32[]{:S(2)}) copy-start(bf16[16,2,4,128]{3,2,1,0:T(4,128)(2,1)} %param.5) | copy-start | bytes 98308
  168.2 5.3 copy-start
  228.7 6.8 %copy-start.18 = (bf16[256,2,4,128]{3,0,2,1:T(8,128)(2,1)S(1)}, bf16[256,2,4,128]{3,0,2,1:T(8,128)(2,1)}, u32[]{:S(2)}) copy-start(bf16[256,2,4,128]{3,0,2,1:T(8,128)(2,1)} %get-tuple-element.16) | copy-start | bytes 1572868
  228.7 7.6 %copy-start.17 = (bf16[256,2,4,128]{3,0,2,1:T(8,128)(2,1)S(1)}, bf16[256,2,4,128]{3,0,2,1:T(8,128)(2,1)}, u32[]{:S(2)}) copy-start(bf16[256,2,4,128]{3,0,2,1:T(8,128)(2,1)} %get-tuple-element.17) | copy-start | bytes 1572868
  230.7 6.5 %copy-start.16 = (bf16[256,2,4,128]{3,0,2,1:T(8,128)(2,1)S(1)}, bf16[256,2,4,128]{3,0,2,1:T(8,128)(2,1)}, u32[]{:S(2)}) copy-start(bf16[256,2,4,128]{3,0,2,1:T(8,128)(2,1)} %get-tuple-element.18) | copy-start | bytes 1572868
  232.6 5.4 copy-start.15
  234.6 4.3 copy-start.14
  235.4 4.3 copy-start.13
  236.3 4.3 copy-start.12
  237.2 4.3 copy-start.11
  238.9 4.3 copy-start.10
  239.8 4.3 copy-start.9
  240.6 4.3 copy-start.8
  241.5 4.3 copy-start.7
  242.3 4.3 copy-start.6
  243.2 4.3 copy-start.5
  244.1 4.3 copy-start.4
  244.9 4.3 copy-start.2
  249.2 4.3 copy-start.3
  251.0 3.5 copy-start.44
  251.0 3.7 copy-start.43
  252.7 2.3 copy-start.42
  253.5 1.7 copy-start.41
  254.4 1.1 copy-start.40
  254.4 1.3 copy-start.39
  254.7 1.3 copy-start.38
  254.9 1.3 copy-start.37
  255.2 1.3 copy-start.36
  255.5 1.3 copy-start.35
  255.7 1.3 copy-start.34
  256.0 1.3 copy-start.33
  256.2 1.3 copy-start.32
  256.5 1.3 copy-start.31
  256.8 1.3 copy-start.30
  257.0 1.3 copy-start.29
  257.3 1.3 copy-start.28
  257.5 1.3 copy-start.27
  257.8 1.3 copy-start.26
  258.0 1.3 copy-start.25
  258.3 1.3 copy-start.24
  258.6 1.3 copy-start.23
  258.8 1.3 copy-start.22
  259.1 1.3 copy-start.21
  259.3 1.3 copy-start.20
  259.6 1.3 copy-start.19
Sparse Core Ops, SparseCore 0:
  23.9 68.7 reduce-scatter.3
  95.5 68.5 all-gather.1
  254.5 291.9 all-reduce.3
where the time goes:
time: 557 us; the launch traced here: 555 us
  waiting for transfers between devices  417 us (75%)
  local copies, waits for them, and re-layouts  67.3 us (12%)
  matrix products  35.8 us (6%)
  starting transfers between devices  16.8 us (3%)
  between operations  14.4 us (3%)
    psum x1, waiting for transfers between devices, per_device(): weight_grad = lax.psum(filter_sum, 'space') * scale  285 us
    all_gather x1, waiting for transfers between devices, per_device(): piece = lax.all_gather(rimmed_field, 'chan', axis=0, tiled=True)  69.6 us
    slice x29, local copies, waits for them, and re-layouts, per_device(): padded[:, 2 * a:2 * a + local_rows, 2 * b:2 * b + planes, 2 * c:2 * c + e...  61.5 us
    unnamed x4, waiting for transfers between devices  61.2 us
    dot_general x27, matrix products, per_device(): lax.dot_general(flat_cot, window, (((1,), (1,)), ((), ())), preferred_ele...  27.5 us
  transfers between devices with their start and end apart: 7, of which 5 were waited for; matrix products, arithmetic and copies ran while one was open for 2% of the time, Pallas kernels for 0%

commit v1 on v0

v1 whole, which is shorter than its diff:
```python
import functools
import math

import jax
import jax.numpy as jnp
from jax import lax
from jax.experimental import pallas as pl
from jax.experimental.pallas import tpu as pltpu
from jax.sharding import Mesh
from jax.sharding import PartitionSpec as P

BF = jnp.bfloat16
F32 = jnp.float32
VMEM = pl.BlockSpec(memory_space=pltpu.VMEM)
SMEM = pl.BlockSpec(memory_space=pltpu.SMEM)
TAPS = 27
OWN = 16
CELLS = 1024
ROWS = TAPS * OWN
WIDE = CELLS + 512
LIMIT = 48 * 1024 * 1024


def call(body, outs, ins, scratch=(), flops=0, moved=0):
    return pl.pallas_call(
        body,
        out_shape=outs,
        in_specs=ins,
        out_specs=[VMEM] * len(outs),
        scratch_shapes=list(scratch),
        compiler_params=pltpu.CompilerParams(vmem_limit_bytes=LIMIT),
        cost_estimate=pl.CostEstimate(flops=flops, bytes_accessed=moved, transcendentals=0),
    )


def shape(dims, kind):
    return jax.ShapeDtypeStruct(dims, kind)


def lanes(dims):
    return lax.broadcasted_iota(jnp.int32, dims, len(dims) - 1)


def moved_by(block, step):
    if step == 0:
        return block
    at = lanes(block.shape) + step
    turned = pltpu.roll(block, (-step) % 128, 1)
    return jnp.where((at >= 0) & (at < 128), turned, 0.0)


def pack_body(field, filters, out):
    own = field[...]
    for c in range(16):
        out[c, :, 0:CELLS] = own
    lane = lanes((OWN, 128))
    for g in range(4):
        parts = [jnp.zeros((OWN, 128), F32) for _ in range(16)]
        for j in range(8):
            k = 8 * g + j
            if k >= TAPS:
                break
            here = (lane >= 16 * j) & (lane < 16 * j + 16)
            for h in range(2):
                block = filters[k, :, 128 * h : 128 * h + 128].astype(F32)
                for q in range(8):
                    step = (16 * (j - q)) % 128
                    turned = block if step == 0 else pltpu.roll(block, step, 1)
                    parts[8 * h + q] = jnp.where(here, turned, parts[8 * h + q])
        for c in range(16):
            out[c, :, CELLS + 128 * g : CELLS + 128 * g + 128] = parts[c].astype(BF)


def taps_sum(products, a, sign):
    blocks = []
    for r in range(2):
        for z in range(4):
            total = None
            for c in range(3):
                column = None
                for b in range(3):
                    source = z + sign * 2 * (b - 1)
                    if source < 0 or source > 3:
                        continue
                    k = 9 * a + 3 * b + c
                    lane = 128 * (4 * r + source)
                    part = products[16 * k : 16 * k + 16, lane : lane + 128]
                    column = part if column is None else column + part
                column = moved_by(column, sign * 2 * (c - 1))
                total = column if total is None else total + column
            blocks.append(total)
    return blocks


def grad_body(core, gathered, below, own, above, keep, send, shifted):
    zero = jnp.zeros((OWN, 128), BF)
    for a, source in ((0, above), (1, own), (2, below)):
        for r in range(2):
            rolled = []
            for z in range(4):
                lane = 128 * (4 * r + z)
                block = source[:, lane : lane + 128].astype(F32)
                rolled.append([moved_by(block, -2 * (c - 1)).astype(BF) for c in range(3)])
            for z in range(4):
                for b in range(3):
                    at = z - 2 * (b - 1)
                    for c in range(3):
                        k = 9 * a + 3 * b + c
                        lane = 128 * (4 * r + z)
                        shifted[16 * k : 16 * k + 16, lane : lane + 128] = (
                            rolled[at][c] if 0 <= at < 4 else zero
                        )
    total = lax.dot_general(
        shifted[...],
        gathered[:, 0:CELLS],
        (((1,), (1,)), ((), ())),
        preferred_element_type=F32,
    )
    low, high = total[:, 0:128], total[:, 128:256]
    first = core[0] == 0
    keep[0:ROWS, :] = jnp.where(first, low, high)
    keep[ROWS:512, :] = jnp.zeros((512 - ROWS, 128), F32)
    send[...] = jnp.where(first, high, low)


def forward_body(gathered, filters, out, products):
    products[...] = jnp.dot(
        filters[...].reshape(ROWS, 256), gathered[:, 0:CELLS], preferred_element_type=F32
    )
    for a in range(3):
        for n, block in enumerate(taps_sum(products, a, 1)):
            out[a, :, 128 * n : 128 * n + 128] = block


def adjoint_body(gathered, cotangent, out, products):
    products[...] = lax.dot_general(
        gathered[:, CELLS : CELLS + ROWS],
        cotangent[...],
        (((0,), (0,)), ((), ())),
        preferred_element_type=F32,
    )
    for a in range(3):
        for n, block in enumerate(taps_sum(products, a, -1)):
            out[a, :, 128 * n : 128 * n + 128] = block


def per_device(field, filters, cotangent):
    scale = 1.0 / math.sqrt(32768)
    space = ("pair", "core")
    core = lax.axis_index("core").astype(jnp.int32).reshape(1)
    own_field = field.reshape(OWN, CELLS)
    own_cot = cotangent.reshape(OWN, CELLS)

    up = [(i, i + 1) for i in range(31)]
    down = [(i + 1, i) for i in range(31)]
    below = lax.ppermute(own_cot, space, up)
    above = lax.ppermute(own_cot, space, down)
    wide_cot = jnp.concatenate([own_cot, jnp.zeros_like(own_cot)], axis=0)
    all_cot = lax.all_gather(wide_cot, "chan", axis=0, tiled=False)[:, :OWN].reshape(256, CELLS)

    packed = call(pack_body, [shape((16, OWN, WIDE), BF)], [VMEM] * 2, moved=1 << 20)(
        own_field, filters
    )[0]
    gathered = lax.all_to_all(packed, "chan", 0, 0).reshape(256, WIDE)

    keep, send = call(
        grad_body,
        [shape((512, 128), F32), shape((ROWS, 128), F32)],
        [SMEM] + [VMEM] * 4,
        [pltpu.VMEM((ROWS, CELLS), BF)],
        flops=2 * ROWS * CELLS * 256,
        moved=1 << 20,
    )(core, gathered, below, own_cot, above)
    swapped = lax.ppermute(send, "core", [(0, 1), (1, 0)])
    ys = call(
        forward_body,
        [shape((3, OWN, CELLS), F32)],
        [VMEM] * 2,
        [pltpu.VMEM((ROWS, CELLS), F32)],
        flops=2 * ROWS * CELLS * 256,
        moved=1 << 20,
    )(gathered, filters)[0]
    half = keep + jnp.pad(swapped, ((0, 512 - ROWS), (0, 0)))
    parts = lax.all_to_all(half.reshape(16, 32, 128), "pair", 0, 0)
    mine = jnp.sum(parts, axis=0) * scale
    zs = call(
        adjoint_body,
        [shape((3, OWN, CELLS), F32)],
        [VMEM] * 2,
        [pltpu.VMEM((ROWS, CELLS), F32)],
        flops=2 * ROWS * CELLS * 256,
        moved=1 << 20,
    )(gathered, all_cot)[0]
    from_before = lax.ppermute(jnp.concatenate([ys[0], zs[2]], axis=0), space, up)
    from_after = lax.ppermute(jnp.concatenate([ys[2], zs[0]], axis=0), space, down)
    full = lax.all_to_all(jnp.broadcast_to(mine[None], (16, 32, 128)), "pair", 0, 0)
    full = full.reshape(512, 128)[:ROWS]
    other = lax.ppermute(full, "core", [(0, 1), (1, 0)])
    first = core[0] == 0
    weight_grad = jnp.concatenate(
        [jnp.where(first, full, other), jnp.where(first, other, full)], axis=1
    ).reshape(TAPS, OWN, 256)
    out_field = (ys[1] + from_before[:OWN] + from_after[:OWN]).astype(BF).reshape(field.shape)
    input_grad = (zs[1] + from_before[OWN:] + from_after[OWN:]).astype(BF).reshape(field.shape)
    return out_field, input_grad, weight_grad


def solution(mesh):
    fine = Mesh(mesh.devices.reshape(16, 2, 16), ("pair", "core", "chan"))
    cells = P("chan", ("pair", "core"), None, None)
    taps = P(None, "chan", None)
    return jax.shard_map(
        per_device,
        mesh=fine,
        in_specs=(cells, taps, cells),
        out_specs=(cells, cells, taps),
        check_vma=False,
    )
```

time: 557 us -> 135 us (0.24)
  waiting for transfers between devices: 417 us -> 45.8 us
  local copies, waits for them, and re-layouts: 67.3 us -> 5.47 us
  starting transfers between devices: 16.8 us -> 64.1 us
  matrix products: 35.8 us -> 0 us
    psum x1 -> x0, waiting for transfers between devices: 285 us -> none  [per_device(): weight_grad = lax.psum(filter_sum, 'space') * scale]
    unnamed x4 -> x1, waiting for transfers between devices: 61.2 us -> 0.02 us
    slice x31 -> x2, local copies, waits for them, and re-layouts: 62 us -> 1.1 us  [the longest x1 1.08 us: per_device(): lax.all_gather(wide_cot, 'chan', axis=0, tiled=False)[:, :OWN]]
    all_gather x1, waiting for transfers between devices: 69.6 us -> 31.8 us  [per_device(): lax.all_gather(wide_cot, 'chan', axis=0, tiled=False)[:, :OWN]]
    dot_general x55 -> x0, matrix products: 35.8 us -> none  [the longest x27 27.5 us: per_device(): lax.dot_general(flat_cot, window, (((1,), (1,)), ((), ())), preferred_ele...]
    all_to_all x0 -> x3, starting transfers between devices: none -> 29 us  [the longest x1 12.1 us: per_device(): gathered = lax.all_to_all(packed, 'chan', 0, 0).reshape(256, WIDE)]
    ppermute x4 -> x6, starting transfers between devices: 16.7 us -> 35.1 us  [the longest x1 13.6 us: per_device(): lax.ppermute(jnp.concatenate([ys[2], zs[0]], axis=0), space, down)]
    all_to_all x0 -> x3, waiting for transfers between devices: none -> 11.9 us  [the longest x1 11.9 us: per_device(): gathered = lax.all_to_all(packed, 'chan', 0, 0).reshape(256, WIDE)]
  transfers between devices with their start and end apart: 7 -> 10, of which waited for: 5 -> 4; matrix products, arithmetic and copies ran while one was open for 2% -> 3% of each run, Pallas kernels for 0% -> 1%
where the time goes in v1:
time: 135 us; the launch traced here: 134 us
  starting transfers between devices  64.1 us (47%)
  waiting for transfers between devices  45.8 us (34%)
  between operations  14.3 us (11%)
  local copies, waits for them, and re-layouts  5.47 us (4%)
  Pallas kernels  2.82 us (2%)
  other arithmetic  1.63 us (1%)
    all_gather x1, waiting for transfers between devices, per_device(): lax.all_gather(wide_cot, 'chan', axis=0, tiled=False)[:, :OWN]  31.8 us
    ppermute x1, starting transfers between devices, per_device(): lax.ppermute(jnp.concatenate([ys[2], zs[0]], axis=0), space, down)  13.6 us
    all_to_all x1, starting transfers between devices, per_device(): gathered = lax.all_to_all(packed, 'chan', 0, 0).reshape(256, WIDE)  12.1 us
    all_to_all x1, waiting for transfers between devices, per_device(): gathered = lax.all_to_all(packed, 'chan', 0, 0).reshape(256, WIDE)  11.9 us
    all_to_all x1, starting transfers between devices, per_device(): parts = lax.all_to_all(half.reshape(16, 32, 128), 'pair', 0, 0)  8.62 us
    all_to_all x1, starting transfers between devices, per_device(): lax.all_to_all(jnp.broadcast_to(mine[None], (16, 32, 128)), 'pair', 0, 0)  8.22 us
    ppermute x1, starting transfers between devices, per_device(): other = lax.ppermute(full, 'core', [(0, 1), (1, 0)])  7.65 us
    ppermute x1, starting transfers between devices, per_device(): swapped = lax.ppermute(send, 'core', [(0, 1), (1, 0)])  4.49 us
  transfers between devices with their start and end apart: 10, of which 4 were waited for; matrix products, arithmetic and copies ran while one was open for 3% of the time, Pallas kernels for 1%

profile of v1, /device:TPU:1, one launch (start us, length us, event | category | flops | bytes accessed | tf_op | source)
XLA Modules:
  0.0 134.1 jit_solution(7007646830612357579)
XLA Ops:
  7.2 0.8 reshape.39.field
  7.9 0.0 copy-start
  8.0 0.9 copy-done
  8.9 1.4 %shard_map.58 = bf16[16,16,1536]{2,1,0:T(8,128)(2,1)} custom-call(bf16[16,1024]{1,0:T(8,128)(2,1)S(1)} %reshape.39.field, bf16[27,16,256]{2,1,0:T(8,128)(2,1)S(1)} %copy-done), custom_call_target="tpu_custom_call" | custom-call | bytes 1048576 | tf_op jit(solution)/shard_map/pallas_call | solution.py:161
  10.3 0.0 copy-start.2
  10.3 12.1 %all-to-all-start = ((bf16[16,16,1536]{2,1,0:T(8,128)(2,1)}), bf16[16,16,1536]{2,1,0:T(8,128)(2,1)S(1)}, u32[]{:S(2)}, u32[]{:S(2)}) async-start(bf16[16,16,1536]{2,1,0:T(8,128)(2,1)} %shard_map.58), calls=%async_computation | async-start | bytes 1572864 | tf_op jit(solution)/shard_map/all_to_all | solution.py:164
  22.4 0.0 all-gather.3.cloned.1.call-start
  22.5 0.0 copy-done.2
  22.5 0.6 concatenate.12
  23.1 0.0 all-gather.3.cloned.1.call-update
  23.2 2.9 %collective-permute-start.3 = (bf16[16,1024]{1,0:T(8,128)(2,1)S(1)}, bf16[16,1024]{1,0:T(8,128)(2,1)S(1)}, u32[]{:S(2)}, u32[]{:S(2)}) collective-permute-start(bf16[16,1024]{1,0:T(8,128)(2,1)S(1)} %reshape.41.own), channel_id=1, source_target_pairs={{16,0},{32,16},{48,32},{64,48},{80,64},{96,80},{112,96},{128,112},... | collective-permute-start | bytes 98312 | tf_op jit(solution)/shard_map/ppermute | solution.py:157
  26.0 3.0 %collective-permute-start.2 = (bf16[16,1024]{1,0:T(8,128)(2,1)S(1)}, bf16[16,1024]{1,0:T(8,128)(2,1)S(1)}, u32[]{:S(2)}, u32[]{:S(2)}) collective-permute-start(bf16[16,1024]{1,0:T(8,128)(2,1)S(1)} %reshape.41.own), channel_id=1, source_target_pairs={{0,16},{16,32},{32,48},{48,64},{64,80},{80,96},{96,112},{112,128},... | collective-permute-start | bytes 98312 | tf_op jit(solution)/shard_map/ppermute | solution.py:156
  29.1 0.0 collective-permute-done.3.above
  29.1 1.0 collective-permute-done.2.below
  30.1 11.9 %all-to-all-done = bf16[16,16,1536]{2,1,0:T(8,128)(2,1)S(1)} async-done(((bf16[16,16,1536]{2,1,0:T(8,128)(2,1)}), bf16[16,16,1536]{2,1,0:T(8,128)(2,1)S(1)}, u32[]{:S(2)}, u32[]{:S(2)}) %all-to-all-start) | async-done | bytes 786464 | tf_op jit(solution)/shard_map/all_to_all | solution.py:164
  42.0 0.4 shard_map.61
  42.4 4.5 %collective-permute-start.4 = (f32[432,128]{1,0:T(8,128)S(1)}, f32[432,128]{1,0:T(8,128)S(1)}, u32[]{:S(2)}, u32[]{:S(2)}) collective-permute-start(f32[432,128]{1,0:T(8,128)S(1)} %get-tuple-element.6), channel_id=1, source_target_pairs={{0,16},{16,0},{1,17},{17,1},{2,18},{18,2},{3,19},{19,3},{4,20},{20... | collective-permute-start | bytes 663560 | tf_op jit(solution)/shard_map/ppermute | solution.py:174
  46.9 1.1 collective-permute-done.4
  48.0 0.7 pad_add_fusion
  48.8 0.0 copy-start.1
  48.8 8.6 %all-to-all-start.1 = ((f32[16,32,128]{2,1,0:T(8,128)}), f32[16,32,128]{2,1,0:T(8,128)S(1)}, u32[]{:S(2)}, u32[]{:S(2)}) async-start(f32[16,32,128]{2,1,0:T(8,128)} %bitcast.10), calls=%async_computation.1 | async-start | bytes 524288 | tf_op jit(solution)/shard_map/all_to_all | solution.py:184
  57.4 0.0 copy-done.1
  57.4 0.5 shard_map.59
  57.9 31.8 %all-gather.3.cloned.1.call-done = bf16[512,1024]{1,0:T(8,128)(2,1)} async-done(((bf16[32,1024]{1,0:T(8,128)(2,1)}), bf16[512,1024]{1,0:T(8,128)(2,1)}) %all-gather.3.cloned.1.call-update) | async-done | bytes 1048592 | tf_op jit(solution)/shard_map/all_gather | solution.py:159
  89.6 1.1 slice.50
  90.7 0.5 shard_map.60
  91.2 0.0 all-to-all-done.1
  91.3 0.7 broadcast_in_dim.2
  92.0 8.2 %all-to-all-start.2 = ((f32[16,32,128]{2,1,0:T(8,128)}), f32[16,32,128]{2,1,0:T(8,128)S(1)}, u32[]{:S(2)}, u32[]{:S(2)}) async-start(f32[16,32,128]{2,1,0:T(8,128)} %broadcast_in_dim.2), calls=%async_computation.2 | async-start | bytes 524288 | tf_op jit(solution)/shard_map/all_to_all | solution.py:196
  100.3 13.6 %collective-permute-start.1 = (f32[32,1024]{1,0:T(8,128)S(1)}, f32[32,1024]{1,0:T(8,128)S(1)}, u32[]{:S(2)}, u32[]{:S(2)}) collective-permute-start(f32[32,1024]{1,0:T(8,128)S(1)} %pad_maximum_fusion.2), channel_id=1, source_target_pairs={{16,0},{32,16},{48,32},{64,48},{80,64},{96,80},{112,96},{128,112},... | collective-permute-start | bytes 393224 | tf_op jit(solution)/shard_map/ppermute | solution.py:195
  113.9 3.4 %collective-permute-start = (f32[32,1024]{1,0:T(8,128)S(1)}, f32[32,1024]{1,0:T(8,128)S(1)}, u32[]{:S(2)}, u32[]{:S(2)}) collective-permute-start(f32[32,1024]{1,0:T(8,128)S(1)} %pad_maximum_fusion.1), channel_id=1, source_target_pairs={{0,16},{16,32},{32,48},{48,64},{64,80},{80,96},{96,112},{112,128},... | collective-permute-start | bytes 393224 | tf_op jit(solution)/shard_map/ppermute | solution.py:194
  117.4 0.0 all-to-all-done.2
  117.4 7.6 %collective-permute-start.5 = (f32[432,128]{1,0:T(8,128)S(1)}, f32[432,128]{1,0:T(8,128)S(1)}, u32[]{:S(2)}, u32[]{:S(2)}) collective-permute-start(f32[432,128]{1,0:T(8,128)S(1)} %slice.59), channel_id=1, source_target_pairs={{0,16},{16,0},{1,17},{17,1},{2,18},{18,2},{3,19},{19,3},{4,20},{20... | collective-permute-start | bytes 663560 | tf_op jit(solution)/shard_map/ppermute | solution.py:198
  125.1 0.0 collective-permute-done.1
  125.1 0.0 collective-permute-done
  125.1 0.6 reshape.44
  125.8 0.6 reshape.43
  126.4 0.0 collective-permute-done.5
  126.4 0.8 pad_maximum_fusion
  (9 shorter events, 0.2 us)
Async XLA Ops:
  7.9 0.9 copy-start
  10.3 12.2 %copy-start.2 = (bf16[16,2,4,128]{3,2,1,0:T(4,128)(2,1)S(1)}, bf16[16,2,4,128]{3,2,1,0:T(4,128)(2,1)}, u32[]{:S(2)}) copy-start(bf16[16,2,4,128]{3,2,1,0:T(4,128)(2,1)} %param.5) | copy-start | bytes 98308
  10.3 31.7 %all-to-all-start = ((bf16[16,16,1536]{2,1,0:T(8,128)(2,1)}), bf16[16,16,1536]{2,1,0:T(8,128)(2,1)S(1)}, u32[]{:S(2)}, u32[]{:S(2)}) async-start(bf16[16,16,1536]{2,1,0:T(8,128)(2,1)} %shard_map.58), calls=%async_computation | async-start | bytes 1572864 | tf_op jit(solution)/shard_map/all_to_all | solution.py:164
  22.4 67.2 %all-gather.3.cloned.1.call-start = ((), (), s32[]{:S(2)}) async-start(), calls=%async_computation.3 | async-start | bytes 1114112 | tf_op jit(solution)/shard_map/all_gather | solution.py:159
  23.2 5.9 %collective-permute-start.3 = (bf16[16,1024]{1,0:T(8,128)(2,1)S(1)}, bf16[16,1024]{1,0:T(8,128)(2,1)S(1)}, u32[]{:S(2)}, u32[]{:S(2)}) collective-permute-start(bf16[16,1024]{1,0:T(8,128)(2,1)S(1)} %reshape.41.own), channel_id=1, source_target_pairs={{16,0},{32,16},{48,32},{64,48},{80,64},{96,80},{112,96},{128,112},... | collective-permute-start | bytes 98312 | tf_op jit(solution)/shard_map/ppermute | solution.py:157
  26.0 4.0 %collective-permute-start.2 = (bf16[16,1024]{1,0:T(8,128)(2,1)S(1)}, bf16[16,1024]{1,0:T(8,128)(2,1)S(1)}, u32[]{:S(2)}, u32[]{:S(2)}) collective-permute-start(bf16[16,1024]{1,0:T(8,128)(2,1)S(1)} %reshape.41.own), channel_id=1, source_target_pairs={{0,16},{16,32},{32,48},{48,64},{64,80},{80,96},{96,112},{112,128},... | collective-permute-start | bytes 98312 | tf_op jit(solution)/shard_map/ppermute | solution.py:156
  42.4 5.6 %collective-permute-start.4 = (f32[432,128]{1,0:T(8,128)S(1)}, f32[432,128]{1,0:T(8,128)S(1)}, u32[]{:S(2)}, u32[]{:S(2)}) collective-permute-start(f32[432,128]{1,0:T(8,128)S(1)} %get-tuple-element.6), channel_id=1, source_target_pairs={{0,16},{16,0},{1,17},{17,1},{2,18},{18,2},{3,19},{19,3},{4,20},{20... | collective-permute-start | bytes 663560 | tf_op jit(solution)/shard_map/ppermute | solution.py:174
  48.8 8.6 %copy-start.1 = (bf16[27,16,256]{2,1,0:T(8,128)(2,1)S(1)}, bf16[27,16,256]{2,1,0:T(8,128)(2,1)}, u32[]{:S(2)}) copy-start(bf16[27,16,256]{2,1,0:T(8,128)(2,1)} %filters.3) | copy-start | bytes 663556
  48.8 42.5 %all-to-all-start.1 = ((f32[16,32,128]{2,1,0:T(8,128)}), f32[16,32,128]{2,1,0:T(8,128)S(1)}, u32[]{:S(2)}, u32[]{:S(2)}) async-start(f32[16,32,128]{2,1,0:T(8,128)} %bitcast.10), calls=%async_computation.1 | async-start | bytes 524288 | tf_op jit(solution)/shard_map/all_to_all | solution.py:184
  92.0 25.4 %all-to-all-start.2 = ((f32[16,32,128]{2,1,0:T(8,128)}), f32[16,32,128]{2,1,0:T(8,128)S(1)}, u32[]{:S(2)}, u32[]{:S(2)}) async-start(f32[16,32,128]{2,1,0:T(8,128)} %broadcast_in_dim.2), calls=%async_computation.2 | async-start | bytes 524288 | tf_op jit(solution)/shard_map/all_to_all | solution.py:196
  100.3 24.8 %collective-permute-start.1 = (f32[32,1024]{1,0:T(8,128)S(1)}, f32[32,1024]{1,0:T(8,128)S(1)}, u32[]{:S(2)}, u32[]{:S(2)}) collective-permute-start(f32[32,1024]{1,0:T(8,128)S(1)} %pad_maximum_fusion.2), channel_id=1, source_target_pairs={{16,0},{32,16},{48,32},{64,48},{80,64},{96,80},{112,96},{128,112},... | collective-permute-start | bytes 393224 | tf_op jit(solution)/shard_map/ppermute | solution.py:195
  113.9 11.2 %collective-permute-start = (f32[32,1024]{1,0:T(8,128)S(1)}, f32[32,1024]{1,0:T(8,128)S(1)}, u32[]{:S(2)}, u32[]{:S(2)}) collective-permute-start(f32[32,1024]{1,0:T(8,128)S(1)} %pad_maximum_fusion.1), channel_id=1, source_target_pairs={{0,16},{16,32},{32,48},{48,64},{64,80},{80,96},{96,112},{112,128},... | collective-permute-start | bytes 393224 | tf_op jit(solution)/shard_map/ppermute | solution.py:194
  117.4 9.0 %collective-permute-start.5 = (f32[432,128]{1,0:T(8,128)S(1)}, f32[432,128]{1,0:T(8,128)S(1)}, u32[]{:S(2)}, u32[]{:S(2)}) collective-permute-start(f32[432,128]{1,0:T(8,128)S(1)} %slice.59), channel_id=1, source_target_pairs={{0,16},{16,0},{1,17},{17,1},{2,18},{18,2},{3,19},{19,3},{4,20},{20... | collective-permute-start | bytes 663560 | tf_op jit(solution)/shard_map/ppermute | solution.py:198
Sparse Core Ops, SparseCore 0:
  25.3 64.2 all-gather.2

commit v2 on v1

--- a/solution.py
+++ b/solution.py
@@ -12,12 +12,12 @@
 BF = jnp.bfloat16
 F32 = jnp.float32
 VMEM = pl.BlockSpec(memory_space=pltpu.VMEM)
-SMEM = pl.BlockSpec(memory_space=pltpu.SMEM)
 TAPS = 27
 OWN = 16
 CELLS = 1024
 ROWS = TAPS * OWN
-WIDE = CELLS + 512
+WIDE = 2 * CELLS + 512
+SCALE = 1.0 / math.sqrt(32768)
 LIMIT = 48 * 1024 * 1024
 
 
@@ -49,10 +49,10 @@
     return jnp.where((at >= 0) & (at < 128), turned, 0.0)
 
 
-def pack_body(field, filters, out):
-    own = field[...]
-    for c in range(16):
-        out[c, :, 0:CELLS] = own
+def pack_body(field, cotangent, filters, out):
+    for at, rows in ((0, field[...]), (CELLS, cotangent[...])):
+        for c in range(16):
+            out[c, :, at : at + CELLS] = rows
     lane = lanes((OWN, 128))
     for g in range(4):
         parts = [jnp.zeros((OWN, 128), F32) for _ in range(16)]
@@ -68,7 +68,8 @@
                     turned = block if step == 0 else pltpu.roll(block, step, 1)
                     parts[8 * h + q] = jnp.where(here, turned, parts[8 * h + q])
         for c in range(16):
-            out[c, :, CELLS + 128 * g : CELLS + 128 * g + 128] = parts[c].astype(BF)
+            at = 2 * CELLS + 128 * g
+            out[c, :, at : at + 128] = parts[c].astype(BF)
 
 
 def taps_sum(products, a, sign):
@@ -92,7 +93,7 @@
     return blocks
 
 
-def grad_body(core, gathered, below, own, above, keep, send, shifted):
+def grad_body(gathered, below, own, above, out, shifted):
     zero = jnp.zeros((OWN, 128), BF)
     for a, source in ((0, above), (1, own), (2, below)):
         for r in range(2):
@@ -110,17 +111,26 @@
                         shifted[16 * k : 16 * k + 16, lane : lane + 128] = (
                             rolled[at][c] if 0 <= at < 4 else zero
                         )
-    total = lax.dot_general(
+    out[0:ROWS, :] = lax.dot_general(
         shifted[...],
         gathered[:, 0:CELLS],
         (((1,), (1,)), ((), ())),
         preferred_element_type=F32,
     )
-    low, high = total[:, 0:128], total[:, 128:256]
-    first = core[0] == 0
-    keep[0:ROWS, :] = jnp.where(first, low, high)
-    keep[ROWS:512, :] = jnp.zeros((512 - ROWS, 128), F32)
-    send[...] = jnp.where(first, high, low)
+    out[ROWS:512, :] = jnp.zeros((512 - ROWS, 256), F32)
+
+
+def sum_body(parts, out):
+    total = parts[0]
+    for n in range(1, 16):
+        total = total + parts[n]
+    out[...] = total * SCALE
+
+
+def share_body(mine, other, out):
+    total = mine[...] + other[...]
+    for n in range(16):
+        out[n] = total
 
 
 def forward_body(gathered, filters, out, products):
@@ -132,10 +142,10 @@
             out[a, :, 128 * n : 128 * n + 128] = block
 
 
-def adjoint_body(gathered, cotangent, out, products):
+def adjoint_body(gathered, out, products):
     products[...] = lax.dot_general(
-        gathered[:, CELLS : CELLS + ROWS],
-        cotangent[...],
+        gathered[:, 2 * CELLS : 2 * CELLS + ROWS],
+        gathered[:, CELLS : 2 * CELLS],
         (((0,), (0,)), ((), ())),
         preferred_element_type=F32,
     )
@@ -145,33 +155,28 @@
 
 
 def per_device(field, filters, cotangent):
-    scale = 1.0 / math.sqrt(32768)
     space = ("pair", "core")
-    core = lax.axis_index("core").astype(jnp.int32).reshape(1)
     own_field = field.reshape(OWN, CELLS)
     own_cot = cotangent.reshape(OWN, CELLS)
-
     up = [(i, i + 1) for i in range(31)]
     down = [(i + 1, i) for i in range(31)]
+
+    packed = call(pack_body, [shape((16, OWN, WIDE), BF)], [VMEM] * 3, moved=1 << 20)(
+        own_field, own_cot, filters
+    )[0]
+    gathered = lax.all_to_all(packed, "chan", 0, 0).reshape(256, WIDE)
     below = lax.ppermute(own_cot, space, up)
     above = lax.ppermute(own_cot, space, down)
-    wide_cot = jnp.concatenate([own_cot, jnp.zeros_like(own_cot)], axis=0)
-    all_cot = lax.all_gather(wide_cot, "chan", axis=0, tiled=False)[:, :OWN].reshape(256, CELLS)
-
-    packed = call(pack_body, [shape((16, OWN, WIDE), BF)], [VMEM] * 2, moved=1 << 20)(
-        own_field, filters
-    )[0]
-    gathered = lax.all_to_all(packed, "chan", 0, 0).reshape(256, WIDE)
-
-    keep, send = call(
+
+    own_grad = call(
         grad_body,
-        [shape((512, 128), F32), shape((ROWS, 128), F32)],
-        [SMEM] + [VMEM] * 4,
+        [shape((512, 256), F32)],
+        [VMEM] * 4,
         [pltpu.VMEM((ROWS, CELLS), BF)],
         flops=2 * ROWS * CELLS * 256,
         moved=1 << 20,
-    )(core, gathered, below, own_cot, above)
-    swapped = lax.ppermute(send, "core", [(0, 1), (1, 0)])
+    )(gathered, below, own_cot, above)[0]
+    parts = lax.all_to_all(own_grad.reshape(16, 32, 256), "pair", 0, 0)
     ys = call(
         forward_body,
         [shape((3, OWN, CELLS), F32)],
@@ -180,28 +185,23 @@
         flops=2 * ROWS * CELLS * 256,
         moved=1 << 20,
     )(gathered, filters)[0]
-    half = keep + jnp.pad(swapped, ((0, 512 - ROWS), (0, 0)))
-    parts = lax.all_to_all(half.reshape(16, 32, 128), "pair", 0, 0)
-    mine = jnp.sum(parts, axis=0) * scale
+    mine = call(sum_body, [shape((32, 256), F32)], [VMEM], moved=1 << 19)(parts)[0]
+    other = lax.ppermute(mine, "core", [(0, 1), (1, 0)])
+    shared = call(share_body, [shape((16, 32, 256), F32)], [VMEM] * 2, moved=1 << 19)(mine, other)[0]
+    full = lax.all_to_all(shared, "pair", 0, 0)
     zs = call(
         adjoint_body,
         [shape((3, OWN, CELLS), F32)],
-        [VMEM] * 2,
+        [VMEM],
         [pltpu.VMEM((ROWS, CELLS), F32)],
         flops=2 * ROWS * CELLS * 256,
         moved=1 << 20,
-    )(gathered, all_cot)[0]
+    )(gathered)[0]
     from_before = lax.ppermute(jnp.concatenate([ys[0], zs[2]], axis=0), space, up)
     from_after = lax.ppermute(jnp.concatenate([ys[2], zs[0]], axis=0), space, down)
-    full = lax.all_to_all(jnp.broadcast_to(mine[None], (16, 32, 128)), "pair", 0, 0)
-    full = full.reshape(512, 128)[:ROWS]
-    other = lax.ppermute(full, "core", [(0, 1), (1, 0)])
-    first = core[0] == 0
-    weight_grad = jnp.concatenate(
-        [jnp.where(first, full, other), jnp.where(first, other, full)], axis=1
-    ).reshape(TAPS, OWN, 256)
     out_field = (ys[1] + from_before[:OWN] + from_after[:OWN]).astype(BF).reshape(field.shape)
     input_grad = (zs[1] + from_before[OWN:] + from_after[OWN:]).astype(BF).reshape(field.shape)
+    weight_grad = full.reshape(512, 256)[:ROWS].reshape(TAPS, OWN, 256)
     return out_field, input_grad, weight_grad
 
 

time: 135 us -> 105 us (0.78)
  the two profiles are of different devices: /device:TPU:1 before, /device:TPU:120 now
where the time goes in v2:
time: 105 us; the launch traced here: 104 us
  starting transfers between devices  35.6 us (34%)
  waiting for transfers between devices  34.9 us (33%)
  blocking collectives  24.4 us (23%)
  local copies, waits for them, and re-layouts  4.57 us (4%)
  Pallas kernels  3.92 us (4%)
    all_to_all x1, blocking collectives, per_device(): parts = lax.all_to_all(own_grad.reshape(16, 32, 256), 'pair', 0, 0)  24.4 us
    all_to_all x1, waiting for transfers between devices, per_device(): gathered = lax.all_to_all(packed, 'chan', 0, 0).reshape(256, WIDE)  17.6 us
    all_to_all x1, starting transfers between devices, per_device(): gathered = lax.all_to_all(packed, 'chan', 0, 0).reshape(256, WIDE)  10.9 us
    ppermute x1, waiting for transfers between devices, per_device(): lax.ppermute(jnp.concatenate([ys[0], zs[2]], axis=0), space, up)  9.59 us
    ppermute x1, starting transfers between devices, per_device(): above = lax.ppermute(own_cot, space, down)  6.65 us
    ppermute x1, starting transfers between devices, per_device(): lax.ppermute(jnp.concatenate([ys[2], zs[0]], axis=0), space, down)  6.65 us
    ppermute x1, waiting for transfers between devices, per_device(): above = lax.ppermute(own_cot, space, down)  6.55 us
    all_to_all x1, starting transfers between devices, per_device(): full = lax.all_to_all(shared, 'pair', 0, 0)  5.56 us
  transfers between devices with their start and end apart: 7, of which 4 were waited for; matrix products, arithmetic and copies ran while one was open for 1% of the time, Pallas kernels for 1%

profile of v2, /device:TPU:120, one launch (start us, length us, event | category | flops | bytes accessed | tf_op | source)
XLA Modules:
  0.0 104.2 jit_solution(2115234459134193063)
XLA Ops:
  0.6 0.8 reshape.31.cotangent.own
  1.4 0.8 reshape.30.field
  2.2 0.0 copy-start
  2.2 0.9 copy-done
  3.1 1.6 %shard_map.58 = bf16[16,16,2560]{2,1,0:T(8,128)(2,1)} custom-call(bf16[16,1024]{1,0:T(8,128)(2,1)S(1)} %reshape.30.field, bf16[16,1024]{1,0:T(8,128)(2,1)S(1)} %reshape.31.cotangent.own, bf16[27,16,256]{2,1,0:T(8,128)(2,1)S(1)} %copy-done), custom_call_target="tpu_custom_call" | custom-call | bytes 1048576 | tf_op jit(solution)/shard_map/pallas_call | solution.py:164
  4.8 10.9 %all-to-all-start = ((bf16[16,16,2560]{2,1,0:T(8,128)(2,1)}), bf16[16,16,2560]{2,1,0:T(8,128)(2,1)S(1)}, u32[]{:S(2)}, u32[]{:S(2)}) async-start(bf16[16,16,2560]{2,1,0:T(8,128)(2,1)} %shard_map.58), calls=%async_computation | async-start | bytes 2621440 | tf_op jit(solution)/shard_map/all_to_all | solution.py:167
  15.6 1.9 %collective-permute-start.2 = (bf16[16,1024]{1,0:T(8,128)(2,1)S(1)}, bf16[16,1024]{1,0:T(8,128)(2,1)S(1)}, u32[]{:S(2)}, u32[]{:S(2)}) collective-permute-start(bf16[16,1024]{1,0:T(8,128)(2,1)S(1)} %reshape.31.cotangent.own), channel_id=1, source_target_pairs={{0,16},{16,32},{32,48},{48,64},{64,80},{80,96},{96,112},{112,128},... | collective-permute-start | bytes 98312 | tf_op jit(solution)/shard_map/ppermute | solution.py:168
  17.6 6.7 %collective-permute-start.3 = (bf16[16,1024]{1,0:T(8,128)(2,1)S(1)}, bf16[16,1024]{1,0:T(8,128)(2,1)S(1)}, u32[]{:S(2)}, u32[]{:S(2)}) collective-permute-start(bf16[16,1024]{1,0:T(8,128)(2,1)S(1)} %reshape.31.cotangent.own), channel_id=1, source_target_pairs={{16,0},{32,16},{48,32},{64,48},{80,64},{96,80},{112,96},{128,112},... | collective-permute-start | bytes 98312 | tf_op jit(solution)/shard_map/ppermute | solution.py:169
  24.2 0.0 collective-permute-done.2.below
  24.2 6.6 %collective-permute-done.3.above = bf16[16,1024]{1,0:T(8,128)(2,1)S(1)} collective-permute-done((bf16[16,1024]{1,0:T(8,128)(2,1)S(1)}, bf16[16,1024]{1,0:T(8,128)(2,1)S(1)}, u32[]{:S(2)}, u32[]{:S(2)}) %collective-permute-start.3) | collective-permute-done | bytes 32800 | tf_op jit(solution)/shard_map/ppermute | solution.py:169
  30.8 17.6 %all-to-all-done = bf16[16,16,2560]{2,1,0:T(8,128)(2,1)S(1)} async-done(((bf16[16,16,2560]{2,1,0:T(8,128)(2,1)}), bf16[16,16,2560]{2,1,0:T(8,128)(2,1)S(1)}, u32[]{:S(2)}, u32[]{:S(2)}) %all-to-all-start) | async-done | bytes 1310752 | tf_op jit(solution)/shard_map/all_to_all | solution.py:167
  48.4 0.4 shard_map.61
  48.8 24.4 %all_to_all.15.parts = f32[16,32,256]{2,1,0:T(8,128)S(1)} all-to-all(f32[16,32,256]{2,1,0:T(8,128)S(1)} %bitcast.23), channel_id=1, replica_groups=mesh['pair'=16,'core'=2,'chan'=16] {'pair'}, dimensions={0} | all-to-all | bytes 1048576 | tf_op jit(solution)/shard_map/all_to_all | solution.py:179
  73.3 0.0 copy-start.1
  73.3 2.1 %collective-permute-start.4 = (f32[32,256]{1,0:T(8,128)S(1)}, f32[32,256]{1,0:T(8,128)S(1)}, u32[]{:S(2)}, u32[]{:S(2)}) collective-permute-start(f32[32,256]{1,0:T(8,128)S(1)} %shard_map.62.mine), channel_id=1, source_target_pairs={{0,16},{16,0},{1,17},{17,1},{2,18},{18,2},{3,19},{19,3},{4,20},{20... | collective-permute-start | bytes 98312 | tf_op jit(solution)/shard_map/ppermute | solution.py:189
  75.3 1.2 %collective-permute-done.4.other = f32[32,256]{1,0:T(8,128)S(1)} collective-permute-done((f32[32,256]{1,0:T(8,128)S(1)}, f32[32,256]{1,0:T(8,128)S(1)}, u32[]{:S(2)}, u32[]{:S(2)}) %collective-permute-start.4) | collective-permute-done | bytes 32800 | tf_op jit(solution)/shard_map/ppermute | solution.py:189
  76.5 0.9 shard_map.63
  77.4 5.6 %all-to-all-start.2 = ((f32[16,32,256]{2,1,0:T(8,128)}), f32[16,32,256]{2,1,0:T(8,128)S(1)}, u32[]{:S(2)}, u32[]{:S(2)}) async-start(f32[16,32,256]{2,1,0:T(8,128)} %shard_map.63), calls=%async_computation.2 | async-start | bytes 1048576 | tf_op jit(solution)/shard_map/all_to_all | solution.py:191
  82.9 0.0 copy-done.1
  82.9 0.5 shard_map.59
  83.4 0.5 shard_map.60
  84.0 1.9 %collective-permute-start = (f32[32,1024]{1,0:T(8,128)S(1)}, f32[32,1024]{1,0:T(8,128)S(1)}, u32[]{:S(2)}, u32[]{:S(2)}) collective-permute-start(f32[32,1024]{1,0:T(8,128)S(1)} %pad_maximum_fusion), channel_id=1, source_target_pairs={{0,16},{16,32},{32,48},{48,64},{64,80},{80,96},{96,112},{112,128},... | collective-permute-start | bytes 393224 | tf_op jit(solution)/shard_map/ppermute | solution.py:200
  85.9 6.7 %collective-permute-start.1 = (f32[32,1024]{1,0:T(8,128)S(1)}, f32[32,1024]{1,0:T(8,128)S(1)}, u32[]{:S(2)}, u32[]{:S(2)}) collective-permute-start(f32[32,1024]{1,0:T(8,128)S(1)} %pad_maximum_fusion.1), channel_id=1, source_target_pairs={{16,0},{32,16},{48,32},{64,48},{80,64},{96,80},{112,96},{128,112},... | collective-permute-start | bytes 393224 | tf_op jit(solution)/shard_map/ppermute | solution.py:201
  92.6 9.6 %collective-permute-done = f32[32,1024]{1,0:T(8,128)S(1)} collective-permute-done((f32[32,1024]{1,0:T(8,128)S(1)}, f32[32,1024]{1,0:T(8,128)S(1)}, u32[]{:S(2)}, u32[]{:S(2)}) %collective-permute-start) | collective-permute-done | bytes 131104 | tf_op jit(solution)/shard_map/ppermute | solution.py:200
  102.2 0.0 collective-permute-done.1
  102.2 0.6 reshape.33
  102.8 0.6 reshape.34
  103.5 0.0 all-to-all-done.2
  103.5 0.8 slice.54
  (5 shorter events, 0.1 us)
Async XLA Ops:
  2.2 0.9 copy-start
  4.8 43.6 %all-to-all-start = ((bf16[16,16,2560]{2,1,0:T(8,128)(2,1)}), bf16[16,16,2560]{2,1,0:T(8,128)(2,1)S(1)}, u32[]{:S(2)}, u32[]{:S(2)}) async-start(bf16[16,16,2560]{2,1,0:T(8,128)(2,1)} %shard_map.58), calls=%async_computation | async-start | bytes 2621440 | tf_op jit(solution)/shard_map/all_to_all | solution.py:167
  15.6 8.6 %collective-permute-start.2 = (bf16[16,1024]{1,0:T(8,128)(2,1)S(1)}, bf16[16,1024]{1,0:T(8,128)(2,1)S(1)}, u32[]{:S(2)}, u32[]{:S(2)}) collective-permute-start(bf16[16,1024]{1,0:T(8,128)(2,1)S(1)} %reshape.31.cotangent.own), channel_id=1, source_target_pairs={{0,16},{16,32},{32,48},{48,64},{64,80},{80,96},{96,112},{112,128},... | collective-permute-start | bytes 98312 | tf_op jit(solution)/shard_map/ppermute | solution.py:168
  17.6 13.2 %collective-permute-start.3 = (bf16[16,1024]{1,0:T(8,128)(2,1)S(1)}, bf16[16,1024]{1,0:T(8,128)(2,1)S(1)}, u32[]{:S(2)}, u32[]{:S(2)}) collective-permute-start(bf16[16,1024]{1,0:T(8,128)(2,1)S(1)} %reshape.31.cotangent.own), channel_id=1, source_target_pairs={{16,0},{32,16},{48,32},{64,48},{80,64},{96,80},{112,96},{128,112},... | collective-permute-start | bytes 98312 | tf_op jit(solution)/shard_map/ppermute | solution.py:169
  73.3 9.7 %copy-start.1 = (bf16[27,16,256]{2,1,0:T(8,128)(2,1)S(1)}, bf16[27,16,256]{2,1,0:T(8,128)(2,1)}, u32[]{:S(2)}) copy-start(bf16[27,16,256]{2,1,0:T(8,128)(2,1)} %filters.3) | copy-start | bytes 663556
  73.3 3.2 %collective-permute-start.4 = (f32[32,256]{1,0:T(8,128)S(1)}, f32[32,256]{1,0:T(8,128)S(1)}, u32[]{:S(2)}, u32[]{:S(2)}) collective-permute-start(f32[32,256]{1,0:T(8,128)S(1)} %shard_map.62.mine), channel_id=1, source_target_pairs={{0,16},{16,0},{1,17},{17,1},{2,18},{18,2},{3,19},{19,3},{4,20},{20... | collective-permute-start | bytes 98312 | tf_op jit(solution)/shard_map/ppermute | solution.py:189
  77.4 26.1 %all-to-all-start.2 = ((f32[16,32,256]{2,1,0:T(8,128)}), f32[16,32,256]{2,1,0:T(8,128)S(1)}, u32[]{:S(2)}, u32[]{:S(2)}) async-start(f32[16,32,256]{2,1,0:T(8,128)} %shard_map.63), calls=%async_computation.2 | async-start | bytes 1048576 | tf_op jit(solution)/shard_map/all_to_all | solution.py:191
  84.0 18.2 %collective-permute-start = (f32[32,1024]{1,0:T(8,128)S(1)}, f32[32,1024]{1,0:T(8,128)S(1)}, u32[]{:S(2)}, u32[]{:S(2)}) collective-permute-start(f32[32,1024]{1,0:T(8,128)S(1)} %pad_maximum_fusion), channel_id=1, source_target_pairs={{0,16},{16,32},{32,48},{48,64},{64,80},{80,96},{96,112},{112,128},... | collective-permute-start | bytes 393224 | tf_op jit(solution)/shard_map/ppermute | solution.py:200
  85.9 16.2 %collective-permute-start.1 = (f32[32,1024]{1,0:T(8,128)S(1)}, f32[32,1024]{1,0:T(8,128)S(1)}, u32[]{:S(2)}, u32[]{:S(2)}) collective-permute-start(f32[32,1024]{1,0:T(8,128)S(1)} %pad_maximum_fusion.1), channel_id=1, source_target_pairs={{16,0},{32,16},{48,32},{64,48},{80,64},{96,80},{112,96},{128,112},... | collective-permute-start | bytes 393224 | tf_op jit(solution)/shard_map/ppermute | solution.py:201

commit v3 on v2

--- a/solution.py
+++ b/solution.py
@@ -11,6 +11,7 @@
 
 BF = jnp.bfloat16
 F32 = jnp.float32
+ANY = pl.BlockSpec(memory_space=pl.ANY)
 VMEM = pl.BlockSpec(memory_space=pltpu.VMEM)
 TAPS = 27
 OWN = 16
@@ -120,38 +121,35 @@
     out[ROWS:512, :] = jnp.zeros((512 - ROWS, 256), F32)
 
 
-def sum_body(parts, out):
+def sum_body(parts, _after, out):
     total = parts[0]
     for n in range(1, 16):
         total = total + parts[n]
     out[...] = total * SCALE
 
 
-def share_body(mine, other, out):
-    total = mine[...] + other[...]
+def share_body(both, _after, _too, out):
+    total = both[0] + both[1]
     for n in range(16):
         out[n] = total
 
 
-def forward_body(gathered, filters, out, products):
+def contributions_body(gathered, filters, up, down, mid, products):
     products[...] = jnp.dot(
         filters[...].reshape(ROWS, 256), gathered[:, 0:CELLS], preferred_element_type=F32
     )
-    for a in range(3):
+    for a, out in ((0, up), (1, mid), (2, down)):
         for n, block in enumerate(taps_sum(products, a, 1)):
-            out[a, :, 128 * n : 128 * n + 128] = block
-
-
-def adjoint_body(gathered, out, products):
+            out[0:OWN, 128 * n : 128 * n + 128] = block
     products[...] = lax.dot_general(
         gathered[:, 2 * CELLS : 2 * CELLS + ROWS],
         gathered[:, CELLS : 2 * CELLS],
         (((0,), (0,)), ((), ())),
         preferred_element_type=F32,
     )
-    for a in range(3):
+    for a, out in ((0, down), (1, mid), (2, up)):
         for n, block in enumerate(taps_sum(products, a, -1)):
-            out[a, :, 128 * n : 128 * n + 128] = block
+            out[OWN : 2 * OWN, 128 * n : 128 * n + 128] = block
 
 
 def per_device(field, filters, cotangent):
@@ -177,30 +175,25 @@
         moved=1 << 20,
     )(gathered, below, own_cot, above)[0]
     parts = lax.all_to_all(own_grad.reshape(16, 32, 256), "pair", 0, 0)
-    ys = call(
-        forward_body,
-        [shape((3, OWN, CELLS), F32)],
+    to_next, to_last, own_sums = call(
+        contributions_body,
+        [shape((2 * OWN, CELLS), F32)] * 3,
         [VMEM] * 2,
         [pltpu.VMEM((ROWS, CELLS), F32)],
-        flops=2 * ROWS * CELLS * 256,
+        flops=4 * ROWS * CELLS * 256,
         moved=1 << 20,
-    )(gathered, filters)[0]
-    mine = call(sum_body, [shape((32, 256), F32)], [VMEM], moved=1 << 19)(parts)[0]
-    other = lax.ppermute(mine, "core", [(0, 1), (1, 0)])
-    shared = call(share_body, [shape((16, 32, 256), F32)], [VMEM] * 2, moved=1 << 19)(mine, other)[0]
+    )(gathered, filters)
+    from_last = lax.ppermute(to_next, space, up)
+    from_next = lax.ppermute(to_last, space, down)
+    mine = call(sum_body, [shape((32, 256), F32)], [VMEM, ANY], moved=1 << 19)(parts, own_sums)[0]
+    both = lax.all_gather(mine, "core", axis=0)
+    shared = call(share_body, [shape((16, 32, 256), F32)], [VMEM, ANY, ANY], moved=1 << 19)(
+        both, from_last, from_next
+    )[0]
     full = lax.all_to_all(shared, "pair", 0, 0)
-    zs = call(
-        adjoint_body,
-        [shape((3, OWN, CELLS), F32)],
-        [VMEM],
-        [pltpu.VMEM((ROWS, CELLS), F32)],
-        flops=2 * ROWS * CELLS * 256,
-        moved=1 << 20,
-    )(gathered)[0]
-    from_before = lax.ppermute(jnp.concatenate([ys[0], zs[2]], axis=0), space, up)
-    from_after = lax.ppermute(jnp.concatenate([ys[2], zs[0]], axis=0), space, down)
-    out_field = (ys[1] + from_before[:OWN] + from_after[:OWN]).astype(BF).reshape(field.shape)
-    input_grad = (zs[1] + from_before[OWN:] + from_after[OWN:]).astype(BF).reshape(field.shape)
+    outs = (own_sums + from_last + from_next).astype(BF)
+    out_field = outs[:OWN].reshape(field.shape)
+    input_grad = outs[OWN:].reshape(field.shape)
     weight_grad = full.reshape(512, 256)[:ROWS].reshape(TAPS, OWN, 256)
     return out_field, input_grad, weight_grad
 

time: 105 us -> 103 us (0.981)
  the two profiles are of different devices: /device:TPU:120 before, /device:TPU:72 now
where the time goes in v3:
time: 103 us
  waiting for transfers between devices  61 us (59%)
  starting transfers between devices  30 us (29%)
  local copies, waits for them, and re-layouts  4.55 us (4%)
  Pallas kernels  4.45 us (4%)
  blocking collectives  1.85 us (2%)
    all_to_all x1, waiting for transfers between devices, per_device(): gathered = lax.all_to_all(packed, 'chan', 0, 0).reshape(256, WIDE)  26.6 us
    all_to_all x1, waiting for transfers between devices, per_device(): full = lax.all_to_all(shared, 'pair', 0, 0)  17.2 us
    all_to_all x1, waiting for transfers between devices, per_device(): parts = lax.all_to_all(own_grad.reshape(16, 32, 256), 'pair', 0, 0)  13.7 us
    all_to_all x1, starting transfers between devices, per_device(): gathered = lax.all_to_all(packed, 'chan', 0, 0).reshape(256, WIDE)  10.9 us
    all_to_all x1, starting transfers between devices, per_device(): parts = lax.all_to_all(own_grad.reshape(16, 32, 256), 'pair', 0, 0)  8.77 us
    all_to_all x1, starting transfers between devices, per_device(): full = lax.all_to_all(shared, 'pair', 0, 0)  5.16 us
    ppermute x1, waiting for transfers between devices, per_device(): above = lax.ppermute(own_cot, space, down)  3.52 us
  transfers between devices with their start and end apart: 7, of which 4 were waited for; matrix products, arithmetic and copies ran while one was open for 1% of the time, Pallas kernels for 1%

profile of v3, /device:TPU:72, one launch (start us, length us, event | category | flops | bytes accessed | tf_op | source)
XLA Modules:
  0.0 102.6 jit_solution(4214745028966973934)
XLA Ops:
  0.6 0.8 reshape.31.cotangent.own
  1.4 0.8 reshape.30.field
  2.2 0.0 copy-start
  2.2 0.9 copy-done
  3.1 1.6 %shard_map.58 = bf16[16,16,2560]{2,1,0:T(8,128)(2,1)} custom-call(bf16[16,1024]{1,0:T(8,128)(2,1)S(1)} %reshape.30.field, bf16[16,1024]{1,0:T(8,128)(2,1)S(1)} %reshape.31.cotangent.own, bf16[27,16,256]{2,1,0:T(8,128)(2,1)S(1)} %copy-done), custom_call_target="tpu_custom_call" | custom-call | bytes 1048576 | tf_op jit(solution)/shard_map/pallas_call | solution.py:162
  4.8 10.9 %all-to-all-start = ((bf16[16,16,2560]{2,1,0:T(8,128)(2,1)}), bf16[16,16,2560]{2,1,0:T(8,128)(2,1)S(1)}, u32[]{:S(2)}, u32[]{:S(2)}) async-start(bf16[16,16,2560]{2,1,0:T(8,128)(2,1)} %shard_map.58), calls=%async_computation | async-start | bytes 2621440 | tf_op jit(solution)/shard_map/all_to_all | solution.py:165
  15.6 1.3 %collective-permute-start.2 = (bf16[16,1024]{1,0:T(8,128)(2,1)S(1)}, bf16[16,1024]{1,0:T(8,128)(2,1)S(1)}, u32[]{:S(2)}, u32[]{:S(2)}) collective-permute-start(bf16[16,1024]{1,0:T(8,128)(2,1)S(1)} %reshape.31.cotangent.own), channel_id=1, source_target_pairs={{0,16},{16,32},{32,48},{48,64},{64,80},{80,96},{96,112},{112,128},... | collective-permute-start | bytes 98312 | tf_op jit(solution)/shard_map/ppermute | solution.py:166
  16.9 1.3 %collective-permute-start.3 = (bf16[16,1024]{1,0:T(8,128)(2,1)S(1)}, bf16[16,1024]{1,0:T(8,128)(2,1)S(1)}, u32[]{:S(2)}, u32[]{:S(2)}) collective-permute-start(bf16[16,1024]{1,0:T(8,128)(2,1)S(1)} %reshape.31.cotangent.own), channel_id=1, source_target_pairs={{16,0},{32,16},{48,32},{64,48},{80,64},{96,80},{112,96},{128,112},... | collective-permute-start | bytes 98312 | tf_op jit(solution)/shard_map/ppermute | solution.py:167
  18.2 0.0 collective-permute-done.2.below
  18.2 3.5 %collective-permute-done.3.above = bf16[16,1024]{1,0:T(8,128)(2,1)S(1)} collective-permute-done((bf16[16,1024]{1,0:T(8,128)(2,1)S(1)}, bf16[16,1024]{1,0:T(8,128)(2,1)S(1)}, u32[]{:S(2)}, u32[]{:S(2)}) %collective-permute-start.3) | collective-permute-done | bytes 32800 | tf_op jit(solution)/shard_map/ppermute | solution.py:167
  21.8 26.6 %all-to-all-done = bf16[16,16,2560]{2,1,0:T(8,128)(2,1)S(1)} async-done(((bf16[16,16,2560]{2,1,0:T(8,128)(2,1)}), bf16[16,16,2560]{2,1,0:T(8,128)(2,1)S(1)}, u32[]{:S(2)}, u32[]{:S(2)}) %all-to-all-start) | async-done | bytes 1310752 | tf_op jit(solution)/shard_map/all_to_all | solution.py:165
  48.4 0.0 copy-start.1
  48.4 1.3 %shard_map.60 = f32[512,256]{1,0:T(8,128)} custom-call(bf16[256,2560]{1,0:T(8,128)(2,1)S(1)} %bitcast.5, bf16[16,1024]{1,0:T(8,128)(2,1)S(1)} %collective-permute-done.2.below, bf16[16,1024]{1,0:T(8,128)(2,1)S(1)} %reshape.31.cotangent.own, bf16[16,1024]{1,0:T(8,128)(2,1)S(1)} %collective-permute-done.3.above), custom_call_target="tpu_custom_call" | custom-call | flops 226492416 | bytes 1048576 | tf_op jit(solution)/shard_map/pallas_call | solution.py:169
  49.6 8.8 %all-to-all-start.1 = ((f32[16,32,256]{2,1,0:T(8,128)}), f32[16,32,256]{2,1,0:T(8,128)S(1)}, u32[]{:S(2)}, u32[]{:S(2)}) async-start(f32[16,32,256]{2,1,0:T(8,128)} %bitcast.1), calls=%async_computation.1 | async-start | bytes 1048576 | tf_op jit(solution)/shard_map/all_to_all | solution.py:177
  58.4 0.0 copy-done.1
  58.4 0.7 shard_map.59
  59.1 1.3 %collective-permute-start = (f32[32,1024]{1,0:T(8,128)S(1)}, f32[32,1024]{1,0:T(8,128)S(1)}, u32[]{:S(2)}, u32[]{:S(2)}) collective-permute-start(f32[32,1024]{1,0:T(8,128)S(1)} %get-tuple-element.7), channel_id=1, source_target_pairs={{0,16},{16,32},{32,48},{48,64},{64,80},{80,96},{96,112},{112,128},... | collective-permute-start | bytes 393224 | tf_op jit(solution)/shard_map/ppermute | solution.py:186
  60.4 1.3 %collective-permute-start.1 = (f32[32,1024]{1,0:T(8,128)S(1)}, f32[32,1024]{1,0:T(8,128)S(1)}, u32[]{:S(2)}, u32[]{:S(2)}) collective-permute-start(f32[32,1024]{1,0:T(8,128)S(1)} %get-tuple-element.8), channel_id=1, source_target_pairs={{16,0},{32,16},{48,32},{64,48},{80,64},{96,80},{112,96},{128,112},... | collective-permute-start | bytes 393224 | tf_op jit(solution)/shard_map/ppermute | solution.py:187
  61.7 13.7 %all-to-all-done.1.parts = f32[16,32,256]{2,1,0:T(8,128)S(1)} async-done(((f32[16,32,256]{2,1,0:T(8,128)}), f32[16,32,256]{2,1,0:T(8,128)S(1)}, u32[]{:S(2)}, u32[]{:S(2)}) %all-to-all-start.1) | async-done | bytes 524320 | tf_op jit(solution)/shard_map/all_to_all | solution.py:177
  75.4 1.9 %all-gather = f32[64,256]{1,0:T(8,128)S(1)} all-gather(f32[32,256]{1,0:T(8,128)S(1)} %shard_map.61), channel_id=2, replica_groups=mesh['pair'=16,'core'=2,'chan'=16] {'core'}, dimensions={0}, use_global_device_ids=true | all-gather | bytes 98304 | tf_op jit(solution)/shard_map/all_gather | solution.py:189
  77.3 0.0 collective-permute-done._after
  77.3 0.0 collective-permute-done.1._too
  77.3 0.9 shard_map.62
  78.1 5.2 %all-to-all-start.2 = ((f32[16,32,256]{2,1,0:T(8,128)}), f32[16,32,256]{2,1,0:T(8,128)S(1)}, u32[]{:S(2)}, u32[]{:S(2)}) async-start(f32[16,32,256]{2,1,0:T(8,128)} %shard_map.62), calls=%async_computation.2 | async-start | bytes 1048576 | tf_op jit(solution)/shard_map/all_to_all | solution.py:193
  83.3 0.6 reshape.33
  84.0 0.6 reshape.34
  84.6 17.2 %all-to-all-done.2 = f32[16,32,256]{2,1,0:T(8,128)S(1)} async-done(((f32[16,32,256]{2,1,0:T(8,128)}), f32[16,32,256]{2,1,0:T(8,128)S(1)}, u32[]{:S(2)}, u32[]{:S(2)}) %all-to-all-start.2) | async-done | bytes 524320 | tf_op jit(solution)/shard_map/all_to_all | solution.py:193
  101.8 0.8 slice.14
  (3 shorter events, 0.1 us)
Async XLA Ops:
  2.2 0.9 copy-start
  4.8 43.6 %all-to-all-start = ((bf16[16,16,2560]{2,1,0:T(8,128)(2,1)}), bf16[16,16,2560]{2,1,0:T(8,128)(2,1)S(1)}, u32[]{:S(2)}, u32[]{:S(2)}) async-start(bf16[16,16,2560]{2,1,0:T(8,128)(2,1)} %shard_map.58), calls=%async_computation | async-start | bytes 2621440 | tf_op jit(solution)/shard_map/all_to_all | solution.py:165
  15.6 2.6 %collective-permute-start.2 = (bf16[16,1024]{1,0:T(8,128)(2,1)S(1)}, bf16[16,1024]{1,0:T(8,128)(2,1)S(1)}, u32[]{:S(2)}, u32[]{:S(2)}) collective-permute-start(bf16[16,1024]{1,0:T(8,128)(2,1)S(1)} %reshape.31.cotangent.own), channel_id=1, source_target_pairs={{0,16},{16,32},{32,48},{48,64},{64,80},{80,96},{96,112},{112,128},... | collective-permute-start | bytes 98312 | tf_op jit(solution)/shard_map/ppermute | solution.py:166
  16.9 4.8 %collective-permute-start.3 = (bf16[16,1024]{1,0:T(8,128)(2,1)S(1)}, bf16[16,1024]{1,0:T(8,128)(2,1)S(1)}, u32[]{:S(2)}, u32[]{:S(2)}) collective-permute-start(bf16[16,1024]{1,0:T(8,128)(2,1)S(1)} %reshape.31.cotangent.own), channel_id=1, source_target_pairs={{16,0},{32,16},{48,32},{64,48},{80,64},{96,80},{112,96},{128,112},... | collective-permute-start | bytes 98312 | tf_op jit(solution)/shard_map/ppermute | solution.py:167
  48.4 10.0 %copy-start.1 = (bf16[27,16,256]{2,1,0:T(8,128)(2,1)S(1)}, bf16[27,16,256]{2,1,0:T(8,128)(2,1)}, u32[]{:S(2)}) copy-start(bf16[27,16,256]{2,1,0:T(8,128)(2,1)} %filters.3) | copy-start | bytes 663556
  49.6 25.8 %all-to-all-start.1 = ((f32[16,32,256]{2,1,0:T(8,128)}), f32[16,32,256]{2,1,0:T(8,128)S(1)}, u32[]{:S(2)}, u32[]{:S(2)}) async-start(f32[16,32,256]{2,1,0:T(8,128)} %bitcast.1), calls=%async_computation.1 | async-start | bytes 1048576 | tf_op jit(solution)/shard_map/all_to_all | solution.py:177
  59.1 18.2 %collective-permute-start = (f32[32,1024]{1,0:T(8,128)S(1)}, f32[32,1024]{1,0:T(8,128)S(1)}, u32[]{:S(2)}, u32[]{:S(2)}) collective-permute-start(f32[32,1024]{1,0:T(8,128)S(1)} %get-tuple-element.7), channel_id=1, source_target_pairs={{0,16},{16,32},{32,48},{48,64},{64,80},{80,96},{96,112},{112,128},... | collective-permute-start | bytes 393224 | tf_op jit(solution)/shard_map/ppermute | solution.py:186
  60.4 16.9 %collective-permute-start.1 = (f32[32,1024]{1,0:T(8,128)S(1)}, f32[32,1024]{1,0:T(8,128)S(1)}, u32[]{:S(2)}, u32[]{:S(2)}) collective-permute-start(f32[32,1024]{1,0:T(8,128)S(1)} %get-tuple-element.8), channel_id=1, source_target_pairs={{16,0},{32,16},{48,32},{64,48},{80,64},{96,80},{112,96},{128,112},... | collective-permute-start | bytes 393224 | tf_op jit(solution)/shard_map/ppermute | solution.py:187
  78.1 23.6 %all-to-all-start.2 = ((f32[16,32,256]{2,1,0:T(8,128)}), f32[16,32,256]{2,1,0:T(8,128)S(1)}, u32[]{:S(2)}, u32[]{:S(2)}) async-start(f32[16,32,256]{2,1,0:T(8,128)} %shard_map.62), calls=%async_computation.2 | async-start | bytes 1048576 | tf_op jit(solution)/shard_map/all_to_all | solution.py:193

commit v4 on v3

--- a/solution.py
+++ b/solution.py
@@ -11,7 +11,9 @@
 
 BF = jnp.bfloat16
 F32 = jnp.float32
+HALF = jnp.float16
 ANY = pl.BlockSpec(memory_space=pl.ANY)
+FAR = pl.BlockSpec(memory_space=pltpu.HBM)
 VMEM = pl.BlockSpec(memory_space=pltpu.VMEM)
 TAPS = 27
 OWN = 16
@@ -50,10 +52,23 @@
     return jnp.where((at >= 0) & (at < 128), turned, 0.0)
 
 
-def pack_body(field, cotangent, filters, out):
-    for at, rows in ((0, field[...]), (CELLS, cotangent[...])):
-        for c in range(16):
-            out[c, :, at : at + CELLS] = rows
+def pack_body(field_far, cot_far, filters_far, out, own_cot, field, cotangent, filters, arrived):
+    pairs = ((field_far, field), (cot_far, cotangent), (filters_far, filters))
+    copies = [pltpu.make_async_copy(a, b, arrived.at[n]) for n, (a, b) in enumerate(pairs)]
+    for copy in copies:
+        copy.start()
+    copies[0].wait()
+    copies[1].wait()
+    for r in range(2):
+        for z in range(4):
+            at = 128 * (4 * r + z)
+            mine = cotangent[:, r, z, :]
+            theirs = field[:, r, z, :]
+            own_cot[:, at : at + 128] = mine
+            for c in range(16):
+                out[c, :, at : at + 128] = theirs
+                out[c, :, CELLS + at : CELLS + at + 128] = mine
+    copies[2].wait()
     lane = lanes((OWN, 128))
     for g in range(4):
         parts = [jnp.zeros((OWN, 128), F32) for _ in range(16)]
@@ -112,26 +127,43 @@
                         shifted[16 * k : 16 * k + 16, lane : lane + 128] = (
                             rolled[at][c] if 0 <= at < 4 else zero
                         )
-    out[0:ROWS, :] = lax.dot_general(
+    total = lax.dot_general(
         shifted[...],
         gathered[:, 0:CELLS],
         (((1,), (1,)), ((), ())),
         preferred_element_type=F32,
     )
-    out[ROWS:512, :] = jnp.zeros((512 - ROWS, 256), F32)
+    power, scaled = scaled_down(total)
+    out[...] = jnp.zeros((32, 16, 256), F32)
+    for n in range(31):
+        rows = min(14, ROWS - 14 * n)
+        out[n, 0:rows, :] = scaled[14 * n : 14 * n + rows, :]
+        out[n, 14:16, :] = jnp.broadcast_to(power, (2, 256))
+
+
+def scaled_down(values):
+    most = jnp.full((1, 256), jnp.max(jnp.abs(values)), F32)
+    power = jnp.ceil(jnp.log2(jnp.maximum(most, 2.0**-100)))
+    return power, values * jnp.exp2(14.0 - power)
 
 
 def sum_body(parts, _after, out):
-    total = parts[0]
-    for n in range(1, 16):
-        total = total + parts[n]
-    out[...] = total * SCALE
-
-
-def share_body(both, _after, _too, out):
-    total = both[0] + both[1]
-    for n in range(16):
-        out[n] = total
+    total = jnp.zeros((14, 256), F32)
+    for n in range(32):
+        total = total + parts[n, 0:14, :] * jnp.exp2(parts[n, 14:15, :] - 14.0)
+    power, scaled = scaled_down(total * SCALE)
+    out[0:14, :] = scaled
+    out[14:16, :] = jnp.broadcast_to(power, (2, 256))
+
+
+def share_body(mine, _after, _too, out):
+    out[...] = mine[...]
+
+
+def finish_body(full, out):
+    for n in range(31):
+        rows = min(14, ROWS - 14 * n)
+        out[14 * n : 14 * n + rows, :] = full[n, 0:rows, :] * jnp.exp2(full[n, 14:15, :] - 14.0)
 
 
 def contributions_body(gathered, filters, up, down, mid, products):
@@ -154,27 +186,34 @@
 
 def per_device(field, filters, cotangent):
     space = ("pair", "core")
-    own_field = field.reshape(OWN, CELLS)
-    own_cot = cotangent.reshape(OWN, CELLS)
     up = [(i, i + 1) for i in range(31)]
     down = [(i + 1, i) for i in range(31)]
 
-    packed = call(pack_body, [shape((16, OWN, WIDE), BF)], [VMEM] * 3, moved=1 << 20)(
-        own_field, own_cot, filters
-    )[0]
+    packed, own_cot = call(
+        pack_body,
+        [shape((16, OWN, WIDE), BF), shape((OWN, CELLS), BF)],
+        [FAR] * 3,
+        [
+            pltpu.VMEM((OWN, 2, 4, 128), BF),
+            pltpu.VMEM((OWN, 2, 4, 128), BF),
+            pltpu.VMEM((TAPS, OWN, 256), BF),
+            pltpu.SemaphoreType.DMA((3,)),
+        ],
+        moved=1 << 20,
+    )(field, cotangent, filters)
     gathered = lax.all_to_all(packed, "chan", 0, 0).reshape(256, WIDE)
     below = lax.ppermute(own_cot, space, up)
     above = lax.ppermute(own_cot, space, down)
 
     own_grad = call(
         grad_body,
-        [shape((512, 256), F32)],
+        [shape((32, 16, 256), F32)],
         [VMEM] * 4,
         [pltpu.VMEM((ROWS, CELLS), BF)],
         flops=2 * ROWS * CELLS * 256,
         moved=1 << 20,
     )(gathered, below, own_cot, above)[0]
-    parts = lax.all_to_all(own_grad.reshape(16, 32, 256), "pair", 0, 0)
+    parts = lax.all_to_all(own_grad.astype(HALF), space, 0, 0).astype(F32)
     to_next, to_last, own_sums = call(
         contributions_body,
         [shape((2 * OWN, CELLS), F32)] * 3,
@@ -185,16 +224,17 @@
     )(gathered, filters)
     from_last = lax.ppermute(to_next, space, up)
     from_next = lax.ppermute(to_last, space, down)
-    mine = call(sum_body, [shape((32, 256), F32)], [VMEM, ANY], moved=1 << 19)(parts, own_sums)[0]
-    both = lax.all_gather(mine, "core", axis=0)
-    shared = call(share_body, [shape((16, 32, 256), F32)], [VMEM, ANY, ANY], moved=1 << 19)(
-        both, from_last, from_next
+    mine = call(sum_body, [shape((16, 256), F32)], [VMEM, ANY], moved=1 << 19)(parts, own_sums)[0]
+    shared = call(share_body, [shape((16, 256), F32)], [VMEM, ANY, ANY], moved=1 << 14)(
+        mine, from_last, from_next
     )[0]
-    full = lax.all_to_all(shared, "pair", 0, 0)
+    shared = jnp.broadcast_to(shared.astype(HALF)[None], (32, 16, 256))
+    full = lax.all_to_all(shared, space, 0, 0).astype(F32)
     outs = (own_sums + from_last + from_next).astype(BF)
     out_field = outs[:OWN].reshape(field.shape)
     input_grad = outs[OWN:].reshape(field.shape)
-    weight_grad = full.reshape(512, 256)[:ROWS].reshape(TAPS, OWN, 256)
+    weight_grad = call(finish_body, [shape((ROWS, 256), F32)], [VMEM], moved=1 << 20)(full)[0]
+    weight_grad = weight_grad.reshape(TAPS, OWN, 256)
     return out_field, input_grad, weight_grad
 
 

time: 103 us -> 99.7 us (0.968)
  the two profiles are of different devices: /device:TPU:72 before, /device:TPU:1 now
where the time goes in v4:
time: 99.7 us; the launch traced here: 98.7 us
  waiting for transfers between devices  45.2 us (45%)
  starting transfers between devices  42.8 us (43%)
  Pallas kernels  4.61 us (5%)
  local copies, waits for them, and re-layouts  4.44 us (4%)
    all_to_all x1, waiting for transfers between devices, per_device(): gathered = lax.all_to_all(packed, 'chan', 0, 0).reshape(256, WIDE)  24.3 us
    all_to_all x1, waiting for transfers between devices, per_device(): full = lax.all_to_all(shared, space, 0, 0).astype(F32)  12.4 us
    all_to_all x1, starting transfers between devices, per_device(): gathered = lax.all_to_all(packed, 'chan', 0, 0).reshape(256, WIDE)  12 us
    all_to_all x1, starting transfers between devices, per_device(): parts = lax.all_to_all(own_grad.astype(HALF), space, 0, 0).astype(F32)  10.6 us
    all_to_all x1, starting transfers between devices, per_device(): full = lax.all_to_all(shared, space, 0, 0).astype(F32)  8.9 us
    all_to_all x1, waiting for transfers between devices, per_device(): parts = lax.all_to_all(own_grad.astype(HALF), space, 0, 0).astype(F32)  7.52 us
    ppermute x1, starting transfers between devices, per_device(): from_last = lax.ppermute(to_next, space, up)  3.54 us
    ppermute x1, starting transfers between devices, per_device(): below = lax.ppermute(own_cot, space, up)  3.02 us
  transfers between devices with their start and end apart: 7, of which 4 were waited for; matrix products, arithmetic and copies ran while one was open for 1% of the time, Pallas kernels for 1%

profile of v4, /device:TPU:1, one launch (start us, length us, event | category | flops | bytes accessed | tf_op | source)
XLA Modules:
  0.0 98.7 jit_solution(13457352256371930996)
XLA Ops:
  0.6 0.0 copy-start
  0.6 0.9 copy-done
  1.6 0.0 copy-start.2
  1.6 0.8 copy-done.2
  2.3 0.0 copy-start.3
  2.3 0.8 copy-done.3
  3.1 2.3 %shard_map.58 = (bf16[16,16,2560]{2,1,0:T(8,128)(2,1)}, bf16[16,1024]{1,0:T(8,128)(2,1)S(1)}) custom-call(bf16[16,2,4,128]{3,2,1,0:T(4,128)(2,1)S(1)} %copy-done.2, bf16[16,2,4,128]{3,2,1,0:T(4,128)(2,1)S(1)} %copy-done.3, bf16[27,16,256]{2,1,0:T(8,128)(2,1)S(1)} %copy-done), custom_call_target="tpu_custom_call" | custom-call | bytes 1048576 | tf_op jit(solution)/shard_map/pallas_call | solution.py:192
  5.3 12.0 %all-to-all-start = ((bf16[16,16,2560]{2,1,0:T(8,128)(2,1)}), bf16[16,16,2560]{2,1,0:T(8,128)(2,1)S(1)}, u32[]{:S(2)}, u32[]{:S(2)}) async-start(bf16[16,16,2560]{2,1,0:T(8,128)(2,1)} %get-tuple-element.8), calls=%async_computation | async-start | bytes 2621440 | tf_op jit(solution)/shard_map/all_to_all | solution.py:204
  17.3 2.9 %collective-permute-start.3 = (bf16[16,1024]{1,0:T(8,128)(2,1)S(1)}, bf16[16,1024]{1,0:T(8,128)(2,1)S(1)}, u32[]{:S(2)}, u32[]{:S(2)}) collective-permute-start(bf16[16,1024]{1,0:T(8,128)(2,1)S(1)} %get-tuple-element.12.own), channel_id=1, source_target_pairs={{16,0},{32,16},{48,32},{64,48},{80,64},{96,80},{112,96},{128,112},... | collective-permute-start | bytes 98312 | tf_op jit(solution)/shard_map/ppermute | solution.py:206
  20.2 3.0 %collective-permute-start.2 = (bf16[16,1024]{1,0:T(8,128)(2,1)S(1)}, bf16[16,1024]{1,0:T(8,128)(2,1)S(1)}, u32[]{:S(2)}, u32[]{:S(2)}) collective-permute-start(bf16[16,1024]{1,0:T(8,128)(2,1)S(1)} %get-tuple-element.12.own), channel_id=1, source_target_pairs={{0,16},{16,32},{32,48},{48,64},{64,80},{80,96},{96,112},{112,128},... | collective-permute-start | bytes 98312 | tf_op jit(solution)/shard_map/ppermute | solution.py:205
  23.2 0.0 collective-permute-done.3.above
  23.3 1.0 %collective-permute-done.2.below = bf16[16,1024]{1,0:T(8,128)(2,1)S(1)} collective-permute-done((bf16[16,1024]{1,0:T(8,128)(2,1)S(1)}, bf16[16,1024]{1,0:T(8,128)(2,1)S(1)}, u32[]{:S(2)}, u32[]{:S(2)}) %collective-permute-start.2) | collective-permute-done | bytes 32800 | tf_op jit(solution)/shard_map/ppermute | solution.py:205
  24.2 24.3 %all-to-all-done = bf16[16,16,2560]{2,1,0:T(8,128)(2,1)S(1)} async-done(((bf16[16,16,2560]{2,1,0:T(8,128)(2,1)}), bf16[16,16,2560]{2,1,0:T(8,128)(2,1)S(1)}, u32[]{:S(2)}, u32[]{:S(2)}) %all-to-all-start) | async-done | bytes 1310752 | tf_op jit(solution)/shard_map/all_to_all | solution.py:204
  48.5 0.0 copy-start.1
  48.5 0.6 shard_map.60
  49.2 0.7 convert_element_type.16
  49.9 10.6 %all-to-all-start.1 = ((f16[32,16,256]{2,1,0:T(8,128)(2,1)}), f16[32,16,256]{2,1,0:T(8,128)(2,1)S(1)}, u32[]{:S(2)}, u32[]{:S(2)}) async-start(f16[32,16,256]{2,1,0:T(8,128)(2,1)} %convert_element_type.16), calls=%async_computation.1 | async-start | bytes 524288 | tf_op jit(solution)/shard_map/all_to_all | solution.py:216
  60.5 0.0 copy-done.1
  60.5 0.7 shard_map.59
  61.2 3.5 %collective-permute-start = (f32[32,1024]{1,0:T(8,128)S(1)}, f32[32,1024]{1,0:T(8,128)S(1)}, u32[]{:S(2)}, u32[]{:S(2)}) collective-permute-start(f32[32,1024]{1,0:T(8,128)S(1)} %get-tuple-element.10), channel_id=1, source_target_pairs={{0,16},{16,32},{32,48},{48,64},{64,80},{80,96},{96,112},{112,128},... | collective-permute-start | bytes 393224 | tf_op jit(solution)/shard_map/ppermute | solution.py:225
  64.8 1.9 %collective-permute-start.1 = (f32[32,1024]{1,0:T(8,128)S(1)}, f32[32,1024]{1,0:T(8,128)S(1)}, u32[]{:S(2)}, u32[]{:S(2)}) collective-permute-start(f32[32,1024]{1,0:T(8,128)S(1)} %get-tuple-element.11), channel_id=1, source_target_pairs={{16,0},{32,16},{48,32},{64,48},{80,64},{96,80},{112,96},{128,112},... | collective-permute-start | bytes 393224 | tf_op jit(solution)/shard_map/ppermute | solution.py:226
  66.7 7.5 %all-to-all-done.1 = f16[32,16,256]{2,1,0:T(8,128)(2,1)S(1)} async-done(((f16[32,16,256]{2,1,0:T(8,128)(2,1)}), f16[32,16,256]{2,1,0:T(8,128)(2,1)S(1)}, u32[]{:S(2)}, u32[]{:S(2)}) %all-to-all-start.1) | async-done | bytes 262176 | tf_op jit(solution)/shard_map/all_to_all | solution.py:216
  74.2 0.1 convert_element_type.17.parts
  74.3 0.2 shard_map.61.mine
  74.5 0.0 collective-permute-done._after
  74.5 0.0 collective-permute-done.1._too
  74.5 0.7 broadcast_in_dim.2
  75.2 8.9 %all-to-all-start.2 = ((f16[32,16,256]{2,1,0:T(8,128)(2,1)}), f16[32,16,256]{2,1,0:T(8,128)(2,1)S(1)}, u32[]{:S(2)}, u32[]{:S(2)}) async-start(f16[32,16,256]{2,1,0:T(8,128)(2,1)} %broadcast_in_dim.2), calls=%async_computation.2 | async-start | bytes 524288 | tf_op jit(solution)/shard_map/all_to_all | solution.py:232
  84.2 0.6 reshape.21
  84.8 0.6 reshape.20
  85.4 12.4 %all-to-all-done.2 = f16[32,16,256]{2,1,0:T(8,128)(2,1)S(1)} async-done(((f16[32,16,256]{2,1,0:T(8,128)(2,1)}), f16[32,16,256]{2,1,0:T(8,128)(2,1)S(1)}, u32[]{:S(2)}, u32[]{:S(2)}) %all-to-all-start.2) | async-done | bytes 262176 | tf_op jit(solution)/shard_map/all_to_all | solution.py:232
  97.8 0.1 convert_element_type.19.full
  97.9 0.8 shard_map.63
  (4 shorter events, 0.0 us)
Async XLA Ops:
  0.6 0.9 copy-start
  1.6 0.8 copy-start.2
  2.3 0.8 copy-start.3
  5.3 43.2 %all-to-all-start = ((bf16[16,16,2560]{2,1,0:T(8,128)(2,1)}), bf16[16,16,2560]{2,1,0:T(8,128)(2,1)S(1)}, u32[]{:S(2)}, u32[]{:S(2)}) async-start(bf16[16,16,2560]{2,1,0:T(8,128)(2,1)} %get-tuple-element.8), calls=%async_computation | async-start | bytes 2621440 | tf_op jit(solution)/shard_map/all_to_all | solution.py:204
  17.3 5.9 %collective-permute-start.3 = (bf16[16,1024]{1,0:T(8,128)(2,1)S(1)}, bf16[16,1024]{1,0:T(8,128)(2,1)S(1)}, u32[]{:S(2)}, u32[]{:S(2)}) collective-permute-start(bf16[16,1024]{1,0:T(8,128)(2,1)S(1)} %get-tuple-element.12.own), channel_id=1, source_target_pairs={{16,0},{32,16},{48,32},{64,48},{80,64},{96,80},{112,96},{128,112},... | collective-permute-start | bytes 98312 | tf_op jit(solution)/shard_map/ppermute | solution.py:206
  20.2 4.0 %collective-permute-start.2 = (bf16[16,1024]{1,0:T(8,128)(2,1)S(1)}, bf16[16,1024]{1,0:T(8,128)(2,1)S(1)}, u32[]{:S(2)}, u32[]{:S(2)}) collective-permute-start(bf16[16,1024]{1,0:T(8,128)(2,1)S(1)} %get-tuple-element.12.own), channel_id=1, source_target_pairs={{0,16},{16,32},{32,48},{48,64},{64,80},{80,96},{96,112},{112,128},... | collective-permute-start | bytes 98312 | tf_op jit(solution)/shard_map/ppermute | solution.py:205
  48.5 12.0 %copy-start.1 = (bf16[27,16,256]{2,1,0:T(8,128)(2,1)S(1)}, bf16[27,16,256]{2,1,0:T(8,128)(2,1)}, u32[]{:S(2)}) copy-start(bf16[27,16,256]{2,1,0:T(8,128)(2,1)} %filters.1) | copy-start | bytes 663556
  49.9 24.3 %all-to-all-start.1 = ((f16[32,16,256]{2,1,0:T(8,128)(2,1)}), f16[32,16,256]{2,1,0:T(8,128)(2,1)S(1)}, u32[]{:S(2)}, u32[]{:S(2)}) async-start(f16[32,16,256]{2,1,0:T(8,128)(2,1)} %convert_element_type.16), calls=%async_computation.1 | async-start | bytes 524288 | tf_op jit(solution)/shard_map/all_to_all | solution.py:216
  61.2 13.3 %collective-permute-start = (f32[32,1024]{1,0:T(8,128)S(1)}, f32[32,1024]{1,0:T(8,128)S(1)}, u32[]{:S(2)}, u32[]{:S(2)}) collective-permute-start(f32[32,1024]{1,0:T(8,128)S(1)} %get-tuple-element.10), channel_id=1, source_target_pairs={{0,16},{16,32},{32,48},{48,64},{64,80},{80,96},{96,112},{112,128},... | collective-permute-start | bytes 393224 | tf_op jit(solution)/shard_map/ppermute | solution.py:225
  64.8 9.7 %collective-permute-start.1 = (f32[32,1024]{1,0:T(8,128)S(1)}, f32[32,1024]{1,0:T(8,128)S(1)}, u32[]{:S(2)}, u32[]{:S(2)}) collective-permute-start(f32[32,1024]{1,0:T(8,128)S(1)} %get-tuple-element.11), channel_id=1, source_target_pairs={{16,0},{32,16},{48,32},{64,48},{80,64},{96,80},{112,96},{128,112},... | collective-permute-start | bytes 393224 | tf_op jit(solution)/shard_map/ppermute | solution.py:226
  75.2 22.6 %all-to-all-start.2 = ((f16[32,16,256]{2,1,0:T(8,128)(2,1)}), f16[32,16,256]{2,1,0:T(8,128)(2,1)S(1)}, u32[]{:S(2)}, u32[]{:S(2)}) async-start(f16[32,16,256]{2,1,0:T(8,128)(2,1)} %broadcast_in_dim.2), calls=%async_computation.2 | async-start | bytes 524288 | tf_op jit(solution)/shard_map/all_to_all | solution.py:232

commit v5 on v4

--- a/solution.py
+++ b/solution.py
@@ -13,25 +13,29 @@
 F32 = jnp.float32
 HALF = jnp.float16
 ANY = pl.BlockSpec(memory_space=pl.ANY)
+SMEM = pl.BlockSpec(memory_space=pltpu.SMEM)
 FAR = pl.BlockSpec(memory_space=pltpu.HBM)
 VMEM = pl.BlockSpec(memory_space=pltpu.VMEM)
 TAPS = 27
 OWN = 16
 CELLS = 1024
 ROWS = TAPS * OWN
-WIDE = 2 * CELLS + 512
+WIDE = 2 * CELLS + 256
+HALF_ROWS = ROWS // 2
 SCALE = 1.0 / math.sqrt(32768)
 LIMIT = 48 * 1024 * 1024
-
-
-def call(body, outs, ins, scratch=(), flops=0, moved=0):
+PACK_LIMIT = 63 * 1024 * 1024
+OUTPUTS_FLOPS = 10**10
+
+
+def call(body, outs, ins, scratch=(), flops=0, moved=0, limit=LIMIT):
     return pl.pallas_call(
         body,
         out_shape=outs,
         in_specs=ins,
         out_specs=[VMEM] * len(outs),
         scratch_shapes=list(scratch),
-        compiler_params=pltpu.CompilerParams(vmem_limit_bytes=LIMIT),
+        compiler_params=pltpu.CompilerParams(vmem_limit_bytes=limit),
         cost_estimate=pl.CostEstimate(flops=flops, bytes_accessed=moved, transcendentals=0),
     )
 
@@ -52,7 +56,9 @@
     return jnp.where((at >= 0) & (at < 128), turned, 0.0)
 
 
-def pack_body(field_far, cot_far, filters_far, out, own_cot, field, cotangent, filters, arrived):
+def pack_body(
+    core, field_far, cot_far, filters_far, out, own_cot, field, cotangent, filters, arrived
+):
     pairs = ((field_far, field), (cot_far, cotangent), (filters_far, filters))
     copies = [pltpu.make_async_copy(a, b, arrived.at[n]) for n, (a, b) in enumerate(pairs)]
     for copy in copies:
@@ -70,15 +76,14 @@
                 out[c, :, CELLS + at : CELLS + at + 128] = mine
     copies[2].wait()
     lane = lanes((OWN, 128))
-    for g in range(4):
+    low = core[0] * 11
+    for g in range(2):
         parts = [jnp.zeros((OWN, 128), F32) for _ in range(16)]
         for j in range(8):
-            k = 8 * g + j
-            if k >= TAPS:
-                break
             here = (lane >= 16 * j) & (lane < 16 * j + 16)
+            tap = filters[pl.ds(low + 8 * g + j, 1)][0].astype(F32)
             for h in range(2):
-                block = filters[k, :, 128 * h : 128 * h + 128].astype(F32)
+                block = tap[:, 128 * h : 128 * h + 128]
                 for q in range(8):
                     step = (16 * (j - q)) % 128
                     turned = block if step == 0 else pltpu.roll(block, step, 1)
@@ -109,7 +114,7 @@
     return blocks
 
 
-def grad_body(gathered, below, own, above, out, shifted):
+def grad_body(core, gathered, below, own, above, keep, send, shifted):
     zero = jnp.zeros((OWN, 128), BF)
     for a, source in ((0, above), (1, own), (2, below)):
         for r in range(2):
@@ -133,10 +138,18 @@
         (((1,), (1,)), ((), ())),
         preferred_element_type=F32,
     )
-    power, scaled = scaled_down(total)
-    out[...] = jnp.zeros((32, 16, 256), F32)
-    for n in range(31):
-        rows = min(14, ROWS - 14 * n)
+    first = core[0] == 0
+    low, high = total[0:HALF_ROWS], total[HALF_ROWS:ROWS]
+    keep[...] = jnp.where(first, low, high)
+    send[0:HALF_ROWS, :] = jnp.where(first, high, low)
+    send[HALF_ROWS : HALF_ROWS + 256, :] = gathered[:, 2 * CELLS : WIDE].astype(F32)
+
+
+def chip_body(keep, swapped, out):
+    power, scaled = scaled_down(keep[...] + swapped[0:HALF_ROWS, :])
+    out[...] = jnp.zeros((16, 16, 256), F32)
+    for n in range(16):
+        rows = min(14, HALF_ROWS - 14 * n)
         out[n, 0:rows, :] = scaled[14 * n : 14 * n + rows, :]
         out[n, 14:16, :] = jnp.broadcast_to(power, (2, 256))
 
@@ -149,35 +162,45 @@
 
 def sum_body(parts, _after, out):
     total = jnp.zeros((14, 256), F32)
-    for n in range(32):
+    for n in range(16):
         total = total + parts[n, 0:14, :] * jnp.exp2(parts[n, 14:15, :] - 14.0)
     power, scaled = scaled_down(total * SCALE)
     out[0:14, :] = scaled
     out[14:16, :] = jnp.broadcast_to(power, (2, 256))
 
 
-def share_body(mine, _after, _too, out):
-    out[...] = mine[...]
-
-
-def finish_body(full, out):
-    for n in range(31):
-        rows = min(14, ROWS - 14 * n)
-        out[14 * n : 14 * n + rows, :] = full[n, 0:rows, :] * jnp.exp2(full[n, 14:15, :] - 14.0)
-
-
-def contributions_body(gathered, filters, up, down, mid, products):
+def finish_body(core, mine, other, out):
+    first = core[0] == 0
+    for n in range(16):
+        rows = min(14, HALF_ROWS - 14 * n)
+        ours = mine[n, 0:rows, :] * jnp.exp2(mine[n, 14:15, :] - 14.0)
+        theirs = other[n, 0:rows, :] * jnp.exp2(other[n, 14:15, :] - 14.0)
+        out[14 * n : 14 * n + rows, :] = jnp.where(first, ours, theirs)
+        at = HALF_ROWS + 14 * n
+        out[at : at + rows, :] = jnp.where(first, theirs, ours)
+
+
+def outputs_body(own, last, following, out):
+    out[...] = (own[...] + last[...] + following[...]).astype(BF)
+
+
+def contributions_body(core, gathered, filters, swapped, up, down, mid, products):
     products[...] = jnp.dot(
         filters[...].reshape(ROWS, 256), gathered[:, 0:CELLS], preferred_element_type=F32
     )
     for a, out in ((0, up), (1, mid), (2, down)):
         for n, block in enumerate(taps_sum(products, a, 1)):
             out[0:OWN, 128 * n : 128 * n + 128] = block
-    products[...] = lax.dot_general(
-        gathered[:, 2 * CELLS : 2 * CELLS + ROWS],
-        gathered[:, CELLS : 2 * CELLS],
-        (((0,), (0,)), ((), ())),
-        preferred_element_type=F32,
+    mine = gathered[:, 2 * CELLS : WIDE]
+    other = swapped[HALF_ROWS : HALF_ROWS + 256, :].astype(BF)
+    first = core[0] == 0
+    cells = gathered[:, CELLS : 2 * CELLS]
+    over = (((0,), (0,)), ((), ()))
+    products[0:256, :] = lax.dot_general(
+        jnp.where(first, mine, other), cells, over, preferred_element_type=F32
+    )
+    products[176:ROWS, :] = lax.dot_general(
+        jnp.where(first, other, mine), cells, over, preferred_element_type=F32
     )
     for a, out in ((0, down), (1, mid), (2, up)):
         for n, block in enumerate(taps_sum(products, a, -1)):
@@ -186,13 +209,15 @@
 
 def per_device(field, filters, cotangent):
     space = ("pair", "core")
+    core = lax.axis_index("core").astype(jnp.int32).reshape(1)
     up = [(i, i + 1) for i in range(31)]
     down = [(i + 1, i) for i in range(31)]
+    swap = [(0, 1), (1, 0)]
 
     packed, own_cot = call(
         pack_body,
         [shape((16, OWN, WIDE), BF), shape((OWN, CELLS), BF)],
-        [FAR] * 3,
+        [SMEM] + [FAR] * 3,
         [
             pltpu.VMEM((OWN, 2, 4, 128), BF),
             pltpu.VMEM((OWN, 2, 4, 128), BF),
@@ -200,42 +225,46 @@
             pltpu.SemaphoreType.DMA((3,)),
         ],
         moved=1 << 20,
-    )(field, cotangent, filters)
+        limit=PACK_LIMIT,
+    )(core, field, cotangent, filters)
     gathered = lax.all_to_all(packed, "chan", 0, 0).reshape(256, WIDE)
     below = lax.ppermute(own_cot, space, up)
     above = lax.ppermute(own_cot, space, down)
 
-    own_grad = call(
+    keep, send = call(
         grad_body,
-        [shape((32, 16, 256), F32)],
-        [VMEM] * 4,
+        [shape((HALF_ROWS, 256), F32), shape((HALF_ROWS + 256, 256), F32)],
+        [SMEM] + [VMEM] * 4,
         [pltpu.VMEM((ROWS, CELLS), BF)],
         flops=2 * ROWS * CELLS * 256,
         moved=1 << 20,
-    )(gathered, below, own_cot, above)[0]
-    parts = lax.all_to_all(own_grad.astype(HALF), space, 0, 0).astype(F32)
+    )(core, gathered, below, own_cot, above)
+    swapped = lax.ppermute(send, "core", swap)
+    chip = call(chip_body, [shape((16, 16, 256), F32)], [VMEM] * 2, moved=1 << 19)(keep, swapped)[0]
+    parts = lax.all_to_all(chip.astype(HALF), "pair", 0, 0).astype(F32)
     to_next, to_last, own_sums = call(
         contributions_body,
         [shape((2 * OWN, CELLS), F32)] * 3,
-        [VMEM] * 2,
+        [SMEM] + [VMEM] * 3,
         [pltpu.VMEM((ROWS, CELLS), F32)],
         flops=4 * ROWS * CELLS * 256,
         moved=1 << 20,
-    )(gathered, filters)
+    )(core, gathered, filters, swapped)
     from_last = lax.ppermute(to_next, space, up)
     from_next = lax.ppermute(to_last, space, down)
     mine = call(sum_body, [shape((16, 256), F32)], [VMEM, ANY], moved=1 << 19)(parts, own_sums)[0]
-    shared = call(share_body, [shape((16, 256), F32)], [VMEM, ANY, ANY], moved=1 << 14)(
-        mine, from_last, from_next
+    spread = jnp.broadcast_to(mine.astype(HALF)[None], (16, 16, 256))
+    full = lax.all_to_all(spread, "pair", 0, 0)
+    other = lax.ppermute(full, "core", swap)
+    weight_grad = call(finish_body, [shape((ROWS, 256), F32)], [SMEM] + [VMEM] * 2, moved=1 << 20)(
+        core, full.astype(F32), other.astype(F32)
     )[0]
-    shared = jnp.broadcast_to(shared.astype(HALF)[None], (32, 16, 256))
-    full = lax.all_to_all(shared, space, 0, 0).astype(F32)
-    outs = (own_sums + from_last + from_next).astype(BF)
+    outs = call(
+        outputs_body, [shape((2 * OWN, CELLS), BF)], [VMEM] * 3, flops=OUTPUTS_FLOPS, moved=1 << 18
+    )(own_sums, from_last, from_next)[0]
     out_field = outs[:OWN].reshape(field.shape)
     input_grad = outs[OWN:].reshape(field.shape)
-    weight_grad = call(finish_body, [shape((ROWS, 256), F32)], [VMEM], moved=1 << 20)(full)[0]
-    weight_grad = weight_grad.reshape(TAPS, OWN, 256)
-    return out_field, input_grad, weight_grad
+    return out_field, input_grad, weight_grad.reshape(TAPS, OWN, 256)
 
 
 def solution(mesh):

time: 99.7 us -> 92.6 us (0.929)
  waiting for transfers between devices: 45.2 us -> 35.6 us
  starting transfers between devices: 42.8 us -> 48 us
  local copies, waits for them, and re-layouts: 4.44 us -> 1.95 us
    ppermute x0 -> x2, starting transfers between devices: none -> 9.63 us  [the longest x1 6.28 us: per_device(): other = lax.ppermute(full, 'core', swap)]
    all_to_all x2, waiting for transfers between devices: 19.9 us -> 11.7 us  [the longest x1 9.19 us: per_device(): full = lax.all_to_all(spread, 'pair', 0, 0)]
    all_to_all x2, starting transfers between devices: 19.5 us -> 14.5 us  [the longest x1 8.39 us: per_device(): parts = lax.all_to_all(chip.astype(HALF), 'pair', 0, 0).astype(F32)]
    all_to_all x1, waiting for transfers between devices: 24.3 us -> 21.5 us  [per_device(): gathered = lax.all_to_all(packed, 'chan', 0, 0).reshape(256, WIDE)]
    unnamed x8 -> x4, local copies, waits for them, and re-layouts: 2.45 us -> 0.01 us
    ppermute x0 -> x2, waiting for transfers between devices: none -> 1.46 us  [the longest x1 1.46 us: per_device(): swapped = lax.ppermute(send, 'core', swap)]
    pallas_call x5 -> x6, Pallas kernels: 4.42 us -> 4.75 us  [the longest x1 2.5 us: per_device(): call(pack_body, [shape((16, OWN, WIDE), BF), shape((OWN, CELLS), BF)], [S...]
  transfers between devices with their start and end apart: 7 -> 9, of which waited for: 4 -> 5; matrix products, arithmetic and copies ran while one was open for 1% -> 2% of each run, Pallas kernels for 1% -> 1%
where the time goes in v5:
time: 92.6 us; the launch traced here: 92.1 us
  starting transfers between devices  48 us (52%)
  waiting for transfers between devices  35.6 us (38%)
  Pallas kernels  4.91 us (5%)
  local copies, waits for them, and re-layouts  1.95 us (2%)
    all_to_all x1, waiting for transfers between devices, per_device(): gathered = lax.all_to_all(packed, 'chan', 0, 0).reshape(256, WIDE)  21.5 us
    all_to_all x1, starting transfers between devices, per_device(): gathered = lax.all_to_all(packed, 'chan', 0, 0).reshape(256, WIDE)  12 us
    all_to_all x1, waiting for transfers between devices, per_device(): full = lax.all_to_all(spread, 'pair', 0, 0)  9.19 us
    all_to_all x1, starting transfers between devices, per_device(): parts = lax.all_to_all(chip.astype(HALF), 'pair', 0, 0).astype(F32)  8.39 us
    ppermute x1, starting transfers between devices, per_device(): other = lax.ppermute(full, 'core', swap)  6.28 us
    all_to_all x1, starting transfers between devices, per_device(): full = lax.all_to_all(spread, 'pair', 0, 0)  6.13 us
    ppermute x1, starting transfers between devices, per_device(): from_last = lax.ppermute(to_next, space, up)  4.09 us
    ppermute x1, starting transfers between devices, per_device(): swapped = lax.ppermute(send, 'core', swap)  3.36 us
  transfers between devices with their start and end apart: 9, of which 5 were waited for; matrix products, arithmetic and copies ran while one was open for 2% of the time, Pallas kernels for 1%

profile of v5, /device:TPU:1, one launch (start us, length us, event | category | flops | bytes accessed | tf_op | source)
XLA Modules:
  0.0 92.1 jit_solution(15434343247033699724)
XLA Ops:
  0.6 2.5 %shard_map.58 = (bf16[16,16,2304]{2,1,0:T(8,128)(2,1)}, bf16[16,1024]{1,0:T(8,128)(2,1)}) custom-call(s32[1]{0:T(128)} %bitcast.core, bf16[16,2,4,128]{3,2,1,0:T(4,128)(2,1)} %field_far.1, bf16[16,2,4,128]{3,2,1,0:T(4,128)(2,1)} %cot_far.1, bf16[27,16,256]{2,1,0:T(8,128)(2,1)} %filters.1), custom_call_target="tpu_custom_call" | custom-call | bytes 1048576 | tf_op jit(solution)/shard_map/pallas_call | solution.py:217
  3.1 0.0 copy-start.1
  3.2 12.0 %all-to-all-start = ((bf16[16,16,2304]{2,1,0:T(8,128)(2,1)}), bf16[16,16,2304]{2,1,0:T(8,128)(2,1)S(1)}, u32[]{:S(2)}, u32[]{:S(2)}) async-start(bf16[16,16,2304]{2,1,0:T(8,128)(2,1)} %get-tuple-element.10), calls=%async_computation | async-start | bytes 2359296 | tf_op jit(solution)/shard_map/all_to_all | solution.py:230
  15.2 0.0 copy-done.1
  15.2 2.9 %collective-permute-start.1 = (bf16[16,1024]{1,0:T(8,128)(2,1)S(1)}, bf16[16,1024]{1,0:T(8,128)(2,1)S(1)}, u32[]{:S(2)}, u32[]{:S(2)}) collective-permute-start(bf16[16,1024]{1,0:T(8,128)(2,1)S(1)} %copy-done.1), channel_id=1, source_target_pairs={{16,0},{32,16},{48,32},{64,48},{80,64},{96,80},{112,96},{128,112},... | collective-permute-start | bytes 98312 | tf_op jit(solution)/shard_map/ppermute | solution.py:232
  18.0 3.0 %collective-permute-start = (bf16[16,1024]{1,0:T(8,128)(2,1)S(1)}, bf16[16,1024]{1,0:T(8,128)(2,1)S(1)}, u32[]{:S(2)}, u32[]{:S(2)}) collective-permute-start(bf16[16,1024]{1,0:T(8,128)(2,1)S(1)} %copy-done.1), channel_id=1, source_target_pairs={{0,16},{16,32},{32,48},{48,64},{64,80},{80,96},{96,112},{112,128},... | collective-permute-start | bytes 98312 | tf_op jit(solution)/shard_map/ppermute | solution.py:231
  21.1 0.0 collective-permute-done.1.above
  21.1 1.0 %collective-permute-done.below = bf16[16,1024]{1,0:T(8,128)(2,1)S(1)} collective-permute-done((bf16[16,1024]{1,0:T(8,128)(2,1)S(1)}, bf16[16,1024]{1,0:T(8,128)(2,1)S(1)}, u32[]{:S(2)}, u32[]{:S(2)}) %collective-permute-start) | collective-permute-done | bytes 32800 | tf_op jit(solution)/shard_map/ppermute | solution.py:231
  22.1 21.5 %all-to-all-done = bf16[16,16,2304]{2,1,0:T(8,128)(2,1)S(1)} async-done(((bf16[16,16,2304]{2,1,0:T(8,128)(2,1)}), bf16[16,16,2304]{2,1,0:T(8,128)(2,1)S(1)}, u32[]{:S(2)}, u32[]{:S(2)}) %all-to-all-start) | async-done | bytes 1179680 | tf_op jit(solution)/shard_map/all_to_all | solution.py:230
  43.5 0.0 copy-start
  43.5 0.5 shard_map.59
  44.0 3.4 %collective-permute-start.2 = (f32[472,256]{1,0:T(8,128)S(1)}, f32[472,256]{1,0:T(8,128)S(1)}, u32[]{:S(2)}, u32[]{:S(2)}) collective-permute-start(f32[472,256]{1,0:T(8,128)S(1)} %get-tuple-element.12), channel_id=1, source_target_pairs={{0,16},{16,0},{1,17},{17,1},{2,18},{18,2},{3,19},{19,3},{4,20},{20... | collective-permute-start | bytes 1449992 | tf_op jit(solution)/shard_map/ppermute | solution.py:242
  47.4 1.5 %collective-permute-done.2.swapped = f32[472,256]{1,0:T(8,128)S(1)} collective-permute-done((f32[472,256]{1,0:T(8,128)S(1)}, f32[472,256]{1,0:T(8,128)S(1)}, u32[]{:S(2)}, u32[]{:S(2)}) %collective-permute-start.2) | collective-permute-done | bytes 483360 | tf_op jit(solution)/shard_map/ppermute | solution.py:242
  48.8 0.2 shard_map.62
  49.0 0.7 convert_element_type.15
  49.7 8.4 %all-to-all-start.1 = ((f16[16,16,256]{2,1,0:T(8,128)(2,1)}), f16[16,16,256]{2,1,0:T(8,128)(2,1)S(1)}, u32[]{:S(2)}, u32[]{:S(2)}) async-start(f16[16,16,256]{2,1,0:T(8,128)(2,1)} %convert_element_type.15), calls=%async_computation.1 | async-start | bytes 262144 | tf_op jit(solution)/shard_map/all_to_all | solution.py:244
  58.1 0.0 copy-done
  58.1 0.7 shard_map.60
  58.8 4.1 %collective-permute-start.3 = (f32[32,1024]{1,0:T(8,128)S(1)}, f32[32,1024]{1,0:T(8,128)S(1)}, u32[]{:S(2)}, u32[]{:S(2)}) collective-permute-start(f32[32,1024]{1,0:T(8,128)S(1)} %get-tuple-element.14), channel_id=1, source_target_pairs={{0,16},{16,32},{32,48},{48,64},{64,80},{80,96},{96,112},{112,128},... | collective-permute-start | bytes 393224 | tf_op jit(solution)/shard_map/ppermute | solution.py:253
  62.9 1.9 %collective-permute-start.4 = (f32[32,1024]{1,0:T(8,128)S(1)}, f32[32,1024]{1,0:T(8,128)S(1)}, u32[]{:S(2)}, u32[]{:S(2)}) collective-permute-start(f32[32,1024]{1,0:T(8,128)S(1)} %get-tuple-element.15), channel_id=1, source_target_pairs={{16,0},{32,16},{48,32},{64,48},{80,64},{96,80},{112,96},{128,112},... | collective-permute-start | bytes 393224 | tf_op jit(solution)/shard_map/ppermute | solution.py:254
  64.9 2.5 %all-to-all-done.1 = f16[16,16,256]{2,1,0:T(8,128)(2,1)S(1)} async-done(((f16[16,16,256]{2,1,0:T(8,128)(2,1)}), f16[16,16,256]{2,1,0:T(8,128)(2,1)S(1)}, u32[]{:S(2)}, u32[]{:S(2)}) %all-to-all-start.1) | async-done | bytes 131104 | tf_op jit(solution)/shard_map/all_to_all | solution.py:244
  67.4 0.2 shard_map.63
  67.5 0.7 broadcast_in_dim.2
  68.2 6.1 %all-to-all-start.2 = ((f16[16,16,256]{2,1,0:T(8,128)(2,1)}), f16[16,16,256]{2,1,0:T(8,128)(2,1)S(1)}, u32[]{:S(2)}, u32[]{:S(2)}) async-start(f16[16,16,256]{2,1,0:T(8,128)(2,1)} %broadcast_in_dim.2), calls=%async_computation.2 | async-start | bytes 262144 | tf_op jit(solution)/shard_map/all_to_all | solution.py:257
  74.4 0.0 collective-permute-done.3.last
  74.4 0.0 collective-permute-done.4.following
  74.4 9.2 %all-to-all-done.2 = f16[16,16,256]{2,1,0:T(8,128)(2,1)S(1)} async-done(((f16[16,16,256]{2,1,0:T(8,128)(2,1)}), f16[16,16,256]{2,1,0:T(8,128)(2,1)S(1)}, u32[]{:S(2)}, u32[]{:S(2)}) %all-to-all-start.2) | async-done | bytes 131104 | tf_op jit(solution)/shard_map/all_to_all | solution.py:257
  83.6 6.3 %collective-permute-start.5 = (f16[16,16,256]{2,1,0:T(8,128)(2,1)S(1)}, f16[16,16,256]{2,1,0:T(8,128)(2,1)S(1)}, u32[]{:S(2)}, u32[]{:S(2)}) collective-permute-start(f16[16,16,256]{2,1,0:T(8,128)(2,1)S(1)} %all-to-all-done.2), channel_id=1, source_target_pairs={{0,16},{16,0},{1,17},{17,1},{2,18},{18,2},{3,19},{19,3},{4,20},{20... | collective-permute-start | bytes 393224 | tf_op jit(solution)/shard_map/ppermute | solution.py:258
  89.9 0.6 reshape.25
  90.5 0.6 reshape.24
  91.2 0.0 collective-permute-done.5
  91.2 0.8 shard_map.64
  (6 shorter events, 0.1 us)
Async XLA Ops:
  3.1 12.0 %copy-start.1 = (bf16[16,1024]{1,0:T(8,128)(2,1)S(1)}, bf16[16,1024]{1,0:T(8,128)(2,1)}, u32[]{:S(2)}) copy-start(bf16[16,1024]{1,0:T(8,128)(2,1)} %get-tuple-element.11.own) | copy-start | bytes 98308
  3.2 40.4 %all-to-all-start = ((bf16[16,16,2304]{2,1,0:T(8,128)(2,1)}), bf16[16,16,2304]{2,1,0:T(8,128)(2,1)S(1)}, u32[]{:S(2)}, u32[]{:S(2)}) async-start(bf16[16,16,2304]{2,1,0:T(8,128)(2,1)} %get-tuple-element.10), calls=%async_computation | async-start | bytes 2359296 | tf_op jit(solution)/shard_map/all_to_all | solution.py:230
  15.2 5.9 %collective-permute-start.1 = (bf16[16,1024]{1,0:T(8,128)(2,1)S(1)}, bf16[16,1024]{1,0:T(8,128)(2,1)S(1)}, u32[]{:S(2)}, u32[]{:S(2)}) collective-permute-start(bf16[16,1024]{1,0:T(8,128)(2,1)S(1)} %copy-done.1), channel_id=1, source_target_pairs={{16,0},{32,16},{48,32},{64,48},{80,64},{96,80},{112,96},{128,112},... | collective-permute-start | bytes 98312 | tf_op jit(solution)/shard_map/ppermute | solution.py:232
  18.0 4.0 %collective-permute-start = (bf16[16,1024]{1,0:T(8,128)(2,1)S(1)}, bf16[16,1024]{1,0:T(8,128)(2,1)S(1)}, u32[]{:S(2)}, u32[]{:S(2)}) collective-permute-start(bf16[16,1024]{1,0:T(8,128)(2,1)S(1)} %copy-done.1), channel_id=1, source_target_pairs={{0,16},{16,32},{32,48},{48,64},{64,80},{80,96},{96,112},{112,128},... | collective-permute-start | bytes 98312 | tf_op jit(solution)/shard_map/ppermute | solution.py:231
  43.5 14.6 %copy-start = (bf16[27,16,256]{2,1,0:T(8,128)(2,1)S(1)}, bf16[27,16,256]{2,1,0:T(8,128)(2,1)}, u32[]{:S(2)}) copy-start(bf16[27,16,256]{2,1,0:T(8,128)(2,1)} %filters.1) | copy-start | bytes 663556
  44.0 4.8 %collective-permute-start.2 = (f32[472,256]{1,0:T(8,128)S(1)}, f32[472,256]{1,0:T(8,128)S(1)}, u32[]{:S(2)}, u32[]{:S(2)}) collective-permute-start(f32[472,256]{1,0:T(8,128)S(1)} %get-tuple-element.12), channel_id=1, source_target_pairs={{0,16},{16,0},{1,17},{17,1},{2,18},{18,2},{3,19},{19,3},{4,20},{20... | collective-permute-start | bytes 1449992 | tf_op jit(solution)/shard_map/ppermute | solution.py:242
  49.7 17.6 %all-to-all-start.1 = ((f16[16,16,256]{2,1,0:T(8,128)(2,1)}), f16[16,16,256]{2,1,0:T(8,128)(2,1)S(1)}, u32[]{:S(2)}, u32[]{:S(2)}) async-start(f16[16,16,256]{2,1,0:T(8,128)(2,1)} %convert_element_type.15), calls=%async_computation.1 | async-start | bytes 262144 | tf_op jit(solution)/shard_map/all_to_all | solution.py:244
  58.8 15.5 %collective-permute-start.3 = (f32[32,1024]{1,0:T(8,128)S(1)}, f32[32,1024]{1,0:T(8,128)S(1)}, u32[]{:S(2)}, u32[]{:S(2)}) collective-permute-start(f32[32,1024]{1,0:T(8,128)S(1)} %get-tuple-element.14), channel_id=1, source_target_pairs={{0,16},{16,32},{32,48},{48,64},{64,80},{80,96},{96,112},{112,128},... | collective-permute-start | bytes 393224 | tf_op jit(solution)/shard_map/ppermute | solution.py:253
  62.9 11.4 %collective-permute-start.4 = (f32[32,1024]{1,0:T(8,128)S(1)}, f32[32,1024]{1,0:T(8,128)S(1)}, u32[]{:S(2)}, u32[]{:S(2)}) collective-permute-start(f32[32,1024]{1,0:T(8,128)S(1)} %get-tuple-element.15), channel_id=1, source_target_pairs={{16,0},{32,16},{48,32},{64,48},{80,64},{96,80},{112,96},{128,112},... | collective-permute-start | bytes 393224 | tf_op jit(solution)/shard_map/ppermute | solution.py:254
  68.2 15.4 %all-to-all-start.2 = ((f16[16,16,256]{2,1,0:T(8,128)(2,1)}), f16[16,16,256]{2,1,0:T(8,128)(2,1)S(1)}, u32[]{:S(2)}, u32[]{:S(2)}) async-start(f16[16,16,256]{2,1,0:T(8,128)(2,1)} %broadcast_in_dim.2), calls=%async_computation.2 | async-start | bytes 262144 | tf_op jit(solution)/shard_map/all_to_all | solution.py:257
  83.6 7.6 %collective-permute-start.5 = (f16[16,16,256]{2,1,0:T(8,128)(2,1)S(1)}, f16[16,16,256]{2,1,0:T(8,128)(2,1)S(1)}, u32[]{:S(2)}, u32[]{:S(2)}) collective-permute-start(f16[16,16,256]{2,1,0:T(8,128)(2,1)S(1)} %all-to-all-done.2), channel_id=1, source_target_pairs={{0,16},{16,0},{1,17},{17,1},{2,18},{18,2},{3,19},{19,3},{4,20},{20... | collective-permute-start | bytes 393224 | tf_op jit(solution)/shard_map/ppermute | solution.py:258

commit v6 on v5

v6 whole, which is shorter than its diff:
```python
import functools
import math

import jax
import jax.numpy as jnp
from jax import lax
from jax.experimental import pallas as pl
from jax.experimental.pallas import tpu as pltpu
from jax.sharding import Mesh
from jax.sharding import PartitionSpec as P

BF = jnp.bfloat16
F32 = jnp.float32
HALF = jnp.float16
ANY = pl.BlockSpec(memory_space=pl.ANY)
SMEM = pl.BlockSpec(memory_space=pltpu.SMEM)
FAR = pl.BlockSpec(memory_space=pltpu.HBM)
VMEM = pl.BlockSpec(memory_space=pltpu.VMEM)
TAPS = 27
OWN = 16
CELLS = 1024
ROWS = TAPS * OWN
WIDE = 2 * CELLS + 256
PART = ROWS // 8
SCALE = 1.0 / math.sqrt(32768)
LIMIT = 16 * 1024 * 1024
PACK_LIMIT = 63 * 1024 * 1024
OUTPUTS_FLOPS = 10**10


def call(body, outs, ins, scratch=(), flops=0, moved=0, limit=LIMIT, outs_at=None):
    return pl.pallas_call(
        body,
        out_shape=outs,
        in_specs=ins,
        out_specs=outs_at or [VMEM] * len(outs),
        scratch_shapes=list(scratch),
        compiler_params=pltpu.CompilerParams(vmem_limit_bytes=limit),
        cost_estimate=pl.CostEstimate(flops=flops, bytes_accessed=moved, transcendentals=0),
    )


def shape(dims, kind):
    return jax.ShapeDtypeStruct(dims, kind)


def lanes(dims):
    return lax.broadcasted_iota(jnp.int32, dims, len(dims) - 1)


def moved_by(block, step):
    if step == 0:
        return block
    at = lanes(block.shape) + step
    turned = pltpu.roll(block, (-step) % 128, 1)
    return jnp.where((at >= 0) & (at < 128), turned, 0.0)


def pack_body(
    core, field_far, cot_far, filters_far, out, own_cot, field, cotangent, filters, cells, taps, arrived, sent
):
    pairs = ((field_far, field), (cot_far, cotangent), (filters_far, filters))
    copies = [pltpu.make_async_copy(a, b, arrived.at[n]) for n, (a, b) in enumerate(pairs)]
    for copy in copies:
        copy.start()
    copies[0].wait()
    copies[1].wait()
    for r in range(2):
        for z in range(4):
            at = 128 * (4 * r + z)
            mine = cotangent[:, r, z, :]
            own_cot[:, at : at + 128] = mine
            cells[:, at : at + 128] = field[:, r, z, :]
            cells[:, CELLS + at : CELLS + at + 128] = mine
    sends = [
        pltpu.make_async_copy(cells, out.at[c, :, pl.ds(0, 2 * CELLS)], sent.at[c]) for c in range(16)
    ]
    for send in sends:
        send.start()
    copies[2].wait()
    lane = lanes((OWN, 128))
    low = core[0] * 11
    for g in range(2):
        parts = [jnp.zeros((OWN, 128), F32) for _ in range(16)]
        for j in range(8):
            here = (lane >= 16 * j) & (lane < 16 * j + 16)
            tap = filters[pl.ds(low + 8 * g + j, 1)][0].astype(F32)
            for h in range(2):
                block = tap[:, 128 * h : 128 * h + 128]
                for q in range(8):
                    step = (16 * (j - q)) % 128
                    turned = block if step == 0 else pltpu.roll(block, step, 1)
                    parts[8 * h + q] = jnp.where(here, turned, parts[8 * h + q])
        for c in range(16):
            taps[c, :, 128 * g : 128 * g + 128] = parts[c].astype(BF)
    last = pltpu.make_async_copy(taps, out.at[:, :, pl.ds(2 * CELLS, 256)], sent.at[16])
    last.start()
    for send in sends:
        send.wait()
    last.wait()


def taps_sum(products, a, sign):
    blocks = []
    for r in range(2):
        for z in range(4):
            total = None
            for c in range(3):
                column = None
                for b in range(3):
                    source = z + sign * 2 * (b - 1)
                    if source < 0 or source > 3:
                        continue
                    k = 9 * a + 3 * b + c
                    lane = 128 * (4 * r + source)
                    part = products[16 * k : 16 * k + 16, lane : lane + 128]
                    column = part if column is None else column + part
                column = moved_by(column, sign * 2 * (c - 1))
                total = column if total is None else total + column
            blocks.append(total)
    return blocks


def grad_body(gathered, below, own, above, out, shifted):
    zero = jnp.zeros((OWN, 128), BF)
    for a, source in ((0, above), (1, own), (2, below)):
        for r in range(2):
            rolled = []
            for z in range(4):
                lane = 128 * (4 * r + z)
                block = source[:, lane : lane + 128].astype(F32)
                rolled.append([moved_by(block, -2 * (c - 1)).astype(BF) for c in range(3)])
            for z in range(4):
                for b in range(3):
                    at = z - 2 * (b - 1)
                    for c in range(3):
                        k = 9 * a + 3 * b + c
                        lane = 128 * (4 * r + z)
                        shifted[16 * k : 16 * k + 16, lane : lane + 128] = (
                            rolled[at][c] if 0 <= at < 4 else zero
                        )
    total = lax.dot_general(
        shifted[...],
        gathered[:, 0:CELLS],
        (((1,), (1,)), ((), ())),
        preferred_element_type=F32,
    )
    power, scaled = scaled_down(total)
    for n in range(8):
        out[n, 0:PART, :] = scaled[PART * n : PART * n + PART, :]
        out[n, PART : PART + 2, :] = jnp.broadcast_to(power, (2, 256))


def scaled_down(values):
    most = jnp.full((1, 256), jnp.max(jnp.abs(values)), F32)
    power = jnp.ceil(jnp.log2(jnp.maximum(most, 2.0**-100)))
    return power, values * jnp.exp2(14.0 - power)


def sum_body(factor, peers, parts, _after, out):
    total = jnp.zeros((PART, 256), F32)
    for n in range(peers):
        total = total + parts[n, 0:PART, :] * jnp.exp2(parts[n, PART : PART + 1, :] - 14.0)
    power, scaled = scaled_down(total * factor)
    out[0:PART, :] = scaled
    out[PART : PART + 2, :] = jnp.broadcast_to(power, (2, 256))


def finish_body(full, out):
    for n in range(8):
        scale = jnp.exp2(full[n, PART : PART + 1, :] - 14.0)
        out[PART * n : PART * n + PART, :] = full[n, 0:PART, :] * scale


def outputs_body(own, near, far, out_field, input_grad):
    for out, at in ((out_field, 0), (input_grad, OWN)):
        for r in range(2):
            for z in range(4):
                here = (slice(at, at + OWN), slice(128 * (4 * r + z), 128 * (4 * r + z) + 128))
                out[:, r, z, :] = (own[here] + near[here] + far[here]).astype(BF)


def contributions_body(core, gathered, filters, swapped, near, far, mid, products):
    first = core[0] == 0
    products[...] = jnp.dot(
        filters[...].reshape(ROWS, 256), gathered[:, 0:CELLS], preferred_element_type=F32
    )
    place(products, 1, first, 0, near, far, mid)
    mine = gathered[:, 2 * CELLS : WIDE]
    other = swapped[...]
    cells = gathered[:, CELLS : 2 * CELLS]
    over = (((0,), (0,)), ((), ()))
    products[0:256, :] = lax.dot_general(
        jnp.where(first, mine, other), cells, over, preferred_element_type=F32
    )
    products[176:ROWS, :] = lax.dot_general(
        jnp.where(first, other, mine), cells, over, preferred_element_type=F32
    )
    place(products, -1, first, OWN, near, far, mid)


def place(products, sign, first, at, near, far, mid):
    following, last = taps_sum(products, 1 - sign, sign), taps_sum(products, 1 + sign, sign)
    for n, block in enumerate(taps_sum(products, 1, sign)):
        here = (slice(at, at + OWN), slice(128 * n, 128 * n + 128))
        mid[here] = block
        near[here] = jnp.where(first, following[n], last[n])
        far[here] = jnp.where(first, last[n], following[n])


def per_device(field, filters, cotangent):
    space = ("far", "near", "core")
    core = lax.axis_index("core").astype(jnp.int32).reshape(1)
    up = [(i, i + 1) for i in range(31)]
    down = [(i + 1, i) for i in range(31)]
    swap = [(0, 1), (1, 0)]
    across = [pair for i in range(1, 31, 2) for pair in ((i, i + 1), (i + 1, i))]

    packed, own_cot = call(
        pack_body,
        [shape((16, OWN, WIDE), BF), shape((OWN, CELLS), BF)],
        [SMEM] + [FAR] * 3,
        [
            pltpu.VMEM((OWN, 2, 4, 128), BF),
            pltpu.VMEM((OWN, 2, 4, 128), BF),
            pltpu.VMEM((TAPS, OWN, 256), BF),
            pltpu.VMEM((OWN, 2 * CELLS), BF),
            pltpu.VMEM((16, OWN, 256), BF),
            pltpu.SemaphoreType.DMA((3,)),
            pltpu.SemaphoreType.DMA((17,)),
        ],
        moved=1 << 20,
        limit=PACK_LIMIT,
        outs_at=[FAR, VMEM],
    )(core, field, cotangent, filters)
    gathered = lax.all_to_all(packed, "chan", 0, 0).reshape(256, WIDE)
    below = lax.ppermute(own_cot, space, up)
    above = lax.ppermute(own_cot, space, down)

    swapped = lax.ppermute(gathered[:, 2 * CELLS :], "core", swap)
    own_grad = call(
        grad_body,
        [shape((8, PART + 2, 256), F32)],
        [VMEM] * 4,
        [pltpu.VMEM((ROWS, CELLS), BF)],
        flops=2 * ROWS * CELLS * 256,
        moved=1 << 20,
    )(gathered, below, own_cot, above)[0]
    parts = lax.all_to_all(own_grad.astype(HALF), ("near", "core"), 0, 0).astype(F32)
    to_near, to_far, own_sums = call(
        contributions_body,
        [shape((2 * OWN, CELLS), F32)] * 3,
        [SMEM] + [VMEM] * 3,
        [pltpu.VMEM((ROWS, CELLS), F32)],
        flops=4 * ROWS * CELLS * 256,
        moved=1 << 20,
    )(core, gathered, filters, swapped)
    from_far = lax.ppermute(to_far, space, across)
    from_near = lax.ppermute(to_near, "core", swap)

    def summed(factor, peers, parts):
        body = functools.partial(sum_body, factor, peers)
        return call(body, [shape((PART + 2, 256), F32)], [VMEM, ANY], moved=1 << 19)(parts, own_sums)[0]

    def spread(part, peers, axes):
        many = jnp.broadcast_to(part.astype(HALF)[None], (peers,) + part.shape)
        return lax.all_to_all(many, axes, 0, 0).astype(F32)

    row = summed(1.0, 8, parts)
    mine = summed(SCALE, 4, spread(row, 4, "far"))
    full = spread(mine, 8, ("near", "core"))
    weight_grad = call(finish_body, [shape((ROWS, 256), F32)], [VMEM], moved=1 << 20)(full)[0]
    out_field, input_grad = call(
        outputs_body, [shape(field.shape, BF)] * 2, [VMEM] * 3, flops=OUTPUTS_FLOPS, moved=1 << 18
    )(own_sums, from_near, from_far)
    return out_field, input_grad, weight_grad.reshape(TAPS, OWN, 256)


def solution(mesh):
    fine = Mesh(mesh.devices.reshape(4, 4, 2, 16), ("far", "near", "core", "chan"))
    cells = P("chan", ("far", "near", "core"), None, None)
    taps = P(None, "chan", None)
    return jax.shard_map(
        per_device,
        mesh=fine,
        in_specs=(cells, taps, cells),
        out_specs=(cells, cells, taps),
        check_vma=False,
    )
```

time: 92.6 us -> 86.2 us (0.931); the launches traced: 92.1 us -> 84.7 us
  starting transfers between devices: 48 us -> 42.3 us
  waiting for transfers between devices: 35.6 us -> 33.3 us
  Pallas kernels: 4.91 us -> 6.07 us
    ppermute x4 -> x3, starting transfers between devices: 15.6 us -> 7.18 us  [the longest x1 3.17 us: per_device(): from_near = lax.ppermute(to_near, 'core', swap)]
    all_to_all x2 -> x3, starting transfers between devices: 14.5 us -> 17.2 us  [the longest x2 11.6 us: spread(): return lax.all_to_all(many, axes, 0, 0).astype(F32)]
    all_to_all x2 -> x3, waiting for transfers between devices: 11.7 us -> 9.56 us  [the longest x2 7.36 us: spread(): return lax.all_to_all(many, axes, 0, 0).astype(F32)]
    reshape x2 -> x0, local copies, waits for them, and re-layouts: 1.26 us -> none  [the longest x1 0.63 us: per_device(): input_grad = outs[OWN:].reshape(field.shape)]
  transfers between devices with their start and end apart: 9 -> 9, of which waited for: 5 -> 6; matrix products, arithmetic and copies ran while one was open for 2% -> 1% of each run, Pallas kernels for 1% -> 2%
where the time goes in v6:
time: 86.2 us; the launch traced here: 84.7 us
  starting transfers between devices  42.3 us (49%)
  waiting for transfers between devices  33.3 us (39%)
  Pallas kernels  6.07 us (7%)
  local copies, waits for them, and re-layouts  1.39 us (2%)
    all_to_all x1, waiting for transfers between devices, per_device(): gathered = lax.all_to_all(packed, 'chan', 0, 0).reshape(256, WIDE)  21.5 us
    all_to_all x1, starting transfers between devices, per_device(): gathered = lax.all_to_all(packed, 'chan', 0, 0).reshape(256, WIDE)  12 us
    all_to_all x2, starting transfers between devices, spread(): return lax.all_to_all(many, axes, 0, 0).astype(F32)  11.6 us
    all_to_all x2, waiting for transfers between devices, spread(): return lax.all_to_all(many, axes, 0, 0).astype(F32)  7.36 us
    all_to_all x1, starting transfers between devices, per_device(): lax.all_to_all(own_grad.astype(HALF), ('near', 'core'), 0, 0).astype(F32)  5.66 us
    ppermute x1, starting transfers between devices, per_device(): from_near = lax.ppermute(to_near, 'core', swap)  3.17 us
    ppermute x1, starting transfers between devices, per_device(): below = lax.ppermute(own_cot, space, up)  3.02 us
    ppermute x1, starting transfers between devices, per_device(): above = lax.ppermute(own_cot, space, down)  2.86 us
  transfers between devices with their start and end apart: 9, of which 6 were waited for; matrix products, arithmetic and copies ran while one was open for 1% of the time, Pallas kernels for 2%

profile of v6, /device:TPU:1, one launch (start us, length us, event | category | flops | bytes accessed | tf_op | source)
XLA Modules:
  0.0 84.7 jit_solution(11872702380259300385)
XLA Ops:
  0.6 2.7 %shard_map.58 = (bf16[16,16,2304]{2,1,0:T(8,128)(2,1)}, bf16[16,1024]{1,0:T(8,128)(2,1)}) custom-call(s32[1]{0:T(128)} %bitcast.core, bf16[16,2,4,128]{3,2,1,0:T(4,128)(2,1)} %field_far.1, bf16[16,2,4,128]{3,2,1,0:T(4,128)(2,1)} %cot_far.1, bf16[27,16,256]{2,1,0:T(8,128)(2,1)} %filters.1), custom_call_target="tpu_custom_call" | custom-call | bytes 1048576 | tf_op jit(solution)/shard_map/pallas_call | solution.py:219
  3.4 0.0 copy-start.1
  3.4 12.0 %all-to-all-start = ((bf16[16,16,2304]{2,1,0:T(8,128)(2,1)}), bf16[16,16,2304]{2,1,0:T(8,128)(2,1)S(1)}, u32[]{:S(2)}, u32[]{:S(2)}) async-start(bf16[16,16,2304]{2,1,0:T(8,128)(2,1)} %get-tuple-element.10), calls=%async_computation | async-start | bytes 2359296 | tf_op jit(solution)/shard_map/all_to_all | solution.py:236
  15.4 0.0 copy-done.1
  15.4 2.9 %collective-permute-start.4 = (bf16[16,1024]{1,0:T(8,128)(2,1)S(1)}, bf16[16,1024]{1,0:T(8,128)(2,1)S(1)}, u32[]{:S(2)}, u32[]{:S(2)}) collective-permute-start(bf16[16,1024]{1,0:T(8,128)(2,1)S(1)} %copy-done.1), channel_id=1, source_target_pairs={{16,0},{32,16},{48,32},{64,48},{80,64},{96,80},{112,96},{128,112},... | collective-permute-start | bytes 98312 | tf_op jit(solution)/shard_map/ppermute | solution.py:238
  18.3 3.0 %collective-permute-start.3 = (bf16[16,1024]{1,0:T(8,128)(2,1)S(1)}, bf16[16,1024]{1,0:T(8,128)(2,1)S(1)}, u32[]{:S(2)}, u32[]{:S(2)}) collective-permute-start(bf16[16,1024]{1,0:T(8,128)(2,1)S(1)} %copy-done.1), channel_id=1, source_target_pairs={{0,16},{16,32},{32,48},{48,64},{64,80},{80,96},{96,112},{112,128},... | collective-permute-start | bytes 98312 | tf_op jit(solution)/shard_map/ppermute | solution.py:237
  21.3 0.0 collective-permute-done.4.above
  21.3 1.0 %collective-permute-done.3.below = bf16[16,1024]{1,0:T(8,128)(2,1)S(1)} collective-permute-done((bf16[16,1024]{1,0:T(8,128)(2,1)S(1)}, bf16[16,1024]{1,0:T(8,128)(2,1)S(1)}, u32[]{:S(2)}, u32[]{:S(2)}) %collective-permute-start.3) | collective-permute-done | bytes 32800 | tf_op jit(solution)/shard_map/ppermute | solution.py:237
  22.3 21.5 %all-to-all-done = bf16[16,16,2304]{2,1,0:T(8,128)(2,1)S(1)} async-done(((bf16[16,16,2304]{2,1,0:T(8,128)(2,1)}), bf16[16,16,2304]{2,1,0:T(8,128)(2,1)S(1)}, u32[]{:S(2)}, u32[]{:S(2)}) %all-to-all-start) | async-done | bytes 1179680 | tf_op jit(solution)/shard_map/all_to_all | solution.py:236
  43.8 0.0 copy-start
  43.8 0.6 shard_map.61
  44.4 0.7 convert_element_type.18
  45.1 5.7 %all-to-all-start.1 = ((f16[8,56,256]{2,1,0:T(8,128)(2,1)}), f16[8,56,256]{2,1,0:T(8,128)(2,1)S(1)}, u32[]{:S(2)}, u32[]{:S(2)}) async-start(f16[8,56,256]{2,1,0:T(8,128)(2,1)} %convert_element_type.18), calls=%async_computation.1 | async-start | bytes 458752 | tf_op jit(solution)/shard_map/all_to_all | solution.py:249
  50.8 1.9 %collective-permute-start = (bf16[256,256]{1,0:T(8,128)(2,1)S(1)}, bf16[256,256]{1,0:T(8,128)(2,1)S(1)}, u32[]{:S(2)}, u32[]{:S(2)}) collective-permute-start(bf16[256,256]{1,0:T(8,128)(2,1)S(1)} %slice.4), channel_id=1, source_target_pairs={{0,16},{16,0},{1,17},{17,1},{2,18},{18,2},{3,19},{19,3},{4,20},{20... | collective-permute-start | bytes 393224 | tf_op jit(solution)/shard_map/ppermute | solution.py:240
  52.7 1.3 %collective-permute-done.swapped = bf16[256,256]{1,0:T(8,128)(2,1)S(1)} collective-permute-done((bf16[256,256]{1,0:T(8,128)(2,1)S(1)}, bf16[256,256]{1,0:T(8,128)(2,1)S(1)}, u32[]{:S(2)}, u32[]{:S(2)}) %collective-permute-start) | collective-permute-done | bytes 131104 | tf_op jit(solution)/shard_map/ppermute | solution.py:240
  54.1 0.0 copy-done
  54.1 0.7 shard_map.59
  54.8 2.2 %all-to-all-done.1 = f16[8,56,256]{2,1,0:T(8,128)(2,1)S(1)} async-done(((f16[8,56,256]{2,1,0:T(8,128)(2,1)}), f16[8,56,256]{2,1,0:T(8,128)(2,1)S(1)}, u32[]{:S(2)}, u32[]{:S(2)}) %all-to-all-start.1) | async-done | bytes 229408 | tf_op jit(solution)/shard_map/all_to_all | solution.py:249
  57.0 0.2 shard_map.62
  57.2 0.7 broadcast_in_dim.4
  57.9 5.9 %all-to-all-start.2 = ((f16[4,56,256]{2,1,0:T(8,128)(2,1)}), f16[4,56,256]{2,1,0:T(8,128)(2,1)S(1)}, u32[]{:S(2)}, u32[]{:S(2)}) async-start(f16[4,56,256]{2,1,0:T(8,128)(2,1)} %broadcast_in_dim.4), calls=%async_computation.2 | async-start | bytes 229376 | tf_op jit(solution)/shard_map/all_to_all | solution.py:267
  63.8 3.2 %collective-permute-start.1 = (f32[32,1024]{1,0:T(8,128)S(1)}, f32[32,1024]{1,0:T(8,128)S(1)}, u32[]{:S(2)}, u32[]{:S(2)}) collective-permute-start(f32[32,1024]{1,0:T(8,128)S(1)} %get-tuple-element.12), channel_id=1, source_target_pairs={{0,16},{16,0},{1,17},{17,1},{2,18},{18,2},{3,19},{19,3},{4,20},{20... | collective-permute-start | bytes 393224 | tf_op jit(solution)/shard_map/ppermute | solution.py:259
  67.0 2.1 %collective-permute-start.2 = (f32[32,1024]{1,0:T(8,128)S(1)}, f32[32,1024]{1,0:T(8,128)S(1)}, u32[]{:S(2)}, u32[]{:S(2)}) collective-permute-start(f32[32,1024]{1,0:T(8,128)S(1)} %get-tuple-element.13), channel_id=1, source_target_pairs={{16,32},{32,16},{48,64},{64,48},{80,96},{96,80},{112,128},{128,112... | collective-permute-start | bytes 393224 | tf_op jit(solution)/shard_map/ppermute | solution.py:258
  69.1 2.0 %all-to-all-done.2 = f16[4,56,256]{2,1,0:T(8,128)(2,1)S(1)} async-done(((f16[4,56,256]{2,1,0:T(8,128)(2,1)}), f16[4,56,256]{2,1,0:T(8,128)(2,1)S(1)}, u32[]{:S(2)}, u32[]{:S(2)}) %all-to-all-start.2) | async-done | bytes 114720 | tf_op jit(solution)/shard_map/all_to_all | solution.py:267
  71.1 0.2 shard_map.63
  71.2 0.7 broadcast_in_dim.5
  71.9 5.6 %all-to-all-start.3 = ((f16[8,56,256]{2,1,0:T(8,128)(2,1)}), f16[8,56,256]{2,1,0:T(8,128)(2,1)S(1)}, u32[]{:S(2)}, u32[]{:S(2)}) async-start(f16[8,56,256]{2,1,0:T(8,128)(2,1)} %broadcast_in_dim.5), calls=%async_computation.3 | async-start | bytes 458752 | tf_op jit(solution)/shard_map/all_to_all | solution.py:267
  77.6 0.0 collective-permute-done.1.near
  77.6 0.0 collective-permute-done.2.far
  77.6 0.8 shard_map.60
  78.4 5.4 %all-to-all-done.3 = f16[8,56,256]{2,1,0:T(8,128)(2,1)S(1)} async-done(((f16[8,56,256]{2,1,0:T(8,128)(2,1)}), f16[8,56,256]{2,1,0:T(8,128)(2,1)S(1)}, u32[]{:S(2)}, u32[]{:S(2)}) %all-to-all-start.3) | async-done | bytes 229408 | tf_op jit(solution)/shard_map/all_to_all | solution.py:267
  83.8 0.8 shard_map.64
  (6 shorter events, 0.1 us)
Async XLA Ops:
  3.4 12.0 %copy-start.1 = (bf16[16,1024]{1,0:T(8,128)(2,1)S(1)}, bf16[16,1024]{1,0:T(8,128)(2,1)}, u32[]{:S(2)}) copy-start(bf16[16,1024]{1,0:T(8,128)(2,1)} %get-tuple-element.16.own) | copy-start | bytes 98308
  3.4 40.4 %all-to-all-start = ((bf16[16,16,2304]{2,1,0:T(8,128)(2,1)}), bf16[16,16,2304]{2,1,0:T(8,128)(2,1)S(1)}, u32[]{:S(2)}, u32[]{:S(2)}) async-start(bf16[16,16,2304]{2,1,0:T(8,128)(2,1)} %get-tuple-element.10), calls=%async_computation | async-start | bytes 2359296 | tf_op jit(solution)/shard_map/all_to_all | solution.py:236
  15.4 5.9 %collective-permute-start.4 = (bf16[16,1024]{1,0:T(8,128)(2,1)S(1)}, bf16[16,1024]{1,0:T(8,128)(2,1)S(1)}, u32[]{:S(2)}, u32[]{:S(2)}) collective-permute-start(bf16[16,1024]{1,0:T(8,128)(2,1)S(1)} %copy-done.1), channel_id=1, source_target_pairs={{16,0},{32,16},{48,32},{64,48},{80,64},{96,80},{112,96},{128,112},... | collective-permute-start | bytes 98312 | tf_op jit(solution)/shard_map/ppermute | solution.py:238
  18.3 4.0 %collective-permute-start.3 = (bf16[16,1024]{1,0:T(8,128)(2,1)S(1)}, bf16[16,1024]{1,0:T(8,128)(2,1)S(1)}, u32[]{:S(2)}, u32[]{:S(2)}) collective-permute-start(bf16[16,1024]{1,0:T(8,128)(2,1)S(1)} %copy-done.1), channel_id=1, source_target_pairs={{0,16},{16,32},{32,48},{48,64},{64,80},{80,96},{96,112},{112,128},... | collective-permute-start | bytes 98312 | tf_op jit(solution)/shard_map/ppermute | solution.py:237
  43.8 10.3 %copy-start = (bf16[27,16,256]{2,1,0:T(8,128)(2,1)S(1)}, bf16[27,16,256]{2,1,0:T(8,128)(2,1)}, u32[]{:S(2)}) copy-start(bf16[27,16,256]{2,1,0:T(8,128)(2,1)} %filters.1) | copy-start | bytes 663556
  45.1 11.9 %all-to-all-start.1 = ((f16[8,56,256]{2,1,0:T(8,128)(2,1)}), f16[8,56,256]{2,1,0:T(8,128)(2,1)S(1)}, u32[]{:S(2)}, u32[]{:S(2)}) async-start(f16[8,56,256]{2,1,0:T(8,128)(2,1)} %convert_element_type.18), calls=%async_computation.1 | async-start | bytes 458752 | tf_op jit(solution)/shard_map/all_to_all | solution.py:249
  50.8 3.2 %collective-permute-start = (bf16[256,256]{1,0:T(8,128)(2,1)S(1)}, bf16[256,256]{1,0:T(8,128)(2,1)S(1)}, u32[]{:S(2)}, u32[]{:S(2)}) collective-permute-start(bf16[256,256]{1,0:T(8,128)(2,1)S(1)} %slice.4), channel_id=1, source_target_pairs={{0,16},{16,0},{1,17},{17,1},{2,18},{18,2},{3,19},{19,3},{4,20},{20... | collective-permute-start | bytes 393224 | tf_op jit(solution)/shard_map/ppermute | solution.py:240
  57.9 13.2 %all-to-all-start.2 = ((f16[4,56,256]{2,1,0:T(8,128)(2,1)}), f16[4,56,256]{2,1,0:T(8,128)(2,1)S(1)}, u32[]{:S(2)}, u32[]{:S(2)}) async-start(f16[4,56,256]{2,1,0:T(8,128)(2,1)} %broadcast_in_dim.4), calls=%async_computation.2 | async-start | bytes 229376 | tf_op jit(solution)/shard_map/all_to_all | solution.py:267
  63.8 13.8 %collective-permute-start.1 = (f32[32,1024]{1,0:T(8,128)S(1)}, f32[32,1024]{1,0:T(8,128)S(1)}, u32[]{:S(2)}, u32[]{:S(2)}) collective-permute-start(f32[32,1024]{1,0:T(8,128)S(1)} %get-tuple-element.12), channel_id=1, source_target_pairs={{0,16},{16,0},{1,17},{17,1},{2,18},{18,2},{3,19},{19,3},{4,20},{20... | collective-permute-start | bytes 393224 | tf_op jit(solution)/shard_map/ppermute | solution.py:259
  67.0 10.6 %collective-permute-start.2 = (f32[32,1024]{1,0:T(8,128)S(1)}, f32[32,1024]{1,0:T(8,128)S(1)}, u32[]{:S(2)}, u32[]{:S(2)}) collective-permute-start(f32[32,1024]{1,0:T(8,128)S(1)} %get-tuple-element.13), channel_id=1, source_target_pairs={{16,32},{32,16},{48,64},{64,48},{80,96},{96,80},{112,128},{128,112... | collective-permute-start | bytes 393224 | tf_op jit(solution)/shard_map/ppermute | solution.py:258
  71.9 11.9 %all-to-all-start.3 = ((f16[8,56,256]{2,1,0:T(8,128)(2,1)}), f16[8,56,256]{2,1,0:T(8,128)(2,1)S(1)}, u32[]{:S(2)}, u32[]{:S(2)}) async-start(f16[8,56,256]{2,1,0:T(8,128)(2,1)} %broadcast_in_dim.5), calls=%async_computation.3 | async-start | bytes 458752 | tf_op jit(solution)/shard_map/all_to_all | solution.py:267

commit v7 on v6

--- a/solution.py
+++ b/solution.py
@@ -20,11 +20,15 @@
 OWN = 16
 CELLS = 1024
 ROWS = TAPS * OWN
-WIDE = 2 * CELLS + 256
+HALF_CELLS = CELLS // 2
+TAPS_AT = CELLS + HALF_CELLS
+WIDE = TAPS_AT + 256
 PART = ROWS // 8
 SCALE = 1.0 / math.sqrt(32768)
 LIMIT = 16 * 1024 * 1024
 PACK_LIMIT = 63 * 1024 * 1024
+CONTRIBUTIONS_FLOPS = 10**10
+ROW_FLOPS = 10**9
 OUTPUTS_FLOPS = 10**10
 
 
@@ -57,8 +61,9 @@
 
 
 def pack_body(
-    core, field_far, cot_far, filters_far, out, own_cot, field, cotangent, filters, cells, taps, arrived, sent
+    core_at, side_at, field_far, cot_far, filters_far, out, own_cot, field, cotangent, filters, cells, taps, arrived, sent
 ):
+    core, side = core_at[0], side_at[0]
     pairs = ((field_far, field), (cot_far, cotangent), (filters_far, filters))
     copies = [pltpu.make_async_copy(a, b, arrived.at[n]) for n, (a, b) in enumerate(pairs)]
     for copy in copies:
@@ -70,16 +75,19 @@
             at = 128 * (4 * r + z)
             mine = cotangent[:, r, z, :]
             own_cot[:, at : at + 128] = mine
-            cells[:, at : at + 128] = field[:, r, z, :]
-            cells[:, CELLS + at : CELLS + at + 128] = mine
+            cells[0, :, at : at + 128] = field[:, r, z, :]
+            cells[1, :, at : at + 128] = field[:, r, z, :]
+            at = CELLS + 128 * z
+            cells[jnp.where(side == r, 0, 1), :, at : at + 128] = mine
     sends = [
-        pltpu.make_async_copy(cells, out.at[c, :, pl.ds(0, 2 * CELLS)], sent.at[c]) for c in range(16)
+        pltpu.make_async_copy(cells.at[c // 8], out.at[c, :, pl.ds(0, TAPS_AT)], sent.at[c])
+        for c in range(16)
     ]
     for send in sends:
         send.start()
     copies[2].wait()
     lane = lanes((OWN, 128))
-    low = core[0] * 11
+    low = core * 11
     for g in range(2):
         parts = [jnp.zeros((OWN, 128), F32) for _ in range(16)]
         for j in range(8):
@@ -93,7 +101,7 @@
                     parts[8 * h + q] = jnp.where(here, turned, parts[8 * h + q])
         for c in range(16):
             taps[c, :, 128 * g : 128 * g + 128] = parts[c].astype(BF)
-    last = pltpu.make_async_copy(taps, out.at[:, :, pl.ds(2 * CELLS, 256)], sent.at[16])
+    last = pltpu.make_async_copy(taps, out.at[:, :, pl.ds(TAPS_AT, 256)], sent.at[16])
     last.start()
     for send in sends:
         send.wait()
@@ -151,13 +159,19 @@
         out[n, PART : PART + 2, :] = jnp.broadcast_to(power, (2, 256))
 
 
+def parts_body(gathered, _after, cells, taps):
+    cells[...] = gathered[:, CELLS:TAPS_AT]
+    taps[...] = gathered[:, TAPS_AT:WIDE]
+
+
 def scaled_down(values):
     most = jnp.full((1, 256), jnp.max(jnp.abs(values)), F32)
     power = jnp.ceil(jnp.log2(jnp.maximum(most, 2.0**-100)))
     return power, values * jnp.exp2(14.0 - power)
 
 
-def sum_body(factor, peers, parts, _after, out):
+def sum_body(factor, peers, parts, *rest):
+    out = rest[-1]
     total = jnp.zeros((PART, 256), F32)
     for n in range(peers):
         total = total + parts[n, 0:PART, :] * jnp.exp2(parts[n, PART : PART + 1, :] - 14.0)
@@ -180,26 +194,30 @@
                 out[:, r, z, :] = (own[here] + near[here] + far[here]).astype(BF)
 
 
-def contributions_body(core, gathered, filters, swapped, near, far, mid, products):
-    first = core[0] == 0
+def contributions_body(core, side_at, gathered, filters, swapped, halves, near, far, mid, products):
+    first, side = core[0] == 0, side_at[0]
     products[...] = jnp.dot(
         filters[...].reshape(ROWS, 256), gathered[:, 0:CELLS], preferred_element_type=F32
     )
-    place(products, 1, first, 0, near, far, mid)
-    mine = gathered[:, 2 * CELLS : WIDE]
+    put(products, 1, first, 0, near, far, mid)
+    mine = gathered[:, TAPS_AT:WIDE]
     other = swapped[...]
-    cells = gathered[:, CELLS : 2 * CELLS]
+    low, high = jnp.where(first, mine, other), jnp.where(first, other, mine)
     over = (((0,), (0,)), ((), ()))
-    products[0:256, :] = lax.dot_general(
-        jnp.where(first, mine, other), cells, over, preferred_element_type=F32
-    )
-    products[176:ROWS, :] = lax.dot_general(
-        jnp.where(first, other, mine), cells, over, preferred_element_type=F32
-    )
-    place(products, -1, first, OWN, near, far, mid)
-
-
-def place(products, sign, first, at, near, far, mid):
+    for r in range(2):
+        rows = []
+        for line in range(2):
+            here = slice(128 * line, 128 * line + 128)
+            kept = (side == line) if r == 0 else (side != line)
+            rows.append(jnp.where(kept, gathered[here, CELLS:TAPS_AT], halves[here, :]))
+        cells = jnp.concatenate(rows, axis=0)
+        at = slice(HALF_CELLS * r, HALF_CELLS * r + HALF_CELLS)
+        products[0:256, at] = lax.dot_general(low, cells, over, preferred_element_type=F32)
+        products[176:ROWS, at] = lax.dot_general(high, cells, over, preferred_element_type=F32)
+    put(products, -1, first, OWN, near, far, mid)
+
+
+def put(products, sign, first, at, near, far, mid):
     following, last = taps_sum(products, 1 - sign, sign), taps_sum(products, 1 + sign, sign)
     for n, block in enumerate(taps_sum(products, 1, sign)):
         here = (slice(at, at + OWN), slice(128 * n, 128 * n + 128))
@@ -210,7 +228,8 @@
 
 def per_device(field, filters, cotangent):
     space = ("far", "near", "core")
-    core = lax.axis_index("core").astype(jnp.int32).reshape(1)
+    chan = ("side", "line")
+    core, side = (lax.axis_index(name).astype(jnp.int32).reshape(1) for name in ("core", "side"))
     up = [(i, i + 1) for i in range(31)]
     down = [(i + 1, i) for i in range(31)]
     swap = [(0, 1), (1, 0)]
@@ -219,12 +238,12 @@
     packed, own_cot = call(
         pack_body,
         [shape((16, OWN, WIDE), BF), shape((OWN, CELLS), BF)],
-        [SMEM] + [FAR] * 3,
+        [SMEM] * 2 + [FAR] * 3,
         [
             pltpu.VMEM((OWN, 2, 4, 128), BF),
             pltpu.VMEM((OWN, 2, 4, 128), BF),
             pltpu.VMEM((TAPS, OWN, 256), BF),
-            pltpu.VMEM((OWN, 2 * CELLS), BF),
+            pltpu.VMEM((2, OWN, TAPS_AT), BF),
             pltpu.VMEM((16, OWN, 256), BF),
             pltpu.SemaphoreType.DMA((3,)),
             pltpu.SemaphoreType.DMA((17,)),
@@ -232,12 +251,11 @@
         moved=1 << 20,
         limit=PACK_LIMIT,
         outs_at=[FAR, VMEM],
-    )(core, field, cotangent, filters)
-    gathered = lax.all_to_all(packed, "chan", 0, 0).reshape(256, WIDE)
+    )(core, side, field, cotangent, filters)
+    gathered = lax.all_to_all(packed, chan, 0, 0).reshape(256, WIDE)
     below = lax.ppermute(own_cot, space, up)
     above = lax.ppermute(own_cot, space, down)
 
-    swapped = lax.ppermute(gathered[:, 2 * CELLS :], "core", swap)
     own_grad = call(
         grad_body,
         [shape((8, PART + 2, 256), F32)],
@@ -246,28 +264,35 @@
         flops=2 * ROWS * CELLS * 256,
         moved=1 << 20,
     )(gathered, below, own_cot, above)[0]
+    half_cells, half_taps = call(
+        parts_body, [shape((256, HALF_CELLS), BF), shape((256, 256), BF)], [VMEM, ANY], moved=1 << 19
+    )(gathered, own_grad)
+    halves = lax.ppermute(half_cells, "side", swap)
+    swapped = lax.ppermute(half_taps, "core", swap)
     parts = lax.all_to_all(own_grad.astype(HALF), ("near", "core"), 0, 0).astype(F32)
     to_near, to_far, own_sums = call(
         contributions_body,
         [shape((2 * OWN, CELLS), F32)] * 3,
-        [SMEM] + [VMEM] * 3,
+        [SMEM] * 2 + [VMEM] * 4,
         [pltpu.VMEM((ROWS, CELLS), F32)],
-        flops=4 * ROWS * CELLS * 256,
+        flops=CONTRIBUTIONS_FLOPS,
         moved=1 << 20,
-    )(core, gathered, filters, swapped)
+    )(core, side, gathered, filters, swapped, halves)
     from_far = lax.ppermute(to_far, space, across)
     from_near = lax.ppermute(to_near, "core", swap)
 
-    def summed(factor, peers, parts):
+    def summed(factor, peers, flops, parts, *after):
         body = functools.partial(sum_body, factor, peers)
-        return call(body, [shape((PART + 2, 256), F32)], [VMEM, ANY], moved=1 << 19)(parts, own_sums)[0]
+        return call(body, [shape((PART + 2, 256), F32)], [VMEM] + [ANY] * len(after), flops=flops)(
+            parts, *after
+        )[0]
 
     def spread(part, peers, axes):
         many = jnp.broadcast_to(part.astype(HALF)[None], (peers,) + part.shape)
         return lax.all_to_all(many, axes, 0, 0).astype(F32)
 
-    row = summed(1.0, 8, parts)
-    mine = summed(SCALE, 4, spread(row, 4, "far"))
+    row = summed(1.0, 8, ROW_FLOPS, parts)
+    mine = summed(SCALE, 4, 0, spread(row, 4, "far"), own_sums)
     full = spread(mine, 8, ("near", "core"))
     weight_grad = call(finish_body, [shape((ROWS, 256), F32)], [VMEM], moved=1 << 20)(full)[0]
     out_field, input_grad = call(
@@ -277,9 +302,9 @@
 
 
 def solution(mesh):
-    fine = Mesh(mesh.devices.reshape(4, 4, 2, 16), ("far", "near", "core", "chan"))
-    cells = P("chan", ("far", "near", "core"), None, None)
-    taps = P(None, "chan", None)
+    fine = Mesh(mesh.devices.reshape(4, 4, 2, 2, 8), ("far", "near", "core", "side", "line"))
+    cells = P(("side", "line"), ("far", "near", "core"), None, None)
+    taps = P(None, ("side", "line"), None)
     return jax.shard_map(
         per_device,
         mesh=fine,

time: 86.2 us -> 81 us (0.940); the launches traced: 84.7 us -> 80.3 us
  waiting for transfers between devices: 33.3 us -> 24 us
  starting transfers between devices: 42.3 us -> 47.3 us
    all_to_all x1, waiting for transfers between devices: 21.5 us -> 15.3 us  [per_device(): gathered = lax.all_to_all(packed, chan, 0, 0).reshape(256, WIDE)]
    ppermute x1 -> x2, starting transfers between devices: 1.92 us -> 5.03 us  [the longest x1 2.84 us: per_device(): halves = lax.ppermute(half_cells, 'side', swap)]
    ppermute x1 -> x2, waiting for transfers between devices: 1.31 us -> 0.01 us  [the longest x1 0.01 us: per_device(): swapped = lax.ppermute(half_taps, 'core', swap)]
    all_to_all x1, starting transfers between devices: 5.66 us -> 6.9 us  [per_device(): lax.all_to_all(own_grad.astype(HALF), ('near', 'core'), 0, 0).astype(F32)]
    all_to_all x1, waiting for transfers between devices: 2.2 us -> 1.12 us  [per_device(): lax.all_to_all(own_grad.astype(HALF), ('near', 'core'), 0, 0).astype(F32)]
  transfers between devices with their start and end apart: 9 -> 10, of which waited for: 6 -> 5; matrix products, arithmetic and copies ran while one was open for 1% -> 2% of each run, Pallas kernels for 2% -> 2%
where the time goes in v7:
time: 81 us; the launch traced here: 80.3 us
  starting transfers between devices  47.3 us (58%)
  waiting for transfers between devices  24 us (30%)
  Pallas kernels  6.1 us (8%)
  local copies, waits for them, and re-layouts  1.38 us (2%)
  other arithmetic  0.81 us (1%)
  between operations  0.81 us (1%)
    all_to_all x1, waiting for transfers between devices, per_device(): gathered = lax.all_to_all(packed, chan, 0, 0).reshape(256, WIDE)  15.3 us
    all_to_all x2, starting transfers between devices, spread(): return lax.all_to_all(many, axes, 0, 0).astype(F32)  12.2 us
    all_to_all x1, starting transfers between devices, per_device(): gathered = lax.all_to_all(packed, chan, 0, 0).reshape(256, WIDE)  12 us
    all_to_all x1, starting transfers between devices, per_device(): lax.all_to_all(own_grad.astype(HALF), ('near', 'core'), 0, 0).astype(F32)  6.9 us
    all_to_all x2, waiting for transfers between devices, spread(): return lax.all_to_all(many, axes, 0, 0).astype(F32)  6.53 us
    ppermute x1, starting transfers between devices, per_device(): from_near = lax.ppermute(to_near, 'core', swap)  3.19 us
    ppermute x1, starting transfers between devices, per_device(): below = lax.ppermute(own_cot, space, up)  3.02 us
    ppermute x1, starting transfers between devices, per_device(): above = lax.ppermute(own_cot, space, down)  2.86 us
  transfers between devices with their start and end apart: 10, of which 5 were waited for; matrix products, arithmetic and copies ran while one was open for 2% of the time, Pallas kernels for 2%

profile of v7, /device:TPU:1, one launch (start us, length us, event | category | flops | bytes accessed | tf_op | source)
XLA Modules:
  0.0 80.3 jit_solution(10144404598572065544)
XLA Ops:
  0.6 2.8 %shard_map.58 = (bf16[16,16,1792]{2,1,0:T(8,128)(2,1)}, bf16[16,1024]{1,0:T(8,128)(2,1)}) custom-call(s32[1]{0:T(128)} %bitcast.core_at.core, s32[1]{0:T(128)} %bitcast.1.side_at, bf16[16,2,4,128]{3,2,1,0:T(4,128)(2,1)} %field_far.1, bf16[16,2,4,128]{3,2,1,0:T(4,128)(2,1)} %cot_far.1, bf16[27,16,256]{2,1,0:T(8,128)(2,1)} %filters.1), custom_call_target="tpu_custom_call" | custom-call | bytes 1048576 | tf_op jit(solution)/shard_map/pallas_call | solution.py:238
  3.4 0.0 copy-start.1
  3.4 12.0 %all-to-all-start = ((bf16[16,16,1792]{2,1,0:T(8,128)(2,1)}), bf16[16,16,1792]{2,1,0:T(8,128)(2,1)S(1)}, u32[]{:S(2)}, u32[]{:S(2)}) async-start(bf16[16,16,1792]{2,1,0:T(8,128)(2,1)} %get-tuple-element.12), calls=%async_computation | async-start | bytes 1835008 | tf_op jit(solution)/shard_map/all_to_all | solution.py:255
  15.4 0.0 copy-done.1
  15.4 2.9 %collective-permute-start.1 = (bf16[16,1024]{1,0:T(8,128)(2,1)S(1)}, bf16[16,1024]{1,0:T(8,128)(2,1)S(1)}, u32[]{:S(2)}, u32[]{:S(2)}) collective-permute-start(bf16[16,1024]{1,0:T(8,128)(2,1)S(1)} %copy-done.1), channel_id=1, source_target_pairs={{16,0},{32,16},{48,32},{64,48},{80,64},{96,80},{112,96},{128,112},... | collective-permute-start | bytes 98312 | tf_op jit(solution)/shard_map/ppermute | solution.py:257
  18.3 3.0 %collective-permute-start = (bf16[16,1024]{1,0:T(8,128)(2,1)S(1)}, bf16[16,1024]{1,0:T(8,128)(2,1)S(1)}, u32[]{:S(2)}, u32[]{:S(2)}) collective-permute-start(bf16[16,1024]{1,0:T(8,128)(2,1)S(1)} %copy-done.1), channel_id=1, source_target_pairs={{0,16},{16,32},{32,48},{48,64},{64,80},{80,96},{96,112},{112,128},... | collective-permute-start | bytes 98312 | tf_op jit(solution)/shard_map/ppermute | solution.py:256
  21.3 0.0 collective-permute-done.1.above
  21.3 1.0 %collective-permute-done.below = bf16[16,1024]{1,0:T(8,128)(2,1)S(1)} collective-permute-done((bf16[16,1024]{1,0:T(8,128)(2,1)S(1)}, bf16[16,1024]{1,0:T(8,128)(2,1)S(1)}, u32[]{:S(2)}, u32[]{:S(2)}) %collective-permute-start) | collective-permute-done | bytes 32800 | tf_op jit(solution)/shard_map/ppermute | solution.py:256
  22.3 15.3 %all-to-all-done = bf16[16,16,1792]{2,1,0:T(8,128)(2,1)S(1)} async-done(((bf16[16,16,1792]{2,1,0:T(8,128)(2,1)}), bf16[16,16,1792]{2,1,0:T(8,128)(2,1)S(1)}, u32[]{:S(2)}, u32[]{:S(2)}) %all-to-all-start) | async-done | bytes 917536 | tf_op jit(solution)/shard_map/all_to_all | solution.py:255
  37.7 0.6 shard_map.59._after
  38.3 0.7 convert_element_type.18
  39.0 6.9 %all-to-all-start.1 = ((f16[8,56,256]{2,1,0:T(8,128)(2,1)}), f16[8,56,256]{2,1,0:T(8,128)(2,1)S(1)}, u32[]{:S(2)}, u32[]{:S(2)}) async-start(f16[8,56,256]{2,1,0:T(8,128)(2,1)} %convert_element_type.18), calls=%async_computation.1 | async-start | bytes 458752 | tf_op jit(solution)/shard_map/all_to_all | solution.py:272
  45.9 2.8 %collective-permute-start.3 = (bf16[256,512]{1,0:T(8,128)(2,1)S(1)}, bf16[256,512]{1,0:T(8,128)(2,1)S(1)}, u32[]{:S(2)}, u32[]{:S(2)}) collective-permute-start(bf16[256,512]{1,0:T(8,128)(2,1)S(1)} %get-tuple-element.15), channel_id=1, source_target_pairs={{0,8},{8,0},{1,9},{9,1},{2,10},{10,2},{3,11},{11,3},{4,12},{12,4},... | collective-permute-start | bytes 786440 | tf_op jit(solution)/shard_map/ppermute | solution.py:270
  48.8 2.2 %collective-permute-start.2 = (bf16[256,256]{1,0:T(8,128)(2,1)S(1)}, bf16[256,256]{1,0:T(8,128)(2,1)S(1)}, u32[]{:S(2)}, u32[]{:S(2)}) collective-permute-start(bf16[256,256]{1,0:T(8,128)(2,1)S(1)} %get-tuple-element.14), channel_id=1, source_target_pairs={{0,16},{16,0},{1,17},{17,1},{2,18},{18,2},{3,19},{19,3},{4,20},{20... | collective-permute-start | bytes 393224 | tf_op jit(solution)/shard_map/ppermute | solution.py:271
  51.0 1.1 %all-to-all-done.1 = f16[8,56,256]{2,1,0:T(8,128)(2,1)S(1)} async-done(((f16[8,56,256]{2,1,0:T(8,128)(2,1)}), f16[8,56,256]{2,1,0:T(8,128)(2,1)S(1)}, u32[]{:S(2)}, u32[]{:S(2)}) %all-to-all-start.1) | async-done | bytes 229408 | tf_op jit(solution)/shard_map/all_to_all | solution.py:272
  52.1 0.2 shard_map.63
  52.3 0.0 copy-start
  52.3 0.7 broadcast_in_dim.4
  53.0 5.9 %all-to-all-start.2 = ((f16[4,56,256]{2,1,0:T(8,128)(2,1)}), f16[4,56,256]{2,1,0:T(8,128)(2,1)S(1)}, u32[]{:S(2)}, u32[]{:S(2)}) async-start(f16[4,56,256]{2,1,0:T(8,128)(2,1)} %broadcast_in_dim.4), calls=%async_computation.2 | async-start | bytes 229376 | tf_op jit(solution)/shard_map/all_to_all | solution.py:292
  58.9 0.0 collective-permute-done.2.swapped
  58.9 0.0 collective-permute-done.3.halves
  58.9 0.0 copy-done
  58.9 0.7 shard_map.61
  59.7 3.2 %collective-permute-start.4 = (f32[32,1024]{1,0:T(8,128)S(1)}, f32[32,1024]{1,0:T(8,128)S(1)}, u32[]{:S(2)}, u32[]{:S(2)}) collective-permute-start(f32[32,1024]{1,0:T(8,128)S(1)} %get-tuple-element.17), channel_id=1, source_target_pairs={{0,16},{16,0},{1,17},{17,1},{2,18},{18,2},{3,19},{19,3},{4,20},{20... | collective-permute-start | bytes 393224 | tf_op jit(solution)/shard_map/ppermute | solution.py:282
  62.9 2.1 %collective-permute-start.5 = (f32[32,1024]{1,0:T(8,128)S(1)}, f32[32,1024]{1,0:T(8,128)S(1)}, u32[]{:S(2)}, u32[]{:S(2)}) collective-permute-start(f32[32,1024]{1,0:T(8,128)S(1)} %get-tuple-element.18), channel_id=1, source_target_pairs={{16,32},{32,16},{48,64},{64,48},{80,96},{96,80},{112,128},{128,112... | collective-permute-start | bytes 393224 | tf_op jit(solution)/shard_map/ppermute | solution.py:281
  65.0 1.1 %all-to-all-done.2 = f16[4,56,256]{2,1,0:T(8,128)(2,1)S(1)} async-done(((f16[4,56,256]{2,1,0:T(8,128)(2,1)}), f16[4,56,256]{2,1,0:T(8,128)(2,1)S(1)}, u32[]{:S(2)}, u32[]{:S(2)}) %all-to-all-start.2) | async-done | bytes 114720 | tf_op jit(solution)/shard_map/all_to_all | solution.py:292
  66.1 0.2 shard_map.64
  66.3 0.7 broadcast_in_dim.5
  67.0 6.2 %all-to-all-start.3 = ((f16[8,56,256]{2,1,0:T(8,128)(2,1)}), f16[8,56,256]{2,1,0:T(8,128)(2,1)S(1)}, u32[]{:S(2)}, u32[]{:S(2)}) async-start(f16[8,56,256]{2,1,0:T(8,128)(2,1)} %broadcast_in_dim.5), calls=%async_computation.3 | async-start | bytes 458752 | tf_op jit(solution)/shard_map/all_to_all | solution.py:292
  73.3 0.0 collective-permute-done.4.near
  73.3 0.0 collective-permute-done.5.far
  73.3 0.8 %shard_map.62 = (bf16[16,2,4,128]{3,2,1,0:T(4,128)(2,1)}, bf16[16,2,4,128]{3,2,1,0:T(4,128)(2,1)}) custom-call(f32[32,1024]{1,0:T(8,128)S(1)} %get-tuple-element.16.own.rest_0_, f32[32,1024]{1,0:T(8,128)S(1)} %collective-permute-done.4.near, f32[32,1024]{1,0:T(8,128)S(1)} %collective-permute-done.5.far), custom_call_target="tpu_custom_call" | custom-call | flops 10000000000 | bytes 262144 | tf_op jit(solution)/shard_map/pallas_call | solution.py:298
  74.1 5.4 %all-to-all-done.3 = f16[8,56,256]{2,1,0:T(8,128)(2,1)S(1)} async-done(((f16[8,56,256]{2,1,0:T(8,128)(2,1)}), f16[8,56,256]{2,1,0:T(8,128)(2,1)S(1)}, u32[]{:S(2)}, u32[]{:S(2)}) %all-to-all-start.3) | async-done | bytes 229408 | tf_op jit(solution)/shard_map/all_to_all | solution.py:292
  79.5 0.8 %shard_map.65 = f32[432,256]{1,0:T(8,128)} custom-call(f32[8,56,256]{2,1,0:T(8,128)S(1)} %convert_element_type.23.full), custom_call_target="tpu_custom_call" | custom-call | bytes 1048576 | tf_op jit(solution)/shard_map/pallas_call | solution.py:297
  (6 shorter events, 0.1 us)
Async XLA Ops:
  3.4 12.0 %copy-start.1 = (bf16[16,1024]{1,0:T(8,128)(2,1)S(1)}, bf16[16,1024]{1,0:T(8,128)(2,1)}, u32[]{:S(2)}) copy-start(bf16[16,1024]{1,0:T(8,128)(2,1)} %get-tuple-element.13.own) | copy-start | bytes 98308
  3.4 34.2 %all-to-all-start = ((bf16[16,16,1792]{2,1,0:T(8,128)(2,1)}), bf16[16,16,1792]{2,1,0:T(8,128)(2,1)S(1)}, u32[]{:S(2)}, u32[]{:S(2)}) async-start(bf16[16,16,1792]{2,1,0:T(8,128)(2,1)} %get-tuple-element.12), calls=%async_computation | async-start | bytes 1835008 | tf_op jit(solution)/shard_map/all_to_all | solution.py:255
  15.4 5.9 %collective-permute-start.1 = (bf16[16,1024]{1,0:T(8,128)(2,1)S(1)}, bf16[16,1024]{1,0:T(8,128)(2,1)S(1)}, u32[]{:S(2)}, u32[]{:S(2)}) collective-permute-start(bf16[16,1024]{1,0:T(8,128)(2,1)S(1)} %copy-done.1), channel_id=1, source_target_pairs={{16,0},{32,16},{48,32},{64,48},{80,64},{96,80},{112,96},{128,112},... | collective-permute-start | bytes 98312 | tf_op jit(solution)/shard_map/ppermute | solution.py:257
  18.3 4.0 %collective-permute-start = (bf16[16,1024]{1,0:T(8,128)(2,1)S(1)}, bf16[16,1024]{1,0:T(8,128)(2,1)S(1)}, u32[]{:S(2)}, u32[]{:S(2)}) collective-permute-start(bf16[16,1024]{1,0:T(8,128)(2,1)S(1)} %copy-done.1), channel_id=1, source_target_pairs={{0,16},{16,32},{32,48},{48,64},{64,80},{80,96},{96,112},{112,128},... | collective-permute-start | bytes 98312 | tf_op jit(solution)/shard_map/ppermute | solution.py:256
  39.0 13.1 %all-to-all-start.1 = ((f16[8,56,256]{2,1,0:T(8,128)(2,1)}), f16[8,56,256]{2,1,0:T(8,128)(2,1)S(1)}, u32[]{:S(2)}, u32[]{:S(2)}) async-start(f16[8,56,256]{2,1,0:T(8,128)(2,1)} %convert_element_type.18), calls=%async_computation.1 | async-start | bytes 458752 | tf_op jit(solution)/shard_map/all_to_all | solution.py:272
  45.9 13.0 %collective-permute-start.3 = (bf16[256,512]{1,0:T(8,128)(2,1)S(1)}, bf16[256,512]{1,0:T(8,128)(2,1)S(1)}, u32[]{:S(2)}, u32[]{:S(2)}) collective-permute-start(bf16[256,512]{1,0:T(8,128)(2,1)S(1)} %get-tuple-element.15), channel_id=1, source_target_pairs={{0,8},{8,0},{1,9},{9,1},{2,10},{10,2},{3,11},{11,3},{4,12},{12,4},... | collective-permute-start | bytes 786440 | tf_op jit(solution)/shard_map/ppermute | solution.py:270
  48.8 10.1 %collective-permute-start.2 = (bf16[256,256]{1,0:T(8,128)(2,1)S(1)}, bf16[256,256]{1,0:T(8,128)(2,1)S(1)}, u32[]{:S(2)}, u32[]{:S(2)}) collective-permute-start(bf16[256,256]{1,0:T(8,128)(2,1)S(1)} %get-tuple-element.14), channel_id=1, source_target_pairs={{0,16},{16,0},{1,17},{17,1},{2,18},{18,2},{3,19},{19,3},{4,20},{20... | collective-permute-start | bytes 393224 | tf_op jit(solution)/shard_map/ppermute | solution.py:271
  52.3 6.6 %copy-start = (bf16[27,16,256]{2,1,0:T(8,128)(2,1)S(1)}, bf16[27,16,256]{2,1,0:T(8,128)(2,1)}, u32[]{:S(2)}) copy-start(bf16[27,16,256]{2,1,0:T(8,128)(2,1)} %filters.1) | copy-start | bytes 663556
  53.0 13.1 %all-to-all-start.2 = ((f16[4,56,256]{2,1,0:T(8,128)(2,1)}), f16[4,56,256]{2,1,0:T(8,128)(2,1)S(1)}, u32[]{:S(2)}, u32[]{:S(2)}) async-start(f16[4,56,256]{2,1,0:T(8,128)(2,1)} %broadcast_in_dim.4), calls=%async_computation.2 | async-start | bytes 229376 | tf_op jit(solution)/shard_map/all_to_all | solution.py:292
  59.7 13.6 %collective-permute-start.4 = (f32[32,1024]{1,0:T(8,128)S(1)}, f32[32,1024]{1,0:T(8,128)S(1)}, u32[]{:S(2)}, u32[]{:S(2)}) collective-permute-start(f32[32,1024]{1,0:T(8,128)S(1)} %get-tuple-element.17), channel_id=1, source_target_pairs={{0,16},{16,0},{1,17},{17,1},{2,18},{18,2},{3,19},{19,3},{4,20},{20... | collective-permute-start | bytes 393224 | tf_op jit(solution)/shard_map/ppermute | solution.py:282
  62.9 10.4 %collective-permute-start.5 = (f32[32,1024]{1,0:T(8,128)S(1)}, f32[32,1024]{1,0:T(8,128)S(1)}, u32[]{:S(2)}, u32[]{:S(2)}) collective-permute-start(f32[32,1024]{1,0:T(8,128)S(1)} %get-tuple-element.18), channel_id=1, source_target_pairs={{16,32},{32,16},{48,64},{64,48},{80,96},{96,80},{112,128},{128,112... | collective-permute-start | bytes 393224 | tf_op jit(solution)/shard_map/ppermute | solution.py:281
  67.0 12.5 %all-to-all-start.3 = ((f16[8,56,256]{2,1,0:T(8,128)(2,1)}), f16[8,56,256]{2,1,0:T(8,128)(2,1)S(1)}, u32[]{:S(2)}, u32[]{:S(2)}) async-start(f16[8,56,256]{2,1,0:T(8,128)(2,1)} %broadcast_in_dim.5), calls=%async_computation.3 | async-start | bytes 458752 | tf_op jit(solution)/shard_map/all_to_all | solution.py:292

commit v8 on v7

--- a/solution.py
+++ b/solution.py
@@ -29,7 +29,7 @@
 PACK_LIMIT = 63 * 1024 * 1024
 CONTRIBUTIONS_FLOPS = 10**10
 ROW_FLOPS = 10**9
-OUTPUTS_FLOPS = 10**10
+FAR_FLOPS = 15 * 10**8
 
 
 def call(body, outs, ins, scratch=(), flops=0, moved=0, limit=LIMIT, outs_at=None):
@@ -64,7 +64,8 @@
     core_at, side_at, field_far, cot_far, filters_far, out, own_cot, field, cotangent, filters, cells, taps, arrived, sent
 ):
     core, side = core_at[0], side_at[0]
-    pairs = ((field_far, field), (cot_far, cotangent), (filters_far, filters))
+    own_taps = filters_far.at[pl.ds(11 * core, 16)]
+    pairs = ((field_far, field), (cot_far, cotangent), (own_taps, filters))
     copies = [pltpu.make_async_copy(a, b, arrived.at[n]) for n, (a, b) in enumerate(pairs)]
     for copy in copies:
         copy.start()
@@ -87,12 +88,11 @@
         send.start()
     copies[2].wait()
     lane = lanes((OWN, 128))
-    low = core * 11
     for g in range(2):
         parts = [jnp.zeros((OWN, 128), F32) for _ in range(16)]
         for j in range(8):
             here = (lane >= 16 * j) & (lane < 16 * j + 16)
-            tap = filters[pl.ds(low + 8 * g + j, 1)][0].astype(F32)
+            tap = filters[8 * g + j].astype(F32)
             for h in range(2):
                 block = tap[:, 128 * h : 128 * h + 128]
                 for q in range(8):
@@ -180,18 +180,30 @@
     out[PART : PART + 2, :] = jnp.broadcast_to(power, (2, 256))
 
 
-def finish_body(full, out):
-    for n in range(8):
-        scale = jnp.exp2(full[n, PART : PART + 1, :] - 14.0)
-        out[PART * n : PART * n + PART, :] = full[n, 0:PART, :] * scale
-
-
-def outputs_body(own, near, far, out_field, input_grad):
+def finish_body(full, out_far, out, sent):
+    half = ROWS // 2
+    copies = []
+    for h in range(2):
+        for n in range(4 * h, 4 * h + 4):
+            scale = jnp.exp2(full[n, PART : PART + 1, :] - 14.0)
+            out[PART * n : PART * n + PART, :] = full[n, 0:PART, :] * scale
+        here = pl.ds(half * h, half)
+        copies.append(pltpu.make_async_copy(out.at[here], out_far.at[here], sent.at[h]))
+        copies[h].start()
+    for copy in copies:
+        copy.wait()
+
+
+def far_body(own, far, out):
+    out[...] = own[...] + far[...]
+
+
+def outputs_body(own, near, out_field, input_grad):
     for out, at in ((out_field, 0), (input_grad, OWN)):
         for r in range(2):
             for z in range(4):
                 here = (slice(at, at + OWN), slice(128 * (4 * r + z), 128 * (4 * r + z) + 128))
-                out[:, r, z, :] = (own[here] + near[here] + far[here]).astype(BF)
+                out[:, r, z, :] = (own[here] + near[here]).astype(BF)
 
 
 def contributions_body(core, side_at, gathered, filters, swapped, halves, near, far, mid, products):
@@ -242,7 +254,7 @@
         [
             pltpu.VMEM((OWN, 2, 4, 128), BF),
             pltpu.VMEM((OWN, 2, 4, 128), BF),
-            pltpu.VMEM((TAPS, OWN, 256), BF),
+            pltpu.VMEM((16, OWN, 256), BF),
             pltpu.VMEM((2, OWN, TAPS_AT), BF),
             pltpu.VMEM((16, OWN, 256), BF),
             pltpu.SemaphoreType.DMA((3,)),
@@ -279,7 +291,6 @@
         moved=1 << 20,
     )(core, side, gathered, filters, swapped, halves)
     from_far = lax.ppermute(to_far, space, across)
-    from_near = lax.ppermute(to_near, "core", swap)
 
     def summed(factor, peers, flops, parts, *after):
         body = functools.partial(sum_body, factor, peers)
@@ -293,11 +304,22 @@
 
     row = summed(1.0, 8, ROW_FLOPS, parts)
     mine = summed(SCALE, 4, 0, spread(row, 4, "far"), own_sums)
+    from_near = lax.ppermute(to_near, "core", swap)
     full = spread(mine, 8, ("near", "core"))
-    weight_grad = call(finish_body, [shape((ROWS, 256), F32)], [VMEM], moved=1 << 20)(full)[0]
-    out_field, input_grad = call(
-        outputs_body, [shape(field.shape, BF)] * 2, [VMEM] * 3, flops=OUTPUTS_FLOPS, moved=1 << 18
-    )(own_sums, from_near, from_far)
+    weight_grad = call(
+        finish_body,
+        [shape((ROWS, 256), F32)],
+        [VMEM],
+        [pltpu.VMEM((ROWS, 256), F32), pltpu.SemaphoreType.DMA((2,))],
+        moved=1 << 20,
+        outs_at=[FAR],
+    )(full)[0]
+    own_and_far = call(far_body, [shape((2 * OWN, CELLS), F32)], [VMEM] * 2, flops=FAR_FLOPS)(
+        own_sums, from_far
+    )[0]
+    out_field, input_grad = call(outputs_body, [shape(field.shape, BF)] * 2, [VMEM] * 2, moved=1 << 18)(
+        own_and_far, from_near
+    )
     return out_field, input_grad, weight_grad.reshape(TAPS, OWN, 256)
 
 

time: 81 us -> 81 us (level)
    all_to_all x2, waiting for transfers between devices: 6.53 us -> 5.24 us  [spread(): return lax.all_to_all(many, axes, 0, 0).astype(F32)]
    ppermute x1, starting transfers between devices: 2.09 us -> 3.36 us  [per_device(): from_far = lax.ppermute(to_far, space, across)]
    ppermute x1, starting transfers between devices: 3.19 us -> 2.01 us  [per_device(): from_near = lax.ppermute(to_near, 'core', swap)]
    ppermute x1, waiting for transfers between devices: 0.01 us -> 1.17 us  [per_device(): from_near = lax.ppermute(to_near, 'core', swap)]
    pallas_call x2 -> x3, Pallas kernels: 1.63 us -> 1.64 us  [the longest x1 0.81 us: per_device(): call(outputs_body, [shape(field.shape, BF)] * 2, [VMEM] * 2, moved=1 << 18)]
  transfers between devices with their start and end apart: 10 -> 10, of which waited for: 5 -> 6; matrix products, arithmetic and copies ran while one was open for 2% -> 2% of each run, Pallas kernels for 2% -> 2%
where the time goes in v8:
time: 81 us; the launch traced here: 80.3 us
  starting transfers between devices  47.3 us (58%)
  waiting for transfers between devices  23.9 us (30%)
  Pallas kernels  6.07 us (7%)
  local copies, waits for them, and re-layouts  1.38 us (2%)
  between operations  0.82 us (1%)
  other arithmetic  0.81 us (1%)
    all_to_all x1, waiting for transfers between devices, per_device(): gathered = lax.all_to_all(packed, chan, 0, 0).reshape(256, WIDE)  15.3 us
    all_to_all x2, starting transfers between devices, spread(): return lax.all_to_all(many, axes, 0, 0).astype(F32)  12.2 us
    all_to_all x1, starting transfers between devices, per_device(): gathered = lax.all_to_all(packed, chan, 0, 0).reshape(256, WIDE)  12 us
    all_to_all x1, starting transfers between devices, per_device(): lax.all_to_all(own_grad.astype(HALF), ('near', 'core'), 0, 0).astype(F32)  6.92 us
    all_to_all x2, waiting for transfers between devices, spread(): return lax.all_to_all(many, axes, 0, 0).astype(F32)  5.24 us
    ppermute x1, starting transfers between devices, per_device(): from_far = lax.ppermute(to_far, space, across)  3.36 us
    ppermute x1, starting transfers between devices, per_device(): below = lax.ppermute(own_cot, space, up)  3.02 us
    ppermute x1, starting transfers between devices, per_device(): above = lax.ppermute(own_cot, space, down)  2.86 us
  transfers between devices with their start and end apart: 10, of which 6 were waited for; matrix products, arithmetic and copies ran while one was open for 2% of the time, Pallas kernels for 2%

profile of v8, /device:TPU:1, one launch (start us, length us, event | category | flops | bytes accessed | tf_op | source)
XLA Modules:
  0.0 80.3 jit_solution(5553590673984770485)
XLA Ops:
  0.6 2.7 %shard_map.58 = (bf16[16,16,1792]{2,1,0:T(8,128)(2,1)}, bf16[16,1024]{1,0:T(8,128)(2,1)}) custom-call(s32[1]{0:T(128)} %bitcast.core_at.core, s32[1]{0:T(128)} %bitcast.1.side_at, bf16[16,2,4,128]{3,2,1,0:T(4,128)(2,1)} %field_far.1, bf16[16,2,4,128]{3,2,1,0:T(4,128)(2,1)} %cot_far.1, bf16[27,16,256]{2,1,0:T(8,128)(2,1)} %filters.1), custom_call_target="tpu_custom_call" | custom-call | bytes 1048576 | tf_op jit(solution)/shard_map/pallas_call | solution.py:250
  3.4 0.0 copy-start.1
  3.4 12.0 %all-to-all-start = ((bf16[16,16,1792]{2,1,0:T(8,128)(2,1)}), bf16[16,16,1792]{2,1,0:T(8,128)(2,1)S(1)}, u32[]{:S(2)}, u32[]{:S(2)}) async-start(bf16[16,16,1792]{2,1,0:T(8,128)(2,1)} %get-tuple-element.12), calls=%async_computation | async-start | bytes 1835008 | tf_op jit(solution)/shard_map/all_to_all | solution.py:267
  15.4 0.0 copy-done.1
  15.4 2.9 %collective-permute-start.1 = (bf16[16,1024]{1,0:T(8,128)(2,1)S(1)}, bf16[16,1024]{1,0:T(8,128)(2,1)S(1)}, u32[]{:S(2)}, u32[]{:S(2)}) collective-permute-start(bf16[16,1024]{1,0:T(8,128)(2,1)S(1)} %copy-done.1), channel_id=1, source_target_pairs={{16,0},{32,16},{48,32},{64,48},{80,64},{96,80},{112,96},{128,112},... | collective-permute-start | bytes 98312 | tf_op jit(solution)/shard_map/ppermute | solution.py:269
  18.3 3.0 %collective-permute-start = (bf16[16,1024]{1,0:T(8,128)(2,1)S(1)}, bf16[16,1024]{1,0:T(8,128)(2,1)S(1)}, u32[]{:S(2)}, u32[]{:S(2)}) collective-permute-start(bf16[16,1024]{1,0:T(8,128)(2,1)S(1)} %copy-done.1), channel_id=1, source_target_pairs={{0,16},{16,32},{32,48},{48,64},{64,80},{80,96},{96,112},{112,128},... | collective-permute-start | bytes 98312 | tf_op jit(solution)/shard_map/ppermute | solution.py:268
  21.3 0.0 collective-permute-done.1.above
  21.3 1.0 %collective-permute-done.below = bf16[16,1024]{1,0:T(8,128)(2,1)S(1)} collective-permute-done((bf16[16,1024]{1,0:T(8,128)(2,1)S(1)}, bf16[16,1024]{1,0:T(8,128)(2,1)S(1)}, u32[]{:S(2)}, u32[]{:S(2)}) %collective-permute-start) | collective-permute-done | bytes 32800 | tf_op jit(solution)/shard_map/ppermute | solution.py:268
  22.3 15.3 %all-to-all-done = bf16[16,16,1792]{2,1,0:T(8,128)(2,1)S(1)} async-done(((bf16[16,16,1792]{2,1,0:T(8,128)(2,1)}), bf16[16,16,1792]{2,1,0:T(8,128)(2,1)S(1)}, u32[]{:S(2)}, u32[]{:S(2)}) %all-to-all-start) | async-done | bytes 917536 | tf_op jit(solution)/shard_map/all_to_all | solution.py:267
  37.6 0.6 shard_map.59._after
  38.2 0.7 convert_element_type.18
  39.0 6.9 %all-to-all-start.1 = ((f16[8,56,256]{2,1,0:T(8,128)(2,1)}), f16[8,56,256]{2,1,0:T(8,128)(2,1)S(1)}, u32[]{:S(2)}, u32[]{:S(2)}) async-start(f16[8,56,256]{2,1,0:T(8,128)(2,1)} %convert_element_type.18), calls=%async_computation.1 | async-start | bytes 458752 | tf_op jit(solution)/shard_map/all_to_all | solution.py:284
  45.9 2.8 %collective-permute-start.3 = (bf16[256,512]{1,0:T(8,128)(2,1)S(1)}, bf16[256,512]{1,0:T(8,128)(2,1)S(1)}, u32[]{:S(2)}, u32[]{:S(2)}) collective-permute-start(bf16[256,512]{1,0:T(8,128)(2,1)S(1)} %get-tuple-element.15), channel_id=1, source_target_pairs={{0,8},{8,0},{1,9},{9,1},{2,10},{10,2},{3,11},{11,3},{4,12},{12,4},... | collective-permute-start | bytes 786440 | tf_op jit(solution)/shard_map/ppermute | solution.py:282
  48.8 2.2 %collective-permute-start.2 = (bf16[256,256]{1,0:T(8,128)(2,1)S(1)}, bf16[256,256]{1,0:T(8,128)(2,1)S(1)}, u32[]{:S(2)}, u32[]{:S(2)}) collective-permute-start(bf16[256,256]{1,0:T(8,128)(2,1)S(1)} %get-tuple-element.14), channel_id=1, source_target_pairs={{0,16},{16,0},{1,17},{17,1},{2,18},{18,2},{3,19},{19,3},{4,20},{20... | collective-permute-start | bytes 393224 | tf_op jit(solution)/shard_map/ppermute | solution.py:283
  51.0 1.1 %all-to-all-done.1 = f16[8,56,256]{2,1,0:T(8,128)(2,1)S(1)} async-done(((f16[8,56,256]{2,1,0:T(8,128)(2,1)}), f16[8,56,256]{2,1,0:T(8,128)(2,1)S(1)}, u32[]{:S(2)}, u32[]{:S(2)}) %all-to-all-start.1) | async-done | bytes 229408 | tf_op jit(solution)/shard_map/all_to_all | solution.py:284
  52.1 0.2 shard_map.64
  52.3 0.0 copy-start
  52.3 0.7 broadcast_in_dim.4
  53.0 5.9 %all-to-all-start.2 = ((f16[4,56,256]{2,1,0:T(8,128)(2,1)}), f16[4,56,256]{2,1,0:T(8,128)(2,1)S(1)}, u32[]{:S(2)}, u32[]{:S(2)}) async-start(f16[4,56,256]{2,1,0:T(8,128)(2,1)} %broadcast_in_dim.4), calls=%async_computation.2 | async-start | bytes 229376 | tf_op jit(solution)/shard_map/all_to_all | solution.py:303
  58.9 0.0 collective-permute-done.2.swapped
  58.9 0.0 collective-permute-done.3.halves
  58.9 0.0 copy-done
  58.9 0.7 shard_map.61
  59.7 3.4 %collective-permute-start.4 = (f32[32,1024]{1,0:T(8,128)S(1)}, f32[32,1024]{1,0:T(8,128)S(1)}, u32[]{:S(2)}, u32[]{:S(2)}) collective-permute-start(f32[32,1024]{1,0:T(8,128)S(1)} %get-tuple-element.17), channel_id=1, source_target_pairs={{16,32},{32,16},{48,64},{64,48},{80,96},{96,80},{112,128},{128,112... | collective-permute-start | bytes 393224 | tf_op jit(solution)/shard_map/ppermute | solution.py:293
  63.0 3.1 %all-to-all-done.2 = f16[4,56,256]{2,1,0:T(8,128)(2,1)S(1)} async-done(((f16[4,56,256]{2,1,0:T(8,128)(2,1)}), f16[4,56,256]{2,1,0:T(8,128)(2,1)S(1)}, u32[]{:S(2)}, u32[]{:S(2)}) %all-to-all-start.2) | async-done | bytes 114720 | tf_op jit(solution)/shard_map/all_to_all | solution.py:303
  66.1 0.2 shard_map.65
  66.3 0.7 broadcast_in_dim.5
  67.0 6.2 %all-to-all-start.3 = ((f16[8,56,256]{2,1,0:T(8,128)(2,1)}), f16[8,56,256]{2,1,0:T(8,128)(2,1)S(1)}, u32[]{:S(2)}, u32[]{:S(2)}) async-start(f16[8,56,256]{2,1,0:T(8,128)(2,1)} %broadcast_in_dim.5), calls=%async_computation.3 | async-start | bytes 458752 | tf_op jit(solution)/shard_map/all_to_all | solution.py:303
  73.2 2.0 %collective-permute-start.5 = (f32[32,1024]{1,0:T(8,128)S(1)}, f32[32,1024]{1,0:T(8,128)S(1)}, u32[]{:S(2)}, u32[]{:S(2)}) collective-permute-start(f32[32,1024]{1,0:T(8,128)S(1)} %get-tuple-element.18), channel_id=1, source_target_pairs={{0,16},{16,0},{1,17},{17,1},{2,18},{18,2},{3,19},{19,3},{4,20},{20... | collective-permute-start | bytes 393224 | tf_op jit(solution)/shard_map/ppermute | solution.py:307
  75.3 0.0 collective-permute-done.4.far
  75.3 1.2 %collective-permute-done.5.near = f32[32,1024]{1,0:T(8,128)S(1)} collective-permute-done((f32[32,1024]{1,0:T(8,128)S(1)}, f32[32,1024]{1,0:T(8,128)S(1)}, u32[]{:S(2)}, u32[]{:S(2)}) %collective-permute-start.5) | collective-permute-done | bytes 131104 | tf_op jit(solution)/shard_map/ppermute | solution.py:307
  76.5 0.8 %shard_map.63 = (bf16[16,2,4,128]{3,2,1,0:T(4,128)(2,1)}, bf16[16,2,4,128]{3,2,1,0:T(4,128)(2,1)}) custom-call(f32[32,1024]{1,0:T(8,128)S(1)} %shard_map.62.own, f32[32,1024]{1,0:T(8,128)S(1)} %collective-permute-done.5.near), custom_call_target="tpu_custom_call" | custom-call | bytes 262144 | tf_op jit(solution)/shard_map/pallas_call | solution.py:320
  77.3 2.2 %all-to-all-done.3 = f16[8,56,256]{2,1,0:T(8,128)(2,1)S(1)} async-done(((f16[8,56,256]{2,1,0:T(8,128)(2,1)}), f16[8,56,256]{2,1,0:T(8,128)(2,1)S(1)}, u32[]{:S(2)}, u32[]{:S(2)}) %all-to-all-start.3) | async-done | bytes 229408 | tf_op jit(solution)/shard_map/all_to_all | solution.py:303
  79.5 0.8 %shard_map.66 = f32[432,256]{1,0:T(8,128)} custom-call(f32[8,56,256]{2,1,0:T(8,128)S(1)} %convert_element_type.23.full), custom_call_target="tpu_custom_call" | custom-call | bytes 1048576 | tf_op jit(solution)/shard_map/pallas_call | solution.py:309
  (7 shorter events, 0.1 us)
Async XLA Ops:
  3.4 12.0 %copy-start.1 = (bf16[16,1024]{1,0:T(8,128)(2,1)S(1)}, bf16[16,1024]{1,0:T(8,128)(2,1)}, u32[]{:S(2)}) copy-start(bf16[16,1024]{1,0:T(8,128)(2,1)} %get-tuple-element.13.own) | copy-start | bytes 98308
  3.4 34.2 %all-to-all-start = ((bf16[16,16,1792]{2,1,0:T(8,128)(2,1)}), bf16[16,16,1792]{2,1,0:T(8,128)(2,1)S(1)}, u32[]{:S(2)}, u32[]{:S(2)}) async-start(bf16[16,16,1792]{2,1,0:T(8,128)(2,1)} %get-tuple-element.12), calls=%async_computation | async-start | bytes 1835008 | tf_op jit(solution)/shard_map/all_to_all | solution.py:267
  15.4 5.9 %collective-permute-start.1 = (bf16[16,1024]{1,0:T(8,128)(2,1)S(1)}, bf16[16,1024]{1,0:T(8,128)(2,1)S(1)}, u32[]{:S(2)}, u32[]{:S(2)}) collective-permute-start(bf16[16,1024]{1,0:T(8,128)(2,1)S(1)} %copy-done.1), channel_id=1, source_target_pairs={{16,0},{32,16},{48,32},{64,48},{80,64},{96,80},{112,96},{128,112},... | collective-permute-start | bytes 98312 | tf_op jit(solution)/shard_map/ppermute | solution.py:269
  18.3 4.0 %collective-permute-start = (bf16[16,1024]{1,0:T(8,128)(2,1)S(1)}, bf16[16,1024]{1,0:T(8,128)(2,1)S(1)}, u32[]{:S(2)}, u32[]{:S(2)}) collective-permute-start(bf16[16,1024]{1,0:T(8,128)(2,1)S(1)} %copy-done.1), channel_id=1, source_target_pairs={{0,16},{16,32},{32,48},{48,64},{64,80},{80,96},{96,112},{112,128},... | collective-permute-start | bytes 98312 | tf_op jit(solution)/shard_map/ppermute | solution.py:268
  39.0 13.1 %all-to-all-start.1 = ((f16[8,56,256]{2,1,0:T(8,128)(2,1)}), f16[8,56,256]{2,1,0:T(8,128)(2,1)S(1)}, u32[]{:S(2)}, u32[]{:S(2)}) async-start(f16[8,56,256]{2,1,0:T(8,128)(2,1)} %convert_element_type.18), calls=%async_computation.1 | async-start | bytes 458752 | tf_op jit(solution)/shard_map/all_to_all | solution.py:284
  45.9 13.0 %collective-permute-start.3 = (bf16[256,512]{1,0:T(8,128)(2,1)S(1)}, bf16[256,512]{1,0:T(8,128)(2,1)S(1)}, u32[]{:S(2)}, u32[]{:S(2)}) collective-permute-start(bf16[256,512]{1,0:T(8,128)(2,1)S(1)} %get-tuple-element.15), channel_id=1, source_target_pairs={{0,8},{8,0},{1,9},{9,1},{2,10},{10,2},{3,11},{11,3},{4,12},{12,4},... | collective-permute-start | bytes 786440 | tf_op jit(solution)/shard_map/ppermute | solution.py:282
  48.8 10.1 %collective-permute-start.2 = (bf16[256,256]{1,0:T(8,128)(2,1)S(1)}, bf16[256,256]{1,0:T(8,128)(2,1)S(1)}, u32[]{:S(2)}, u32[]{:S(2)}) collective-permute-start(bf16[256,256]{1,0:T(8,128)(2,1)S(1)} %get-tuple-element.14), channel_id=1, source_target_pairs={{0,16},{16,0},{1,17},{17,1},{2,18},{18,2},{3,19},{19,3},{4,20},{20... | collective-permute-start | bytes 393224 | tf_op jit(solution)/shard_map/ppermute | solution.py:283
  52.3 6.6 %copy-start = (bf16[27,16,256]{2,1,0:T(8,128)(2,1)S(1)}, bf16[27,16,256]{2,1,0:T(8,128)(2,1)}, u32[]{:S(2)}) copy-start(bf16[27,16,256]{2,1,0:T(8,128)(2,1)} %filters.1) | copy-start | bytes 663556
  53.0 13.1 %all-to-all-start.2 = ((f16[4,56,256]{2,1,0:T(8,128)(2,1)}), f16[4,56,256]{2,1,0:T(8,128)(2,1)S(1)}, u32[]{:S(2)}, u32[]{:S(2)}) async-start(f16[4,56,256]{2,1,0:T(8,128)(2,1)} %broadcast_in_dim.4), calls=%async_computation.2 | async-start | bytes 229376 | tf_op jit(solution)/shard_map/all_to_all | solution.py:303
  59.7 15.6 %collective-permute-start.4 = (f32[32,1024]{1,0:T(8,128)S(1)}, f32[32,1024]{1,0:T(8,128)S(1)}, u32[]{:S(2)}, u32[]{:S(2)}) collective-permute-start(f32[32,1024]{1,0:T(8,128)S(1)} %get-tuple-element.17), channel_id=1, source_target_pairs={{16,32},{32,16},{48,64},{64,48},{80,96},{96,80},{112,128},{128,112... | collective-permute-start | bytes 393224 | tf_op jit(solution)/shard_map/ppermute | solution.py:293
  67.0 12.5 %all-to-all-start.3 = ((f16[8,56,256]{2,1,0:T(8,128)(2,1)}), f16[8,56,256]{2,1,0:T(8,128)(2,1)S(1)}, u32[]{:S(2)}, u32[]{:S(2)}) async-start(f16[8,56,256]{2,1,0:T(8,128)(2,1)} %broadcast_in_dim.5), calls=%async_computation.3 | async-start | bytes 458752 | tf_op jit(solution)/shard_map/all_to_all | solution.py:303
  73.2 3.2 %collective-permute-start.5 = (f32[32,1024]{1,0:T(8,128)S(1)}, f32[32,1024]{1,0:T(8,128)S(1)}, u32[]{:S(2)}, u32[]{:S(2)}) collective-permute-start(f32[32,1024]{1,0:T(8,128)S(1)} %get-tuple-element.18), channel_id=1, source_target_pairs={{0,16},{16,0},{1,17},{17,1},{2,18},{18,2},{3,19},{19,3},{4,20},{20... | collective-permute-start | bytes 393224 | tf_op jit(solution)/shard_map/ppermute | solution.py:307

commit v9 on v8

--- a/solution.py
+++ b/solution.py
@@ -281,7 +281,7 @@
     )(gathered, own_grad)
     halves = lax.ppermute(half_cells, "side", swap)
     swapped = lax.ppermute(half_taps, "core", swap)
-    parts = lax.all_to_all(own_grad.astype(HALF), ("near", "core"), 0, 0).astype(F32)
+    parts = lax.all_to_all(own_grad.astype(HALF), ("core", "near"), 0, 0).astype(F32)
     to_near, to_far, own_sums = call(
         contributions_body,
         [shape((2 * OWN, CELLS), F32)] * 3,
@@ -305,7 +305,7 @@
     row = summed(1.0, 8, ROW_FLOPS, parts)
     mine = summed(SCALE, 4, 0, spread(row, 4, "far"), own_sums)
     from_near = lax.ppermute(to_near, "core", swap)
-    full = spread(mine, 8, ("near", "core"))
+    full = spread(mine, 8, ("core", "near"))
     weight_grad = call(
         finish_body,
         [shape((ROWS, 256), F32)],

time: 81 us -> 80.7 us (level)
  no operation moved by 1% of the time
where the time goes in v9:
time: 80.7 us; the launch traced here: 80 us
  starting transfers between devices  46.7 us (58%)
  waiting for transfers between devices  24.2 us (30%)
  Pallas kernels  6.07 us (8%)
  local copies, waits for them, and re-layouts  1.38 us (2%)
  between operations  0.82 us (1%)
  other arithmetic  0.81 us (1%)
    all_to_all x1, waiting for transfers between devices, per_device(): gathered = lax.all_to_all(packed, chan, 0, 0).reshape(256, WIDE)  15.3 us
    all_to_all x1, starting transfers between devices, per_device(): gathered = lax.all_to_all(packed, chan, 0, 0).reshape(256, WIDE)  12 us
    all_to_all x2, starting transfers between devices, spread(): return lax.all_to_all(many, axes, 0, 0).astype(F32)  11.8 us
    all_to_all x1, starting transfers between devices, per_device(): lax.all_to_all(own_grad.astype(HALF), ('core', 'near'), 0, 0).astype(F32)  6.92 us
    all_to_all x2, waiting for transfers between devices, spread(): return lax.all_to_all(many, axes, 0, 0).astype(F32)  5.56 us
    ppermute x1, starting transfers between devices, per_device(): from_far = lax.ppermute(to_far, space, across)  3.03 us
    ppermute x1, starting transfers between devices, per_device(): below = lax.ppermute(own_cot, space, up)  3.02 us
    ppermute x1, starting transfers between devices, per_device(): above = lax.ppermute(own_cot, space, down)  2.86 us
  transfers between devices with their start and end apart: 10, of which 6 were waited for; matrix products, arithmetic and copies ran while one was open for 2% of the time, Pallas kernels for 2%

profile of v9, /device:TPU:1, one launch (start us, length us, event | category | flops | bytes accessed | tf_op | source)
XLA Modules:
  0.0 80.0 jit_solution(2332072730817503804)
XLA Ops:
  0.6 2.7 %shard_map.58 = (bf16[16,16,1792]{2,1,0:T(8,128)(2,1)}, bf16[16,1024]{1,0:T(8,128)(2,1)}) custom-call(s32[1]{0:T(128)} %bitcast.core_at.core, s32[1]{0:T(128)} %bitcast.1.side_at, bf16[16,2,4,128]{3,2,1,0:T(4,128)(2,1)} %field_far.1, bf16[16,2,4,128]{3,2,1,0:T(4,128)(2,1)} %cot_far.1, bf16[27,16,256]{2,1,0:T(8,128)(2,1)} %filters.1), custom_call_target="tpu_custom_call" | custom-call | bytes 1048576 | tf_op jit(solution)/shard_map/pallas_call | solution.py:250
  3.4 0.0 copy-start.1
  3.4 12.0 %all-to-all-start = ((bf16[16,16,1792]{2,1,0:T(8,128)(2,1)}), bf16[16,16,1792]{2,1,0:T(8,128)(2,1)S(1)}, u32[]{:S(2)}, u32[]{:S(2)}) async-start(bf16[16,16,1792]{2,1,0:T(8,128)(2,1)} %get-tuple-element.12), calls=%async_computation | async-start | bytes 1835008 | tf_op jit(solution)/shard_map/all_to_all | solution.py:267
  15.4 0.0 copy-done.1
  15.4 2.9 %collective-permute-start.1 = (bf16[16,1024]{1,0:T(8,128)(2,1)S(1)}, bf16[16,1024]{1,0:T(8,128)(2,1)S(1)}, u32[]{:S(2)}, u32[]{:S(2)}) collective-permute-start(bf16[16,1024]{1,0:T(8,128)(2,1)S(1)} %copy-done.1), channel_id=1, source_target_pairs={{16,0},{32,16},{48,32},{64,48},{80,64},{96,80},{112,96},{128,112},... | collective-permute-start | bytes 98312 | tf_op jit(solution)/shard_map/ppermute | solution.py:269
  18.3 3.0 %collective-permute-start = (bf16[16,1024]{1,0:T(8,128)(2,1)S(1)}, bf16[16,1024]{1,0:T(8,128)(2,1)S(1)}, u32[]{:S(2)}, u32[]{:S(2)}) collective-permute-start(bf16[16,1024]{1,0:T(8,128)(2,1)S(1)} %copy-done.1), channel_id=1, source_target_pairs={{0,16},{16,32},{32,48},{48,64},{64,80},{80,96},{96,112},{112,128},... | collective-permute-start | bytes 98312 | tf_op jit(solution)/shard_map/ppermute | solution.py:268
  21.3 0.0 collective-permute-done.1.above
  21.3 1.0 %collective-permute-done.below = bf16[16,1024]{1,0:T(8,128)(2,1)S(1)} collective-permute-done((bf16[16,1024]{1,0:T(8,128)(2,1)S(1)}, bf16[16,1024]{1,0:T(8,128)(2,1)S(1)}, u32[]{:S(2)}, u32[]{:S(2)}) %collective-permute-start) | collective-permute-done | bytes 32800 | tf_op jit(solution)/shard_map/ppermute | solution.py:268
  22.3 15.3 %all-to-all-done = bf16[16,16,1792]{2,1,0:T(8,128)(2,1)S(1)} async-done(((bf16[16,16,1792]{2,1,0:T(8,128)(2,1)}), bf16[16,16,1792]{2,1,0:T(8,128)(2,1)S(1)}, u32[]{:S(2)}, u32[]{:S(2)}) %all-to-all-start) | async-done | bytes 917536 | tf_op jit(solution)/shard_map/all_to_all | solution.py:267
  37.6 0.6 shard_map.59._after
  38.2 0.7 convert_element_type.18
  39.0 6.9 %all-to-all-start.1 = ((f16[8,56,256]{2,1,0:T(8,128)(2,1)}), f16[8,56,256]{2,1,0:T(8,128)(2,1)S(1)}, u32[]{:S(2)}, u32[]{:S(2)}) async-start(f16[8,56,256]{2,1,0:T(8,128)(2,1)} %convert_element_type.18), calls=%async_computation.1 | async-start | bytes 458752 | tf_op jit(solution)/shard_map/all_to_all | solution.py:284
  45.9 2.8 %collective-permute-start.3 = (bf16[256,512]{1,0:T(8,128)(2,1)S(1)}, bf16[256,512]{1,0:T(8,128)(2,1)S(1)}, u32[]{:S(2)}, u32[]{:S(2)}) collective-permute-start(bf16[256,512]{1,0:T(8,128)(2,1)S(1)} %get-tuple-element.15), channel_id=1, source_target_pairs={{0,8},{8,0},{1,9},{9,1},{2,10},{10,2},{3,11},{11,3},{4,12},{12,4},... | collective-permute-start | bytes 786440 | tf_op jit(solution)/shard_map/ppermute | solution.py:282
  48.8 2.2 %collective-permute-start.2 = (bf16[256,256]{1,0:T(8,128)(2,1)S(1)}, bf16[256,256]{1,0:T(8,128)(2,1)S(1)}, u32[]{:S(2)}, u32[]{:S(2)}) collective-permute-start(bf16[256,256]{1,0:T(8,128)(2,1)S(1)} %get-tuple-element.14), channel_id=1, source_target_pairs={{0,16},{16,0},{1,17},{17,1},{2,18},{18,2},{3,19},{19,3},{4,20},{20... | collective-permute-start | bytes 393224 | tf_op jit(solution)/shard_map/ppermute | solution.py:283
  51.0 1.1 %all-to-all-done.1 = f16[8,56,256]{2,1,0:T(8,128)(2,1)S(1)} async-done(((f16[8,56,256]{2,1,0:T(8,128)(2,1)}), f16[8,56,256]{2,1,0:T(8,128)(2,1)S(1)}, u32[]{:S(2)}, u32[]{:S(2)}) %all-to-all-start.1) | async-done | bytes 229408 | tf_op jit(solution)/shard_map/all_to_all | solution.py:284
  52.1 0.2 shard_map.64
  52.3 0.0 copy-start
  52.3 0.7 broadcast_in_dim.4
  53.0 5.9 %all-to-all-start.2 = ((f16[4,56,256]{2,1,0:T(8,128)(2,1)}), f16[4,56,256]{2,1,0:T(8,128)(2,1)S(1)}, u32[]{:S(2)}, u32[]{:S(2)}) async-start(f16[4,56,256]{2,1,0:T(8,128)(2,1)} %broadcast_in_dim.4), calls=%async_computation.2 | async-start | bytes 229376 | tf_op jit(solution)/shard_map/all_to_all | solution.py:303
  58.9 0.0 collective-permute-done.2.swapped
  58.9 0.0 collective-permute-done.3.halves
  58.9 0.0 copy-done
  58.9 0.7 shard_map.61
  59.7 3.0 %collective-permute-start.4 = (f32[32,1024]{1,0:T(8,128)S(1)}, f32[32,1024]{1,0:T(8,128)S(1)}, u32[]{:S(2)}, u32[]{:S(2)}) collective-permute-start(f32[32,1024]{1,0:T(8,128)S(1)} %get-tuple-element.17), channel_id=1, source_target_pairs={{16,32},{32,16},{48,64},{64,48},{80,96},{96,80},{112,128},{128,112... | collective-permute-start | bytes 393224 | tf_op jit(solution)/shard_map/ppermute | solution.py:293
  62.7 3.4 %all-to-all-done.2 = f16[4,56,256]{2,1,0:T(8,128)(2,1)S(1)} async-done(((f16[4,56,256]{2,1,0:T(8,128)(2,1)}), f16[4,56,256]{2,1,0:T(8,128)(2,1)S(1)}, u32[]{:S(2)}, u32[]{:S(2)}) %all-to-all-start.2) | async-done | bytes 114720 | tf_op jit(solution)/shard_map/all_to_all | solution.py:303
  66.1 0.2 shard_map.65
  66.3 0.7 broadcast_in_dim.5
  67.0 5.9 %all-to-all-start.3 = ((f16[8,56,256]{2,1,0:T(8,128)(2,1)}), f16[8,56,256]{2,1,0:T(8,128)(2,1)S(1)}, u32[]{:S(2)}, u32[]{:S(2)}) async-start(f16[8,56,256]{2,1,0:T(8,128)(2,1)} %broadcast_in_dim.5), calls=%async_computation.3 | async-start | bytes 458752 | tf_op jit(solution)/shard_map/all_to_all | solution.py:303
  72.9 2.0 %collective-permute-start.5 = (f32[32,1024]{1,0:T(8,128)S(1)}, f32[32,1024]{1,0:T(8,128)S(1)}, u32[]{:S(2)}, u32[]{:S(2)}) collective-permute-start(f32[32,1024]{1,0:T(8,128)S(1)} %get-tuple-element.18), channel_id=1, source_target_pairs={{0,16},{16,0},{1,17},{17,1},{2,18},{18,2},{3,19},{19,3},{4,20},{20... | collective-permute-start | bytes 393224 | tf_op jit(solution)/shard_map/ppermute | solution.py:307
  74.9 0.0 collective-permute-done.4.far
  75.0 1.2 %collective-permute-done.5.near = f32[32,1024]{1,0:T(8,128)S(1)} collective-permute-done((f32[32,1024]{1,0:T(8,128)S(1)}, f32[32,1024]{1,0:T(8,128)S(1)}, u32[]{:S(2)}, u32[]{:S(2)}) %collective-permute-start.5) | collective-permute-done | bytes 131104 | tf_op jit(solution)/shard_map/ppermute | solution.py:307
  76.1 0.8 %shard_map.63 = (bf16[16,2,4,128]{3,2,1,0:T(4,128)(2,1)}, bf16[16,2,4,128]{3,2,1,0:T(4,128)(2,1)}) custom-call(f32[32,1024]{1,0:T(8,128)S(1)} %shard_map.62.own, f32[32,1024]{1,0:T(8,128)S(1)} %collective-permute-done.5.near), custom_call_target="tpu_custom_call" | custom-call | bytes 262144 | tf_op jit(solution)/shard_map/pallas_call | solution.py:320
  77.0 2.2 %all-to-all-done.3 = f16[8,56,256]{2,1,0:T(8,128)(2,1)S(1)} async-done(((f16[8,56,256]{2,1,0:T(8,128)(2,1)}), f16[8,56,256]{2,1,0:T(8,128)(2,1)S(1)}, u32[]{:S(2)}, u32[]{:S(2)}) %all-to-all-start.3) | async-done | bytes 229408 | tf_op jit(solution)/shard_map/all_to_all | solution.py:303
  79.2 0.8 %shard_map.66 = f32[432,256]{1,0:T(8,128)} custom-call(f32[8,56,256]{2,1,0:T(8,128)S(1)} %convert_element_type.23.full), custom_call_target="tpu_custom_call" | custom-call | bytes 1048576 | tf_op jit(solution)/shard_map/pallas_call | solution.py:309
  (7 shorter events, 0.1 us)
Async XLA Ops:
  3.4 12.0 %copy-start.1 = (bf16[16,1024]{1,0:T(8,128)(2,1)S(1)}, bf16[16,1024]{1,0:T(8,128)(2,1)}, u32[]{:S(2)}) copy-start(bf16[16,1024]{1,0:T(8,128)(2,1)} %get-tuple-element.13.own) | copy-start | bytes 98308
  3.4 34.2 %all-to-all-start = ((bf16[16,16,1792]{2,1,0:T(8,128)(2,1)}), bf16[16,16,1792]{2,1,0:T(8,128)(2,1)S(1)}, u32[]{:S(2)}, u32[]{:S(2)}) async-start(bf16[16,16,1792]{2,1,0:T(8,128)(2,1)} %get-tuple-element.12), calls=%async_computation | async-start | bytes 1835008 | tf_op jit(solution)/shard_map/all_to_all | solution.py:267
  15.4 5.9 %collective-permute-start.1 = (bf16[16,1024]{1,0:T(8,128)(2,1)S(1)}, bf16[16,1024]{1,0:T(8,128)(2,1)S(1)}, u32[]{:S(2)}, u32[]{:S(2)}) collective-permute-start(bf16[16,1024]{1,0:T(8,128)(2,1)S(1)} %copy-done.1), channel_id=1, source_target_pairs={{16,0},{32,16},{48,32},{64,48},{80,64},{96,80},{112,96},{128,112},... | collective-permute-start | bytes 98312 | tf_op jit(solution)/shard_map/ppermute | solution.py:269
  18.3 4.0 %collective-permute-start = (bf16[16,1024]{1,0:T(8,128)(2,1)S(1)}, bf16[16,1024]{1,0:T(8,128)(2,1)S(1)}, u32[]{:S(2)}, u32[]{:S(2)}) collective-permute-start(bf16[16,1024]{1,0:T(8,128)(2,1)S(1)} %copy-done.1), channel_id=1, source_target_pairs={{0,16},{16,32},{32,48},{48,64},{64,80},{80,96},{96,112},{112,128},... | collective-permute-start | bytes 98312 | tf_op jit(solution)/shard_map/ppermute | solution.py:268
  39.0 13.1 %all-to-all-start.1 = ((f16[8,56,256]{2,1,0:T(8,128)(2,1)}), f16[8,56,256]{2,1,0:T(8,128)(2,1)S(1)}, u32[]{:S(2)}, u32[]{:S(2)}) async-start(f16[8,56,256]{2,1,0:T(8,128)(2,1)} %convert_element_type.18), calls=%async_computation.1 | async-start | bytes 458752 | tf_op jit(solution)/shard_map/all_to_all | solution.py:284
  45.9 13.0 %collective-permute-start.3 = (bf16[256,512]{1,0:T(8,128)(2,1)S(1)}, bf16[256,512]{1,0:T(8,128)(2,1)S(1)}, u32[]{:S(2)}, u32[]{:S(2)}) collective-permute-start(bf16[256,512]{1,0:T(8,128)(2,1)S(1)} %get-tuple-element.15), channel_id=1, source_target_pairs={{0,8},{8,0},{1,9},{9,1},{2,10},{10,2},{3,11},{11,3},{4,12},{12,4},... | collective-permute-start | bytes 786440 | tf_op jit(solution)/shard_map/ppermute | solution.py:282
  48.8 10.2 %collective-permute-start.2 = (bf16[256,256]{1,0:T(8,128)(2,1)S(1)}, bf16[256,256]{1,0:T(8,128)(2,1)S(1)}, u32[]{:S(2)}, u32[]{:S(2)}) collective-permute-start(bf16[256,256]{1,0:T(8,128)(2,1)S(1)} %get-tuple-element.14), channel_id=1, source_target_pairs={{0,16},{16,0},{1,17},{17,1},{2,18},{18,2},{3,19},{19,3},{4,20},{20... | collective-permute-start | bytes 393224 | tf_op jit(solution)/shard_map/ppermute | solution.py:283
  52.3 6.6 %copy-start = (bf16[27,16,256]{2,1,0:T(8,128)(2,1)S(1)}, bf16[27,16,256]{2,1,0:T(8,128)(2,1)}, u32[]{:S(2)}) copy-start(bf16[27,16,256]{2,1,0:T(8,128)(2,1)} %filters.1) | copy-start | bytes 663556
  53.0 13.1 %all-to-all-start.2 = ((f16[4,56,256]{2,1,0:T(8,128)(2,1)}), f16[4,56,256]{2,1,0:T(8,128)(2,1)S(1)}, u32[]{:S(2)}, u32[]{:S(2)}) async-start(f16[4,56,256]{2,1,0:T(8,128)(2,1)} %broadcast_in_dim.4), calls=%async_computation.2 | async-start | bytes 229376 | tf_op jit(solution)/shard_map/all_to_all | solution.py:303
  59.7 15.2 %collective-permute-start.4 = (f32[32,1024]{1,0:T(8,128)S(1)}, f32[32,1024]{1,0:T(8,128)S(1)}, u32[]{:S(2)}, u32[]{:S(2)}) collective-permute-start(f32[32,1024]{1,0:T(8,128)S(1)} %get-tuple-element.17), channel_id=1, source_target_pairs={{16,32},{32,16},{48,64},{64,48},{80,96},{96,80},{112,128},{128,112... | collective-permute-start | bytes 393224 | tf_op jit(solution)/shard_map/ppermute | solution.py:293
  67.0 12.1 %all-to-all-start.3 = ((f16[8,56,256]{2,1,0:T(8,128)(2,1)}), f16[8,56,256]{2,1,0:T(8,128)(2,1)S(1)}, u32[]{:S(2)}, u32[]{:S(2)}) async-start(f16[8,56,256]{2,1,0:T(8,128)(2,1)} %broadcast_in_dim.5), calls=%async_computation.3 | async-start | bytes 458752 | tf_op jit(solution)/shard_map/all_to_all | solution.py:303
  72.9 3.2 %collective-permute-start.5 = (f32[32,1024]{1,0:T(8,128)S(1)}, f32[32,1024]{1,0:T(8,128)S(1)}, u32[]{:S(2)}, u32[]{:S(2)}) collective-permute-start(f32[32,1024]{1,0:T(8,128)S(1)} %get-tuple-element.18), channel_id=1, source_target_pairs={{0,16},{16,0},{1,17},{17,1},{2,18},{18,2},{3,19},{19,3},{4,20},{20... | collective-permute-start | bytes 393224 | tf_op jit(solution)/shard_map/ppermute | solution.py:307

commit v10 on v9

--- a/solution.py
+++ b/solution.py
@@ -61,7 +61,8 @@
 
 
 def pack_body(
-    core_at, side_at, field_far, cot_far, filters_far, out, own_cot, field, cotangent, filters, cells, taps, arrived, sent
+    core_at, side_at, field_far, cot_far, filters_far, out, own_far,
+    field, cotangent, filters, own_cot, cells, taps, arrived, sent,
 ):
     core, side = core_at[0], side_at[0]
     own_taps = filters_far.at[pl.ds(11 * core, 16)]
@@ -84,6 +85,7 @@
         pltpu.make_async_copy(cells.at[c // 8], out.at[c, :, pl.ds(0, TAPS_AT)], sent.at[c])
         for c in range(16)
     ]
+    sends.append(pltpu.make_async_copy(own_cot, own_far, sent.at[17]))
     for send in sends:
         send.start()
     copies[2].wait()
@@ -255,14 +257,15 @@
             pltpu.VMEM((OWN, 2, 4, 128), BF),
             pltpu.VMEM((OWN, 2, 4, 128), BF),
             pltpu.VMEM((16, OWN, 256), BF),
+            pltpu.VMEM((OWN, CELLS), BF),
             pltpu.VMEM((2, OWN, TAPS_AT), BF),
             pltpu.VMEM((16, OWN, 256), BF),
             pltpu.SemaphoreType.DMA((3,)),
-            pltpu.SemaphoreType.DMA((17,)),
+            pltpu.SemaphoreType.DMA((18,)),
         ],
         moved=1 << 20,
         limit=PACK_LIMIT,
-        outs_at=[FAR, VMEM],
+        outs_at=[FAR, FAR],
     )(core, side, field, cotangent, filters)
     gathered = lax.all_to_all(packed, chan, 0, 0).reshape(256, WIDE)
     below = lax.ppermute(own_cot, space, up)

time: 80.7 us -> 80.1 us (level)
  no operation moved by 1% of the time
where the time goes in v10:
time: 80.1 us; the launch traced here: 79.4 us
  starting transfers between devices  46.7 us (58%)
  waiting for transfers between devices  24.2 us (30%)
  Pallas kernels  5.47 us (7%)
  local copies, waits for them, and re-layouts  1.38 us (2%)
  between operations  0.82 us (1%)
  other arithmetic  0.81 us (1%)
    all_to_all x1, waiting for transfers between devices, per_device(): gathered = lax.all_to_all(packed, chan, 0, 0).reshape(256, WIDE)  15.3 us
    all_to_all x1, starting transfers between devices, per_device(): gathered = lax.all_to_all(packed, chan, 0, 0).reshape(256, WIDE)  12 us
    all_to_all x2, starting transfers between devices, spread(): return lax.all_to_all(many, axes, 0, 0).astype(F32)  11.8 us
    all_to_all x1, starting transfers between devices, per_device(): lax.all_to_all(own_grad.astype(HALF), ('core', 'near'), 0, 0).astype(F32)  6.91 us
    all_to_all x2, waiting for transfers between devices, spread(): return lax.all_to_all(many, axes, 0, 0).astype(F32)  5.55 us
    ppermute x1, starting transfers between devices, per_device(): from_far = lax.ppermute(to_far, space, across)  3.03 us
    ppermute x1, starting transfers between devices, per_device(): below = lax.ppermute(own_cot, space, up)  3.02 us
    ppermute x1, starting transfers between devices, per_device(): above = lax.ppermute(own_cot, space, down)  2.86 us
  transfers between devices with their start and end apart: 10, of which 6 were waited for; matrix products, arithmetic and copies ran while one was open for 2% of the time, Pallas kernels for 2%

profile of v10, /device:TPU:1, one launch (start us, length us, event | category | flops | bytes accessed | tf_op | source)
XLA Modules:
  0.0 79.4 jit_solution(18260950693330246162)
XLA Ops:
  0.6 2.1 %shard_map.58 = (bf16[16,16,1792]{2,1,0:T(8,128)(2,1)}, bf16[16,1024]{1,0:T(8,128)(2,1)}) custom-call(s32[1]{0:T(128)} %bitcast.core_at.core, s32[1]{0:T(128)} %bitcast.1.side_at, bf16[16,2,4,128]{3,2,1,0:T(4,128)(2,1)} %field_far.1, bf16[16,2,4,128]{3,2,1,0:T(4,128)(2,1)} %cot_far.1, bf16[27,16,256]{2,1,0:T(8,128)(2,1)} %filters.1), custom_call_target="tpu_custom_call" | custom-call | bytes 1048576 | tf_op jit(solution)/shard_map/pallas_call | solution.py:252
  2.8 0.0 copy-start.1
  2.8 12.0 %all-to-all-start = ((bf16[16,16,1792]{2,1,0:T(8,128)(2,1)}), bf16[16,16,1792]{2,1,0:T(8,128)(2,1)S(1)}, u32[]{:S(2)}, u32[]{:S(2)}) async-start(bf16[16,16,1792]{2,1,0:T(8,128)(2,1)} %get-tuple-element.12), calls=%async_computation | async-start | bytes 1835008 | tf_op jit(solution)/shard_map/all_to_all | solution.py:270
  14.8 0.0 copy-done.1
  14.8 2.9 %collective-permute-start.1 = (bf16[16,1024]{1,0:T(8,128)(2,1)S(1)}, bf16[16,1024]{1,0:T(8,128)(2,1)S(1)}, u32[]{:S(2)}, u32[]{:S(2)}) collective-permute-start(bf16[16,1024]{1,0:T(8,128)(2,1)S(1)} %copy-done.1), channel_id=1, source_target_pairs={{16,0},{32,16},{48,32},{64,48},{80,64},{96,80},{112,96},{128,112},... | collective-permute-start | bytes 98312 | tf_op jit(solution)/shard_map/ppermute | solution.py:272
  17.7 3.0 %collective-permute-start = (bf16[16,1024]{1,0:T(8,128)(2,1)S(1)}, bf16[16,1024]{1,0:T(8,128)(2,1)S(1)}, u32[]{:S(2)}, u32[]{:S(2)}) collective-permute-start(bf16[16,1024]{1,0:T(8,128)(2,1)S(1)} %copy-done.1), channel_id=1, source_target_pairs={{0,16},{16,32},{32,48},{48,64},{64,80},{80,96},{96,112},{112,128},... | collective-permute-start | bytes 98312 | tf_op jit(solution)/shard_map/ppermute | solution.py:271
  20.7 0.0 collective-permute-done.1.above
  20.7 1.0 %collective-permute-done.below = bf16[16,1024]{1,0:T(8,128)(2,1)S(1)} collective-permute-done((bf16[16,1024]{1,0:T(8,128)(2,1)S(1)}, bf16[16,1024]{1,0:T(8,128)(2,1)S(1)}, u32[]{:S(2)}, u32[]{:S(2)}) %collective-permute-start) | collective-permute-done | bytes 32800 | tf_op jit(solution)/shard_map/ppermute | solution.py:271
  21.7 15.3 %all-to-all-done = bf16[16,16,1792]{2,1,0:T(8,128)(2,1)S(1)} async-done(((bf16[16,16,1792]{2,1,0:T(8,128)(2,1)}), bf16[16,16,1792]{2,1,0:T(8,128)(2,1)S(1)}, u32[]{:S(2)}, u32[]{:S(2)}) %all-to-all-start) | async-done | bytes 917536 | tf_op jit(solution)/shard_map/all_to_all | solution.py:270
  37.0 0.6 shard_map.59._after
  37.7 0.7 convert_element_type.18
  38.4 6.9 %all-to-all-start.1 = ((f16[8,56,256]{2,1,0:T(8,128)(2,1)}), f16[8,56,256]{2,1,0:T(8,128)(2,1)S(1)}, u32[]{:S(2)}, u32[]{:S(2)}) async-start(f16[8,56,256]{2,1,0:T(8,128)(2,1)} %convert_element_type.18), calls=%async_computation.1 | async-start | bytes 458752 | tf_op jit(solution)/shard_map/all_to_all | solution.py:287
  45.3 2.8 %collective-permute-start.3 = (bf16[256,512]{1,0:T(8,128)(2,1)S(1)}, bf16[256,512]{1,0:T(8,128)(2,1)S(1)}, u32[]{:S(2)}, u32[]{:S(2)}) collective-permute-start(bf16[256,512]{1,0:T(8,128)(2,1)S(1)} %get-tuple-element.15), channel_id=1, source_target_pairs={{0,8},{8,0},{1,9},{9,1},{2,10},{10,2},{3,11},{11,3},{4,12},{12,4},... | collective-permute-start | bytes 786440 | tf_op jit(solution)/shard_map/ppermute | solution.py:285
  48.2 2.2 %collective-permute-start.2 = (bf16[256,256]{1,0:T(8,128)(2,1)S(1)}, bf16[256,256]{1,0:T(8,128)(2,1)S(1)}, u32[]{:S(2)}, u32[]{:S(2)}) collective-permute-start(bf16[256,256]{1,0:T(8,128)(2,1)S(1)} %get-tuple-element.14), channel_id=1, source_target_pairs={{0,16},{16,0},{1,17},{17,1},{2,18},{18,2},{3,19},{19,3},{4,20},{20... | collective-permute-start | bytes 393224 | tf_op jit(solution)/shard_map/ppermute | solution.py:286
  50.4 1.1 %all-to-all-done.1 = f16[8,56,256]{2,1,0:T(8,128)(2,1)S(1)} async-done(((f16[8,56,256]{2,1,0:T(8,128)(2,1)}), f16[8,56,256]{2,1,0:T(8,128)(2,1)S(1)}, u32[]{:S(2)}, u32[]{:S(2)}) %all-to-all-start.1) | async-done | bytes 229408 | tf_op jit(solution)/shard_map/all_to_all | solution.py:287
  51.5 0.2 shard_map.64
  51.7 0.0 copy-start
  51.7 0.7 broadcast_in_dim.4
  52.4 5.9 %all-to-all-start.2 = ((f16[4,56,256]{2,1,0:T(8,128)(2,1)}), f16[4,56,256]{2,1,0:T(8,128)(2,1)S(1)}, u32[]{:S(2)}, u32[]{:S(2)}) async-start(f16[4,56,256]{2,1,0:T(8,128)(2,1)} %broadcast_in_dim.4), calls=%async_computation.2 | async-start | bytes 229376 | tf_op jit(solution)/shard_map/all_to_all | solution.py:306
  58.3 0.0 collective-permute-done.2.swapped
  58.3 0.0 collective-permute-done.3.halves
  58.3 0.0 copy-done
  58.3 0.7 shard_map.61
  59.1 3.0 %collective-permute-start.4 = (f32[32,1024]{1,0:T(8,128)S(1)}, f32[32,1024]{1,0:T(8,128)S(1)}, u32[]{:S(2)}, u32[]{:S(2)}) collective-permute-start(f32[32,1024]{1,0:T(8,128)S(1)} %get-tuple-element.17), channel_id=1, source_target_pairs={{16,32},{32,16},{48,64},{64,48},{80,96},{96,80},{112,128},{128,112... | collective-permute-start | bytes 393224 | tf_op jit(solution)/shard_map/ppermute | solution.py:296
  62.1 3.4 %all-to-all-done.2 = f16[4,56,256]{2,1,0:T(8,128)(2,1)S(1)} async-done(((f16[4,56,256]{2,1,0:T(8,128)(2,1)}), f16[4,56,256]{2,1,0:T(8,128)(2,1)S(1)}, u32[]{:S(2)}, u32[]{:S(2)}) %all-to-all-start.2) | async-done | bytes 114720 | tf_op jit(solution)/shard_map/all_to_all | solution.py:306
  65.5 0.2 shard_map.65
  65.7 0.7 broadcast_in_dim.5
  66.4 5.9 %all-to-all-start.3 = ((f16[8,56,256]{2,1,0:T(8,128)(2,1)}), f16[8,56,256]{2,1,0:T(8,128)(2,1)S(1)}, u32[]{:S(2)}, u32[]{:S(2)}) async-start(f16[8,56,256]{2,1,0:T(8,128)(2,1)} %broadcast_in_dim.5), calls=%async_computation.3 | async-start | bytes 458752 | tf_op jit(solution)/shard_map/all_to_all | solution.py:306
  72.3 2.0 %collective-permute-start.5 = (f32[32,1024]{1,0:T(8,128)S(1)}, f32[32,1024]{1,0:T(8,128)S(1)}, u32[]{:S(2)}, u32[]{:S(2)}) collective-permute-start(f32[32,1024]{1,0:T(8,128)S(1)} %get-tuple-element.18), channel_id=1, source_target_pairs={{0,16},{16,0},{1,17},{17,1},{2,18},{18,2},{3,19},{19,3},{4,20},{20... | collective-permute-start | bytes 393224 | tf_op jit(solution)/shard_map/ppermute | solution.py:310
  74.3 0.0 collective-permute-done.4.far
  74.4 1.2 %collective-permute-done.5.near = f32[32,1024]{1,0:T(8,128)S(1)} collective-permute-done((f32[32,1024]{1,0:T(8,128)S(1)}, f32[32,1024]{1,0:T(8,128)S(1)}, u32[]{:S(2)}, u32[]{:S(2)}) %collective-permute-start.5) | collective-permute-done | bytes 131104 | tf_op jit(solution)/shard_map/ppermute | solution.py:310
  75.5 0.8 %shard_map.63 = (bf16[16,2,4,128]{3,2,1,0:T(4,128)(2,1)}, bf16[16,2,4,128]{3,2,1,0:T(4,128)(2,1)}) custom-call(f32[32,1024]{1,0:T(8,128)S(1)} %shard_map.62.own, f32[32,1024]{1,0:T(8,128)S(1)} %collective-permute-done.5.near), custom_call_target="tpu_custom_call" | custom-call | bytes 262144 | tf_op jit(solution)/shard_map/pallas_call | solution.py:323
  76.4 2.2 %all-to-all-done.3 = f16[8,56,256]{2,1,0:T(8,128)(2,1)S(1)} async-done(((f16[8,56,256]{2,1,0:T(8,128)(2,1)}), f16[8,56,256]{2,1,0:T(8,128)(2,1)S(1)}, u32[]{:S(2)}, u32[]{:S(2)}) %all-to-all-start.3) | async-done | bytes 229408 | tf_op jit(solution)/shard_map/all_to_all | solution.py:306
  78.6 0.8 %shard_map.66 = f32[432,256]{1,0:T(8,128)} custom-call(f32[8,56,256]{2,1,0:T(8,128)S(1)} %convert_element_type.23.full), custom_call_target="tpu_custom_call" | custom-call | bytes 1048576 | tf_op jit(solution)/shard_map/pallas_call | solution.py:312
  (7 shorter events, 0.1 us)
Async XLA Ops:
  2.8 12.0 %copy-start.1 = (bf16[16,1024]{1,0:T(8,128)(2,1)S(1)}, bf16[16,1024]{1,0:T(8,128)(2,1)}, u32[]{:S(2)}) copy-start(bf16[16,1024]{1,0:T(8,128)(2,1)} %get-tuple-element.13.own) | copy-start | bytes 98308
  2.8 34.2 %all-to-all-start = ((bf16[16,16,1792]{2,1,0:T(8,128)(2,1)}), bf16[16,16,1792]{2,1,0:T(8,128)(2,1)S(1)}, u32[]{:S(2)}, u32[]{:S(2)}) async-start(bf16[16,16,1792]{2,1,0:T(8,128)(2,1)} %get-tuple-element.12), calls=%async_computation | async-start | bytes 1835008 | tf_op jit(solution)/shard_map/all_to_all | solution.py:270
  14.8 5.9 %collective-permute-start.1 = (bf16[16,1024]{1,0:T(8,128)(2,1)S(1)}, bf16[16,1024]{1,0:T(8,128)(2,1)S(1)}, u32[]{:S(2)}, u32[]{:S(2)}) collective-permute-start(bf16[16,1024]{1,0:T(8,128)(2,1)S(1)} %copy-done.1), channel_id=1, source_target_pairs={{16,0},{32,16},{48,32},{64,48},{80,64},{96,80},{112,96},{128,112},... | collective-permute-start | bytes 98312 | tf_op jit(solution)/shard_map/ppermute | solution.py:272
  17.7 4.0 %collective-permute-start = (bf16[16,1024]{1,0:T(8,128)(2,1)S(1)}, bf16[16,1024]{1,0:T(8,128)(2,1)S(1)}, u32[]{:S(2)}, u32[]{:S(2)}) collective-permute-start(bf16[16,1024]{1,0:T(8,128)(2,1)S(1)} %copy-done.1), channel_id=1, source_target_pairs={{0,16},{16,32},{32,48},{48,64},{64,80},{80,96},{96,112},{112,128},... | collective-permute-start | bytes 98312 | tf_op jit(solution)/shard_map/ppermute | solution.py:271
  38.4 13.1 %all-to-all-start.1 = ((f16[8,56,256]{2,1,0:T(8,128)(2,1)}), f16[8,56,256]{2,1,0:T(8,128)(2,1)S(1)}, u32[]{:S(2)}, u32[]{:S(2)}) async-start(f16[8,56,256]{2,1,0:T(8,128)(2,1)} %convert_element_type.18), calls=%async_computation.1 | async-start | bytes 458752 | tf_op jit(solution)/shard_map/all_to_all | solution.py:287
  45.3 13.0 %collective-permute-start.3 = (bf16[256,512]{1,0:T(8,128)(2,1)S(1)}, bf16[256,512]{1,0:T(8,128)(2,1)S(1)}, u32[]{:S(2)}, u32[]{:S(2)}) collective-permute-start(bf16[256,512]{1,0:T(8,128)(2,1)S(1)} %get-tuple-element.15), channel_id=1, source_target_pairs={{0,8},{8,0},{1,9},{9,1},{2,10},{10,2},{3,11},{11,3},{4,12},{12,4},... | collective-permute-start | bytes 786440 | tf_op jit(solution)/shard_map/ppermute | solution.py:285
  48.2 10.2 %collective-permute-start.2 = (bf16[256,256]{1,0:T(8,128)(2,1)S(1)}, bf16[256,256]{1,0:T(8,128)(2,1)S(1)}, u32[]{:S(2)}, u32[]{:S(2)}) collective-permute-start(bf16[256,256]{1,0:T(8,128)(2,1)S(1)} %get-tuple-element.14), channel_id=1, source_target_pairs={{0,16},{16,0},{1,17},{17,1},{2,18},{18,2},{3,19},{19,3},{4,20},{20... | collective-permute-start | bytes 393224 | tf_op jit(solution)/shard_map/ppermute | solution.py:286
  51.7 6.6 %copy-start = (bf16[27,16,256]{2,1,0:T(8,128)(2,1)S(1)}, bf16[27,16,256]{2,1,0:T(8,128)(2,1)}, u32[]{:S(2)}) copy-start(bf16[27,16,256]{2,1,0:T(8,128)(2,1)} %filters.1) | copy-start | bytes 663556
  52.4 13.1 %all-to-all-start.2 = ((f16[4,56,256]{2,1,0:T(8,128)(2,1)}), f16[4,56,256]{2,1,0:T(8,128)(2,1)S(1)}, u32[]{:S(2)}, u32[]{:S(2)}) async-start(f16[4,56,256]{2,1,0:T(8,128)(2,1)} %broadcast_in_dim.4), calls=%async_computation.2 | async-start | bytes 229376 | tf_op jit(solution)/shard_map/all_to_all | solution.py:306
  59.1 15.2 %collective-permute-start.4 = (f32[32,1024]{1,0:T(8,128)S(1)}, f32[32,1024]{1,0:T(8,128)S(1)}, u32[]{:S(2)}, u32[]{:S(2)}) collective-permute-start(f32[32,1024]{1,0:T(8,128)S(1)} %get-tuple-element.17), channel_id=1, source_target_pairs={{16,32},{32,16},{48,64},{64,48},{80,96},{96,80},{112,128},{128,112... | collective-permute-start | bytes 393224 | tf_op jit(solution)/shard_map/ppermute | solution.py:296
  66.4 12.1 %all-to-all-start.3 = ((f16[8,56,256]{2,1,0:T(8,128)(2,1)}), f16[8,56,256]{2,1,0:T(8,128)(2,1)S(1)}, u32[]{:S(2)}, u32[]{:S(2)}) async-start(f16[8,56,256]{2,1,0:T(8,128)(2,1)} %broadcast_in_dim.5), calls=%async_computation.3 | async-start | bytes 458752 | tf_op jit(solution)/shard_map/all_to_all | solution.py:306
  72.3 3.2 %collective-permute-start.5 = (f32[32,1024]{1,0:T(8,128)S(1)}, f32[32,1024]{1,0:T(8,128)S(1)}, u32[]{:S(2)}, u32[]{:S(2)}) collective-permute-start(f32[32,1024]{1,0:T(8,128)S(1)} %get-tuple-element.18), channel_id=1, source_target_pairs={{0,16},{16,0},{1,17},{17,1},{2,18},{18,2},{3,19},{19,3},{4,20},{20... | collective-permute-start | bytes 393224 | tf_op jit(solution)/shard_map/ppermute | solution.py:310

commit v11 on v10

--- a/solution.py
+++ b/solution.py
@@ -131,7 +131,7 @@
     return blocks
 
 
-def grad_body(gathered, below, own, above, out, shifted):
+def shift_body(below, own, above, shifted):
     zero = jnp.zeros((OWN, 128), BF)
     for a, source in ((0, above), (1, own), (2, below)):
         for r in range(2):
@@ -149,6 +149,9 @@
                         shifted[16 * k : 16 * k + 16, lane : lane + 128] = (
                             rolled[at][c] if 0 <= at < 4 else zero
                         )
+
+
+def grad_body(gathered, shifted, out):
     total = lax.dot_general(
         shifted[...],
         gathered[:, 0:CELLS],
@@ -271,14 +274,16 @@
     below = lax.ppermute(own_cot, space, up)
     above = lax.ppermute(own_cot, space, down)
 
+    shifted = call(shift_body, [shape((ROWS, CELLS), BF)], [VMEM] * 3, moved=1 << 20)(
+        below, own_cot, above
+    )[0]
     own_grad = call(
         grad_body,
         [shape((8, PART + 2, 256), F32)],
-        [VMEM] * 4,
-        [pltpu.VMEM((ROWS, CELLS), BF)],
+        [VMEM] * 2,
         flops=2 * ROWS * CELLS * 256,
         moved=1 << 20,
-    )(gathered, below, own_cot, above)[0]
+    )(gathered, shifted)[0]
     half_cells, half_taps = call(
         parts_body, [shape((256, HALF_CELLS), BF), shape((256, 256), BF)], [VMEM, ANY], moved=1 << 19
     )(gathered, own_grad)

time: 80.1 us -> 80 us (level)
  transfers between devices with their start and end apart: 10 -> 10, of which waited for: 6 -> 6; matrix products, arithmetic and copies ran while one was open for 2% -> 2% of each run, Pallas kernels for 2% -> 3%
where the time goes in v11:
time: 80 us; the launch traced here: 79.3 us
  starting transfers between devices  46.6 us (58%)
  waiting for transfers between devices  24.1 us (30%)
  Pallas kernels  5.57 us (7%)
  local copies, waits for them, and re-layouts  1.38 us (2%)
  between operations  0.83 us (1%)
  other arithmetic  0.81 us (1%)
    all_to_all x1, waiting for transfers between devices, per_device(): gathered = lax.all_to_all(packed, chan, 0, 0).reshape(256, WIDE)  15.2 us
    all_to_all x1, starting transfers between devices, per_device(): gathered = lax.all_to_all(packed, chan, 0, 0).reshape(256, WIDE)  12 us
    all_to_all x2, starting transfers between devices, spread(): return lax.all_to_all(many, axes, 0, 0).astype(F32)  11.8 us
    all_to_all x1, starting transfers between devices, per_device(): lax.all_to_all(own_grad.astype(HALF), ('core', 'near'), 0, 0).astype(F32)  6.92 us
    all_to_all x2, waiting for transfers between devices, spread(): return lax.all_to_all(many, axes, 0, 0).astype(F32)  5.56 us
    ppermute x1, starting transfers between devices, per_device(): from_far = lax.ppermute(to_far, space, across)  3.03 us
    ppermute x1, starting transfers between devices, per_device(): below = lax.ppermute(own_cot, space, up)  3.02 us
    ppermute x1, starting transfers between devices, per_device(): above = lax.ppermute(own_cot, space, down)  2.86 us
  transfers between devices with their start and end apart: 10, of which 6 were waited for; matrix products, arithmetic and copies ran while one was open for 2% of the time, Pallas kernels for 3%

profile of v11, /device:TPU:1, one launch (start us, length us, event | category | flops | bytes accessed | tf_op | source)
XLA Modules:
  0.0 79.3 jit_solution(17101903747470447138)
XLA Ops:
  0.6 2.1 %shard_map.58 = (bf16[16,16,1792]{2,1,0:T(8,128)(2,1)}, bf16[16,1024]{1,0:T(8,128)(2,1)}) custom-call(s32[1]{0:T(128)} %bitcast.core_at.core, s32[1]{0:T(128)} %bitcast.1.side_at, bf16[16,2,4,128]{3,2,1,0:T(4,128)(2,1)} %field_far.1, bf16[16,2,4,128]{3,2,1,0:T(4,128)(2,1)} %cot_far.1, bf16[27,16,256]{2,1,0:T(8,128)(2,1)} %filters.1), custom_call_target="tpu_custom_call" | custom-call | bytes 1048576 | tf_op jit(solution)/shard_map/pallas_call | solution.py:255
  2.8 0.0 copy-start.1
  2.8 12.0 %all-to-all-start = ((bf16[16,16,1792]{2,1,0:T(8,128)(2,1)}), bf16[16,16,1792]{2,1,0:T(8,128)(2,1)S(1)}, u32[]{:S(2)}, u32[]{:S(2)}) async-start(bf16[16,16,1792]{2,1,0:T(8,128)(2,1)} %get-tuple-element.12), calls=%async_computation | async-start | bytes 1835008 | tf_op jit(solution)/shard_map/all_to_all | solution.py:273
  14.8 0.0 copy-done.1
  14.8 2.9 %collective-permute-start.1 = (bf16[16,1024]{1,0:T(8,128)(2,1)S(1)}, bf16[16,1024]{1,0:T(8,128)(2,1)S(1)}, u32[]{:S(2)}, u32[]{:S(2)}) collective-permute-start(bf16[16,1024]{1,0:T(8,128)(2,1)S(1)} %copy-done.1), channel_id=1, source_target_pairs={{16,0},{32,16},{48,32},{64,48},{80,64},{96,80},{112,96},{128,112},... | collective-permute-start | bytes 98312 | tf_op jit(solution)/shard_map/ppermute | solution.py:275
  17.7 3.0 %collective-permute-start = (bf16[16,1024]{1,0:T(8,128)(2,1)S(1)}, bf16[16,1024]{1,0:T(8,128)(2,1)S(1)}, u32[]{:S(2)}, u32[]{:S(2)}) collective-permute-start(bf16[16,1024]{1,0:T(8,128)(2,1)S(1)} %copy-done.1), channel_id=1, source_target_pairs={{0,16},{16,32},{32,48},{48,64},{64,80},{80,96},{96,112},{112,128},... | collective-permute-start | bytes 98312 | tf_op jit(solution)/shard_map/ppermute | solution.py:274
  20.7 0.0 collective-permute-done.1.above
  20.7 1.0 %collective-permute-done.below = bf16[16,1024]{1,0:T(8,128)(2,1)S(1)} collective-permute-done((bf16[16,1024]{1,0:T(8,128)(2,1)S(1)}, bf16[16,1024]{1,0:T(8,128)(2,1)S(1)}, u32[]{:S(2)}, u32[]{:S(2)}) %collective-permute-start) | collective-permute-done | bytes 32800 | tf_op jit(solution)/shard_map/ppermute | solution.py:274
  21.7 0.1 shard_map.59.shifted
  21.8 15.2 %all-to-all-done = bf16[16,16,1792]{2,1,0:T(8,128)(2,1)S(1)} async-done(((bf16[16,16,1792]{2,1,0:T(8,128)(2,1)}), bf16[16,16,1792]{2,1,0:T(8,128)(2,1)S(1)}, u32[]{:S(2)}, u32[]{:S(2)}) %all-to-all-start) | async-done | bytes 917536 | tf_op jit(solution)/shard_map/all_to_all | solution.py:273
  37.0 0.6 shard_map.60._after
  37.6 0.7 convert_element_type.18
  38.3 6.9 %all-to-all-start.1 = ((f16[8,56,256]{2,1,0:T(8,128)(2,1)}), f16[8,56,256]{2,1,0:T(8,128)(2,1)S(1)}, u32[]{:S(2)}, u32[]{:S(2)}) async-start(f16[8,56,256]{2,1,0:T(8,128)(2,1)} %convert_element_type.18), calls=%async_computation.1 | async-start | bytes 458752 | tf_op jit(solution)/shard_map/all_to_all | solution.py:292
  45.3 2.8 %collective-permute-start.3 = (bf16[256,512]{1,0:T(8,128)(2,1)S(1)}, bf16[256,512]{1,0:T(8,128)(2,1)S(1)}, u32[]{:S(2)}, u32[]{:S(2)}) collective-permute-start(bf16[256,512]{1,0:T(8,128)(2,1)S(1)} %get-tuple-element.15), channel_id=1, source_target_pairs={{0,8},{8,0},{1,9},{9,1},{2,10},{10,2},{3,11},{11,3},{4,12},{12,4},... | collective-permute-start | bytes 786440 | tf_op jit(solution)/shard_map/ppermute | solution.py:290
  48.1 2.2 %collective-permute-start.2 = (bf16[256,256]{1,0:T(8,128)(2,1)S(1)}, bf16[256,256]{1,0:T(8,128)(2,1)S(1)}, u32[]{:S(2)}, u32[]{:S(2)}) collective-permute-start(bf16[256,256]{1,0:T(8,128)(2,1)S(1)} %get-tuple-element.14), channel_id=1, source_target_pairs={{0,16},{16,0},{1,17},{17,1},{2,18},{18,2},{3,19},{19,3},{4,20},{20... | collective-permute-start | bytes 393224 | tf_op jit(solution)/shard_map/ppermute | solution.py:291
  50.3 1.1 %all-to-all-done.1 = f16[8,56,256]{2,1,0:T(8,128)(2,1)S(1)} async-done(((f16[8,56,256]{2,1,0:T(8,128)(2,1)}), f16[8,56,256]{2,1,0:T(8,128)(2,1)S(1)}, u32[]{:S(2)}, u32[]{:S(2)}) %all-to-all-start.1) | async-done | bytes 229408 | tf_op jit(solution)/shard_map/all_to_all | solution.py:292
  51.5 0.2 shard_map.65
  51.7 0.0 copy-start
  51.7 0.7 broadcast_in_dim.4
  52.4 5.9 %all-to-all-start.2 = ((f16[4,56,256]{2,1,0:T(8,128)(2,1)}), f16[4,56,256]{2,1,0:T(8,128)(2,1)S(1)}, u32[]{:S(2)}, u32[]{:S(2)}) async-start(f16[4,56,256]{2,1,0:T(8,128)(2,1)} %broadcast_in_dim.4), calls=%async_computation.2 | async-start | bytes 229376 | tf_op jit(solution)/shard_map/all_to_all | solution.py:311
  58.3 0.0 collective-permute-done.2.swapped
  58.3 0.0 collective-permute-done.3.halves
  58.3 0.0 copy-done
  58.3 0.7 shard_map.62
  59.0 3.0 %collective-permute-start.4 = (f32[32,1024]{1,0:T(8,128)S(1)}, f32[32,1024]{1,0:T(8,128)S(1)}, u32[]{:S(2)}, u32[]{:S(2)}) collective-permute-start(f32[32,1024]{1,0:T(8,128)S(1)} %get-tuple-element.17), channel_id=1, source_target_pairs={{16,32},{32,16},{48,64},{64,48},{80,96},{96,80},{112,128},{128,112... | collective-permute-start | bytes 393224 | tf_op jit(solution)/shard_map/ppermute | solution.py:301
  62.1 3.4 %all-to-all-done.2 = f16[4,56,256]{2,1,0:T(8,128)(2,1)S(1)} async-done(((f16[4,56,256]{2,1,0:T(8,128)(2,1)}), f16[4,56,256]{2,1,0:T(8,128)(2,1)S(1)}, u32[]{:S(2)}, u32[]{:S(2)}) %all-to-all-start.2) | async-done | bytes 114720 | tf_op jit(solution)/shard_map/all_to_all | solution.py:311
  65.5 0.2 shard_map.66
  65.7 0.7 broadcast_in_dim.5
  66.4 5.9 %all-to-all-start.3 = ((f16[8,56,256]{2,1,0:T(8,128)(2,1)}), f16[8,56,256]{2,1,0:T(8,128)(2,1)S(1)}, u32[]{:S(2)}, u32[]{:S(2)}) async-start(f16[8,56,256]{2,1,0:T(8,128)(2,1)} %broadcast_in_dim.5), calls=%async_computation.3 | async-start | bytes 458752 | tf_op jit(solution)/shard_map/all_to_all | solution.py:311
  72.3 2.0 %collective-permute-start.5 = (f32[32,1024]{1,0:T(8,128)S(1)}, f32[32,1024]{1,0:T(8,128)S(1)}, u32[]{:S(2)}, u32[]{:S(2)}) collective-permute-start(f32[32,1024]{1,0:T(8,128)S(1)} %get-tuple-element.18), channel_id=1, source_target_pairs={{0,16},{16,0},{1,17},{17,1},{2,18},{18,2},{3,19},{19,3},{4,20},{20... | collective-permute-start | bytes 393224 | tf_op jit(solution)/shard_map/ppermute | solution.py:315
  74.3 0.0 collective-permute-done.4.far
  74.3 1.2 %collective-permute-done.5.near = f32[32,1024]{1,0:T(8,128)S(1)} collective-permute-done((f32[32,1024]{1,0:T(8,128)S(1)}, f32[32,1024]{1,0:T(8,128)S(1)}, u32[]{:S(2)}, u32[]{:S(2)}) %collective-permute-start.5) | collective-permute-done | bytes 131104 | tf_op jit(solution)/shard_map/ppermute | solution.py:315
  75.5 0.8 %shard_map.64 = (bf16[16,2,4,128]{3,2,1,0:T(4,128)(2,1)}, bf16[16,2,4,128]{3,2,1,0:T(4,128)(2,1)}) custom-call(f32[32,1024]{1,0:T(8,128)S(1)} %shard_map.63.own, f32[32,1024]{1,0:T(8,128)S(1)} %collective-permute-done.5.near), custom_call_target="tpu_custom_call" | custom-call | bytes 262144 | tf_op jit(solution)/shard_map/pallas_call | solution.py:328
  76.3 2.2 %all-to-all-done.3 = f16[8,56,256]{2,1,0:T(8,128)(2,1)S(1)} async-done(((f16[8,56,256]{2,1,0:T(8,128)(2,1)}), f16[8,56,256]{2,1,0:T(8,128)(2,1)S(1)}, u32[]{:S(2)}, u32[]{:S(2)}) %all-to-all-start.3) | async-done | bytes 229408 | tf_op jit(solution)/shard_map/all_to_all | solution.py:311
  78.5 0.8 %shard_map.67 = f32[432,256]{1,0:T(8,128)} custom-call(f32[8,56,256]{2,1,0:T(8,128)S(1)} %convert_element_type.23.full), custom_call_target="tpu_custom_call" | custom-call | bytes 1048576 | tf_op jit(solution)/shard_map/pallas_call | solution.py:317
  (7 shorter events, 0.1 us)
Async XLA Ops:
  2.8 12.0 %copy-start.1 = (bf16[16,1024]{1,0:T(8,128)(2,1)S(1)}, bf16[16,1024]{1,0:T(8,128)(2,1)}, u32[]{:S(2)}) copy-start(bf16[16,1024]{1,0:T(8,128)(2,1)} %get-tuple-element.13.own) | copy-start | bytes 98308
  2.8 34.2 %all-to-all-start = ((bf16[16,16,1792]{2,1,0:T(8,128)(2,1)}), bf16[16,16,1792]{2,1,0:T(8,128)(2,1)S(1)}, u32[]{:S(2)}, u32[]{:S(2)}) async-start(bf16[16,16,1792]{2,1,0:T(8,128)(2,1)} %get-tuple-element.12), calls=%async_computation | async-start | bytes 1835008 | tf_op jit(solution)/shard_map/all_to_all | solution.py:273
  14.8 5.9 %collective-permute-start.1 = (bf16[16,1024]{1,0:T(8,128)(2,1)S(1)}, bf16[16,1024]{1,0:T(8,128)(2,1)S(1)}, u32[]{:S(2)}, u32[]{:S(2)}) collective-permute-start(bf16[16,1024]{1,0:T(8,128)(2,1)S(1)} %copy-done.1), channel_id=1, source_target_pairs={{16,0},{32,16},{48,32},{64,48},{80,64},{96,80},{112,96},{128,112},... | collective-permute-start | bytes 98312 | tf_op jit(solution)/shard_map/ppermute | solution.py:275
  17.7 4.0 %collective-permute-start = (bf16[16,1024]{1,0:T(8,128)(2,1)S(1)}, bf16[16,1024]{1,0:T(8,128)(2,1)S(1)}, u32[]{:S(2)}, u32[]{:S(2)}) collective-permute-start(bf16[16,1024]{1,0:T(8,128)(2,1)S(1)} %copy-done.1), channel_id=1, source_target_pairs={{0,16},{16,32},{32,48},{48,64},{64,80},{80,96},{96,112},{112,128},... | collective-permute-start | bytes 98312 | tf_op jit(solution)/shard_map/ppermute | solution.py:274
  38.3 13.1 %all-to-all-start.1 = ((f16[8,56,256]{2,1,0:T(8,128)(2,1)}), f16[8,56,256]{2,1,0:T(8,128)(2,1)S(1)}, u32[]{:S(2)}, u32[]{:S(2)}) async-start(f16[8,56,256]{2,1,0:T(8,128)(2,1)} %convert_element_type.18), calls=%async_computation.1 | async-start | bytes 458752 | tf_op jit(solution)/shard_map/all_to_all | solution.py:292
  45.3 13.0 %collective-permute-start.3 = (bf16[256,512]{1,0:T(8,128)(2,1)S(1)}, bf16[256,512]{1,0:T(8,128)(2,1)S(1)}, u32[]{:S(2)}, u32[]{:S(2)}) collective-permute-start(bf16[256,512]{1,0:T(8,128)(2,1)S(1)} %get-tuple-element.15), channel_id=1, source_target_pairs={{0,8},{8,0},{1,9},{9,1},{2,10},{10,2},{3,11},{11,3},{4,12},{12,4},... | collective-permute-start | bytes 786440 | tf_op jit(solution)/shard_map/ppermute | solution.py:290
  48.1 10.2 %collective-permute-start.2 = (bf16[256,256]{1,0:T(8,128)(2,1)S(1)}, bf16[256,256]{1,0:T(8,128)(2,1)S(1)}, u32[]{:S(2)}, u32[]{:S(2)}) collective-permute-start(bf16[256,256]{1,0:T(8,128)(2,1)S(1)} %get-tuple-element.14), channel_id=1, source_target_pairs={{0,16},{16,0},{1,17},{17,1},{2,18},{18,2},{3,19},{19,3},{4,20},{20... | collective-permute-start | bytes 393224 | tf_op jit(solution)/shard_map/ppermute | solution.py:291
  51.7 6.6 %copy-start = (bf16[27,16,256]{2,1,0:T(8,128)(2,1)S(1)}, bf16[27,16,256]{2,1,0:T(8,128)(2,1)}, u32[]{:S(2)}) copy-start(bf16[27,16,256]{2,1,0:T(8,128)(2,1)} %filters.1) | copy-start | bytes 663556
  52.4 13.1 %all-to-all-start.2 = ((f16[4,56,256]{2,1,0:T(8,128)(2,1)}), f16[4,56,256]{2,1,0:T(8,128)(2,1)S(1)}, u32[]{:S(2)}, u32[]{:S(2)}) async-start(f16[4,56,256]{2,1,0:T(8,128)(2,1)} %broadcast_in_dim.4), calls=%async_computation.2 | async-start | bytes 229376 | tf_op jit(solution)/shard_map/all_to_all | solution.py:311
  59.0 15.2 %collective-permute-start.4 = (f32[32,1024]{1,0:T(8,128)S(1)}, f32[32,1024]{1,0:T(8,128)S(1)}, u32[]{:S(2)}, u32[]{:S(2)}) collective-permute-start(f32[32,1024]{1,0:T(8,128)S(1)} %get-tuple-element.17), channel_id=1, source_target_pairs={{16,32},{32,16},{48,64},{64,48},{80,96},{96,80},{112,128},{128,112... | collective-permute-start | bytes 393224 | tf_op jit(solution)/shard_map/ppermute | solution.py:301
  66.4 12.1 %all-to-all-start.3 = ((f16[8,56,256]{2,1,0:T(8,128)(2,1)}), f16[8,56,256]{2,1,0:T(8,128)(2,1)S(1)}, u32[]{:S(2)}, u32[]{:S(2)}) async-start(f16[8,56,256]{2,1,0:T(8,128)(2,1)} %broadcast_in_dim.5), calls=%async_computation.3 | async-start | bytes 458752 | tf_op jit(solution)/shard_map/all_to_all | solution.py:311
  72.3 3.2 %collective-permute-start.5 = (f32[32,1024]{1,0:T(8,128)S(1)}, f32[32,1024]{1,0:T(8,128)S(1)}, u32[]{:S(2)}, u32[]{:S(2)}) collective-permute-start(f32[32,1024]{1,0:T(8,128)S(1)} %get-tuple-element.18), channel_id=1, source_target_pairs={{0,16},{16,0},{1,17},{17,1},{2,18},{18,2},{3,19},{19,3},{4,20},{20... | collective-permute-start | bytes 393224 | tf_op jit(solution)/shard_map/ppermute | solution.py:315

commit v12 on v11

--- a/solution.py
+++ b/solution.py
@@ -181,8 +181,9 @@
     for n in range(peers):
         total = total + parts[n, 0:PART, :] * jnp.exp2(parts[n, PART : PART + 1, :] - 14.0)
     power, scaled = scaled_down(total * factor)
-    out[0:PART, :] = scaled
-    out[PART : PART + 2, :] = jnp.broadcast_to(power, (2, 256))
+    for n in range(out.shape[0]):
+        out[n, 0:PART, :] = scaled
+        out[n, PART : PART + 2, :] = jnp.broadcast_to(power, (2, 256))
 
 
 def finish_body(full, out_far, out, sent):
@@ -300,20 +301,18 @@
     )(core, side, gathered, filters, swapped, halves)
     from_far = lax.ppermute(to_far, space, across)
 
-    def summed(factor, peers, flops, parts, *after):
+    def summed(factor, peers, following, flops, parts, *after):
         body = functools.partial(sum_body, factor, peers)
-        return call(body, [shape((PART + 2, 256), F32)], [VMEM] + [ANY] * len(after), flops=flops)(
-            parts, *after
-        )[0]
-
-    def spread(part, peers, axes):
-        many = jnp.broadcast_to(part.astype(HALF)[None], (peers,) + part.shape)
-        return lax.all_to_all(many, axes, 0, 0).astype(F32)
-
-    row = summed(1.0, 8, ROW_FLOPS, parts)
-    mine = summed(SCALE, 4, 0, spread(row, 4, "far"), own_sums)
+        outs = [shape((following, PART + 2, 256), F32)]
+        return call(body, outs, [VMEM] + [ANY] * len(after), flops=flops)(parts, *after)[0]
+
+    def spread(many, axes):
+        return lax.all_to_all(many.astype(HALF), axes, 0, 0).astype(F32)
+
+    row = summed(1.0, 8, 4, ROW_FLOPS, parts)
+    mine = summed(SCALE, 4, 8, 0, spread(row, "far"), own_sums)
     from_near = lax.ppermute(to_near, "core", swap)
-    full = spread(mine, 8, ("core", "near"))
+    full = spread(mine, ("core", "near"))
     weight_grad = call(
         finish_body,
         [shape((ROWS, 256), F32)],

time: 80 us -> 80.1 us (level)
  local copies, waits for them, and re-layouts: 1.38 us -> 0.01 us
  other arithmetic: 0.81 us -> 2.17 us
    broadcast_in_dim x2 -> x0, local copies, waits for them, and re-layouts: 1.37 us -> none  [spread(): many = jnp.broadcast_to(part.astype(HALF)[None], (peers,) + part.shape)]
    convert_element_type x4, other arithmetic: 0.06 us -> 1.43 us  [spread(): return lax.all_to_all(many.astype(HALF), axes, 0, 0).astype(F32)]
where the time goes in v12:
time: 80.1 us; the launch traced here: 79.4 us
  starting transfers between devices  46.6 us (58%)
  waiting for transfers between devices  24.1 us (30%)
  Pallas kernels  5.62 us (7%)
  other arithmetic  2.17 us (3%)
  between operations  0.81 us (1%)
    all_to_all x1, waiting for transfers between devices, per_device(): gathered = lax.all_to_all(packed, chan, 0, 0).reshape(256, WIDE)  15.2 us
    all_to_all x1, starting transfers between devices, per_device(): gathered = lax.all_to_all(packed, chan, 0, 0).reshape(256, WIDE)  12 us
    all_to_all x2, starting transfers between devices, spread(): return lax.all_to_all(many.astype(HALF), axes, 0, 0).astype(F32)  11.8 us
    all_to_all x1, starting transfers between devices, per_device(): lax.all_to_all(own_grad.astype(HALF), ('core', 'near'), 0, 0).astype(F32)  6.92 us
    all_to_all x2, waiting for transfers between devices, spread(): return lax.all_to_all(many.astype(HALF), axes, 0, 0).astype(F32)  5.56 us
    ppermute x1, starting transfers between devices, per_device(): from_far = lax.ppermute(to_far, space, across)  3.03 us
    ppermute x1, starting transfers between devices, per_device(): below = lax.ppermute(own_cot, space, up)  3.02 us
    ppermute x1, starting transfers between devices, per_device(): above = lax.ppermute(own_cot, space, down)  2.86 us
  transfers between devices with their start and end apart: 10, of which 6 were waited for; matrix products, arithmetic and copies ran while one was open for 2% of the time, Pallas kernels for 3%

profile of v12, /device:TPU:1, one launch (start us, length us, event | category | flops | bytes accessed | tf_op | source)
XLA Modules:
  0.0 79.4 jit_solution(10975546238840242561)
XLA Ops:
  0.6 2.1 %shard_map.58 = (bf16[16,16,1792]{2,1,0:T(8,128)(2,1)}, bf16[16,1024]{1,0:T(8,128)(2,1)}) custom-call(s32[1]{0:T(128)} %bitcast.core_at.core, s32[1]{0:T(128)} %bitcast.1.side_at, bf16[16,2,4,128]{3,2,1,0:T(4,128)(2,1)} %field_far.1, bf16[16,2,4,128]{3,2,1,0:T(4,128)(2,1)} %cot_far.1, bf16[27,16,256]{2,1,0:T(8,128)(2,1)} %filters.1), custom_call_target="tpu_custom_call" | custom-call | bytes 1048576 | tf_op jit(solution)/shard_map/pallas_call | solution.py:256
  2.8 0.0 copy-start.1
  2.8 12.0 %all-to-all-start = ((bf16[16,16,1792]{2,1,0:T(8,128)(2,1)}), bf16[16,16,1792]{2,1,0:T(8,128)(2,1)S(1)}, u32[]{:S(2)}, u32[]{:S(2)}) async-start(bf16[16,16,1792]{2,1,0:T(8,128)(2,1)} %get-tuple-element.12), calls=%async_computation | async-start | bytes 1835008 | tf_op jit(solution)/shard_map/all_to_all | solution.py:274
  14.8 0.0 copy-done.1
  14.8 2.9 %collective-permute-start.1 = (bf16[16,1024]{1,0:T(8,128)(2,1)S(1)}, bf16[16,1024]{1,0:T(8,128)(2,1)S(1)}, u32[]{:S(2)}, u32[]{:S(2)}) collective-permute-start(bf16[16,1024]{1,0:T(8,128)(2,1)S(1)} %copy-done.1), channel_id=1, source_target_pairs={{16,0},{32,16},{48,32},{64,48},{80,64},{96,80},{112,96},{128,112},... | collective-permute-start | bytes 98312 | tf_op jit(solution)/shard_map/ppermute | solution.py:276
  17.7 3.0 %collective-permute-start = (bf16[16,1024]{1,0:T(8,128)(2,1)S(1)}, bf16[16,1024]{1,0:T(8,128)(2,1)S(1)}, u32[]{:S(2)}, u32[]{:S(2)}) collective-permute-start(bf16[16,1024]{1,0:T(8,128)(2,1)S(1)} %copy-done.1), channel_id=1, source_target_pairs={{0,16},{16,32},{32,48},{48,64},{64,80},{80,96},{96,112},{112,128},... | collective-permute-start | bytes 98312 | tf_op jit(solution)/shard_map/ppermute | solution.py:275
  20.7 0.0 collective-permute-done.1.above
  20.7 1.0 %collective-permute-done.below = bf16[16,1024]{1,0:T(8,128)(2,1)S(1)} collective-permute-done((bf16[16,1024]{1,0:T(8,128)(2,1)S(1)}, bf16[16,1024]{1,0:T(8,128)(2,1)S(1)}, u32[]{:S(2)}, u32[]{:S(2)}) %collective-permute-start) | collective-permute-done | bytes 32800 | tf_op jit(solution)/shard_map/ppermute | solution.py:275
  21.7 0.1 shard_map.59.shifted
  21.8 15.2 %all-to-all-done = bf16[16,16,1792]{2,1,0:T(8,128)(2,1)S(1)} async-done(((bf16[16,16,1792]{2,1,0:T(8,128)(2,1)}), bf16[16,16,1792]{2,1,0:T(8,128)(2,1)S(1)}, u32[]{:S(2)}, u32[]{:S(2)}) %all-to-all-start) | async-done | bytes 917536 | tf_op jit(solution)/shard_map/all_to_all | solution.py:274
  37.0 0.6 shard_map.60._after
  37.6 0.7 convert_element_type.18
  38.3 6.9 %all-to-all-start.1 = ((f16[8,56,256]{2,1,0:T(8,128)(2,1)}), f16[8,56,256]{2,1,0:T(8,128)(2,1)S(1)}, u32[]{:S(2)}, u32[]{:S(2)}) async-start(f16[8,56,256]{2,1,0:T(8,128)(2,1)} %convert_element_type.18), calls=%async_computation.1 | async-start | bytes 458752 | tf_op jit(solution)/shard_map/all_to_all | solution.py:293
  45.3 2.8 %collective-permute-start.3 = (bf16[256,512]{1,0:T(8,128)(2,1)S(1)}, bf16[256,512]{1,0:T(8,128)(2,1)S(1)}, u32[]{:S(2)}, u32[]{:S(2)}) collective-permute-start(bf16[256,512]{1,0:T(8,128)(2,1)S(1)} %get-tuple-element.15), channel_id=1, source_target_pairs={{0,8},{8,0},{1,9},{9,1},{2,10},{10,2},{3,11},{11,3},{4,12},{12,4},... | collective-permute-start | bytes 786440 | tf_op jit(solution)/shard_map/ppermute | solution.py:291
  48.1 2.2 %collective-permute-start.2 = (bf16[256,256]{1,0:T(8,128)(2,1)S(1)}, bf16[256,256]{1,0:T(8,128)(2,1)S(1)}, u32[]{:S(2)}, u32[]{:S(2)}) collective-permute-start(bf16[256,256]{1,0:T(8,128)(2,1)S(1)} %get-tuple-element.14), channel_id=1, source_target_pairs={{0,16},{16,0},{1,17},{17,1},{2,18},{18,2},{3,19},{19,3},{4,20},{20... | collective-permute-start | bytes 393224 | tf_op jit(solution)/shard_map/ppermute | solution.py:292
  50.3 1.1 %all-to-all-done.1 = f16[8,56,256]{2,1,0:T(8,128)(2,1)S(1)} async-done(((f16[8,56,256]{2,1,0:T(8,128)(2,1)}), f16[8,56,256]{2,1,0:T(8,128)(2,1)S(1)}, u32[]{:S(2)}, u32[]{:S(2)}) %all-to-all-start.1) | async-done | bytes 229408 | tf_op jit(solution)/shard_map/all_to_all | solution.py:293
  51.5 0.2 shard_map.65
  51.7 0.0 copy-start
  51.7 0.7 convert_element_type.20
  52.4 5.9 %all-to-all-start.2 = ((f16[4,56,256]{2,1,0:T(8,128)(2,1)}), f16[4,56,256]{2,1,0:T(8,128)(2,1)S(1)}, u32[]{:S(2)}, u32[]{:S(2)}) async-start(f16[4,56,256]{2,1,0:T(8,128)(2,1)} %convert_element_type.20), calls=%async_computation.2 | async-start | bytes 229376 | tf_op jit(solution)/shard_map/all_to_all | solution.py:310
  58.3 0.0 collective-permute-done.2.swapped
  58.3 0.0 collective-permute-done.3.halves
  58.3 0.0 copy-done
  58.3 0.7 shard_map.62
  59.1 3.0 %collective-permute-start.4 = (f32[32,1024]{1,0:T(8,128)S(1)}, f32[32,1024]{1,0:T(8,128)S(1)}, u32[]{:S(2)}, u32[]{:S(2)}) collective-permute-start(f32[32,1024]{1,0:T(8,128)S(1)} %get-tuple-element.17), channel_id=1, source_target_pairs={{16,32},{32,16},{48,64},{64,48},{80,96},{96,80},{112,128},{128,112... | collective-permute-start | bytes 393224 | tf_op jit(solution)/shard_map/ppermute | solution.py:302
  62.1 3.4 %all-to-all-done.2 = f16[4,56,256]{2,1,0:T(8,128)(2,1)S(1)} async-done(((f16[4,56,256]{2,1,0:T(8,128)(2,1)}), f16[4,56,256]{2,1,0:T(8,128)(2,1)S(1)}, u32[]{:S(2)}, u32[]{:S(2)}) %all-to-all-start.2) | async-done | bytes 114720 | tf_op jit(solution)/shard_map/all_to_all | solution.py:310
  65.5 0.2 shard_map.66
  65.7 0.7 convert_element_type.22
  66.4 5.9 %all-to-all-start.3 = ((f16[8,56,256]{2,1,0:T(8,128)(2,1)}), f16[8,56,256]{2,1,0:T(8,128)(2,1)S(1)}, u32[]{:S(2)}, u32[]{:S(2)}) async-start(f16[8,56,256]{2,1,0:T(8,128)(2,1)} %convert_element_type.22), calls=%async_computation.3 | async-start | bytes 458752 | tf_op jit(solution)/shard_map/all_to_all | solution.py:310
  72.3 2.0 %collective-permute-start.5 = (f32[32,1024]{1,0:T(8,128)S(1)}, f32[32,1024]{1,0:T(8,128)S(1)}, u32[]{:S(2)}, u32[]{:S(2)}) collective-permute-start(f32[32,1024]{1,0:T(8,128)S(1)} %get-tuple-element.18), channel_id=1, source_target_pairs={{0,16},{16,0},{1,17},{17,1},{2,18},{18,2},{3,19},{19,3},{4,20},{20... | collective-permute-start | bytes 393224 | tf_op jit(solution)/shard_map/ppermute | solution.py:314
  74.3 0.0 collective-permute-done.4.far
  74.4 1.2 %collective-permute-done.5.near = f32[32,1024]{1,0:T(8,128)S(1)} collective-permute-done((f32[32,1024]{1,0:T(8,128)S(1)}, f32[32,1024]{1,0:T(8,128)S(1)}, u32[]{:S(2)}, u32[]{:S(2)}) %collective-permute-start.5) | collective-permute-done | bytes 131104 | tf_op jit(solution)/shard_map/ppermute | solution.py:314
  75.5 0.8 %shard_map.64 = (bf16[16,2,4,128]{3,2,1,0:T(4,128)(2,1)}, bf16[16,2,4,128]{3,2,1,0:T(4,128)(2,1)}) custom-call(f32[32,1024]{1,0:T(8,128)S(1)} %shard_map.63.own, f32[32,1024]{1,0:T(8,128)S(1)} %collective-permute-done.5.near), custom_call_target="tpu_custom_call" | custom-call | bytes 262144 | tf_op jit(solution)/shard_map/pallas_call | solution.py:327
  76.4 2.2 %all-to-all-done.3 = f16[8,56,256]{2,1,0:T(8,128)(2,1)S(1)} async-done(((f16[8,56,256]{2,1,0:T(8,128)(2,1)}), f16[8,56,256]{2,1,0:T(8,128)(2,1)S(1)}, u32[]{:S(2)}, u32[]{:S(2)}) %all-to-all-start.3) | async-done | bytes 229408 | tf_op jit(solution)/shard_map/all_to_all | solution.py:310
  78.6 0.8 %shard_map.67 = f32[432,256]{1,0:T(8,128)} custom-call(f32[8,56,256]{2,1,0:T(8,128)S(1)} %convert_element_type.23.full), custom_call_target="tpu_custom_call" | custom-call | bytes 1048576 | tf_op jit(solution)/shard_map/pallas_call | solution.py:316
  (5 shorter events, 0.1 us)
Async XLA Ops:
  2.8 12.0 %copy-start.1 = (bf16[16,1024]{1,0:T(8,128)(2,1)S(1)}, bf16[16,1024]{1,0:T(8,128)(2,1)}, u32[]{:S(2)}) copy-start(bf16[16,1024]{1,0:T(8,128)(2,1)} %get-tuple-element.13.own) | copy-start | bytes 98308
  2.8 34.2 %all-to-all-start = ((bf16[16,16,1792]{2,1,0:T(8,128)(2,1)}), bf16[16,16,1792]{2,1,0:T(8,128)(2,1)S(1)}, u32[]{:S(2)}, u32[]{:S(2)}) async-start(bf16[16,16,1792]{2,1,0:T(8,128)(2,1)} %get-tuple-element.12), calls=%async_computation | async-start | bytes 1835008 | tf_op jit(solution)/shard_map/all_to_all | solution.py:274
  14.8 5.9 %collective-permute-start.1 = (bf16[16,1024]{1,0:T(8,128)(2,1)S(1)}, bf16[16,1024]{1,0:T(8,128)(2,1)S(1)}, u32[]{:S(2)}, u32[]{:S(2)}) collective-permute-start(bf16[16,1024]{1,0:T(8,128)(2,1)S(1)} %copy-done.1), channel_id=1, source_target_pairs={{16,0},{32,16},{48,32},{64,48},{80,64},{96,80},{112,96},{128,112},... | collective-permute-start | bytes 98312 | tf_op jit(solution)/shard_map/ppermute | solution.py:276
  17.7 4.0 %collective-permute-start = (bf16[16,1024]{1,0:T(8,128)(2,1)S(1)}, bf16[16,1024]{1,0:T(8,128)(2,1)S(1)}, u32[]{:S(2)}, u32[]{:S(2)}) collective-permute-start(bf16[16,1024]{1,0:T(8,128)(2,1)S(1)} %copy-done.1), channel_id=1, source_target_pairs={{0,16},{16,32},{32,48},{48,64},{64,80},{80,96},{96,112},{112,128},... | collective-permute-start | bytes 98312 | tf_op jit(solution)/shard_map/ppermute | solution.py:275
  38.3 13.1 %all-to-all-start.1 = ((f16[8,56,256]{2,1,0:T(8,128)(2,1)}), f16[8,56,256]{2,1,0:T(8,128)(2,1)S(1)}, u32[]{:S(2)}, u32[]{:S(2)}) async-start(f16[8,56,256]{2,1,0:T(8,128)(2,1)} %convert_element_type.18), calls=%async_computation.1 | async-start | bytes 458752 | tf_op jit(solution)/shard_map/all_to_all | solution.py:293
  45.3 13.0 %collective-permute-start.3 = (bf16[256,512]{1,0:T(8,128)(2,1)S(1)}, bf16[256,512]{1,0:T(8,128)(2,1)S(1)}, u32[]{:S(2)}, u32[]{:S(2)}) collective-permute-start(bf16[256,512]{1,0:T(8,128)(2,1)S(1)} %get-tuple-element.15), channel_id=1, source_target_pairs={{0,8},{8,0},{1,9},{9,1},{2,10},{10,2},{3,11},{11,3},{4,12},{12,4},... | collective-permute-start | bytes 786440 | tf_op jit(solution)/shard_map/ppermute | solution.py:291
  48.1 10.2 %collective-permute-start.2 = (bf16[256,256]{1,0:T(8,128)(2,1)S(1)}, bf16[256,256]{1,0:T(8,128)(2,1)S(1)}, u32[]{:S(2)}, u32[]{:S(2)}) collective-permute-start(bf16[256,256]{1,0:T(8,128)(2,1)S(1)} %get-tuple-element.14), channel_id=1, source_target_pairs={{0,16},{16,0},{1,17},{17,1},{2,18},{18,2},{3,19},{19,3},{4,20},{20... | collective-permute-start | bytes 393224 | tf_op jit(solution)/shard_map/ppermute | solution.py:292
  51.7 6.6 %copy-start = (bf16[27,16,256]{2,1,0:T(8,128)(2,1)S(1)}, bf16[27,16,256]{2,1,0:T(8,128)(2,1)}, u32[]{:S(2)}) copy-start(bf16[27,16,256]{2,1,0:T(8,128)(2,1)} %filters.1) | copy-start | bytes 663556
  52.4 13.1 %all-to-all-start.2 = ((f16[4,56,256]{2,1,0:T(8,128)(2,1)}), f16[4,56,256]{2,1,0:T(8,128)(2,1)S(1)}, u32[]{:S(2)}, u32[]{:S(2)}) async-start(f16[4,56,256]{2,1,0:T(8,128)(2,1)} %convert_element_type.20), calls=%async_computation.2 | async-start | bytes 229376 | tf_op jit(solution)/shard_map/all_to_all | solution.py:310
  59.1 15.3 %collective-permute-start.4 = (f32[32,1024]{1,0:T(8,128)S(1)}, f32[32,1024]{1,0:T(8,128)S(1)}, u32[]{:S(2)}, u32[]{:S(2)}) collective-permute-start(f32[32,1024]{1,0:T(8,128)S(1)} %get-tuple-element.17), channel_id=1, source_target_pairs={{16,32},{32,16},{48,64},{64,48},{80,96},{96,80},{112,128},{128,112... | collective-permute-start | bytes 393224 | tf_op jit(solution)/shard_map/ppermute | solution.py:302
  66.4 12.1 %all-to-all-start.3 = ((f16[8,56,256]{2,1,0:T(8,128)(2,1)}), f16[8,56,256]{2,1,0:T(8,128)(2,1)S(1)}, u32[]{:S(2)}, u32[]{:S(2)}) async-start(f16[8,56,256]{2,1,0:T(8,128)(2,1)} %convert_element_type.22), calls=%async_computation.3 | async-start | bytes 458752 | tf_op jit(solution)/shard_map/all_to_all | solution.py:310
  72.3 3.2 %collective-permute-start.5 = (f32[32,1024]{1,0:T(8,128)S(1)}, f32[32,1024]{1,0:T(8,128)S(1)}, u32[]{:S(2)}, u32[]{:S(2)}) collective-permute-start(f32[32,1024]{1,0:T(8,128)S(1)} %get-tuple-element.18), channel_id=1, source_target_pairs={{0,16},{16,0},{1,17},{17,1},{2,18},{18,2},{3,19},{19,3},{4,20},{20... | collective-permute-start | bytes 393224 | tf_op jit(solution)/shard_map/ppermute | solution.py:314

commit v13 on v11

--- a/solution.py
+++ b/solution.py
@@ -102,12 +102,12 @@
                     turned = block if step == 0 else pltpu.roll(block, step, 1)
                     parts[8 * h + q] = jnp.where(here, turned, parts[8 * h + q])
         for c in range(16):
-            taps[c, :, 128 * g : 128 * g + 128] = parts[c].astype(BF)
-    last = pltpu.make_async_copy(taps, out.at[:, :, pl.ds(TAPS_AT, 256)], sent.at[16])
-    last.start()
+            taps[g, c] = parts[c].astype(BF)
+        there = out.at[:, :, pl.ds(TAPS_AT + 128 * g, 128)]
+        sends.append(pltpu.make_async_copy(taps.at[g], there, sent.at[18 if g else 16]))
+        sends[-1].start()
     for send in sends:
         send.wait()
-    last.wait()
 
 
 def taps_sum(products, a, sign):
@@ -262,9 +262,9 @@
             pltpu.VMEM((16, OWN, 256), BF),
             pltpu.VMEM((OWN, CELLS), BF),
             pltpu.VMEM((2, OWN, TAPS_AT), BF),
-            pltpu.VMEM((16, OWN, 256), BF),
+            pltpu.VMEM((2, 16, OWN, 128), BF),
             pltpu.SemaphoreType.DMA((3,)),
-            pltpu.SemaphoreType.DMA((18,)),
+            pltpu.SemaphoreType.DMA((19,)),
         ],
         moved=1 << 20,
         limit=PACK_LIMIT,

time: 80 us -> 80 us (level)
  no operation moved by 1% of the time
where the time goes in v13:
time: 80 us; the launch traced here: 79.3 us
  starting transfers between devices  46.7 us (58%)
  waiting for transfers between devices  24.1 us (30%)
  Pallas kernels  5.54 us (7%)
  local copies, waits for them, and re-layouts  1.38 us (2%)
  between operations  0.83 us (1%)
  other arithmetic  0.81 us (1%)
    all_to_all x1, waiting for transfers between devices, per_device(): gathered = lax.all_to_all(packed, chan, 0, 0).reshape(256, WIDE)  15.2 us
    all_to_all x1, starting transfers between devices, per_device(): gathered = lax.all_to_all(packed, chan, 0, 0).reshape(256, WIDE)  12 us
    all_to_all x2, starting transfers between devices, spread(): return lax.all_to_all(many, axes, 0, 0).astype(F32)  11.8 us
    all_to_all x1, starting transfers between devices, per_device(): lax.all_to_all(own_grad.astype(HALF), ('core', 'near'), 0, 0).astype(F32)  6.91 us
    all_to_all x2, waiting for transfers between devices, spread(): return lax.all_to_all(many, axes, 0, 0).astype(F32)  5.55 us
    ppermute x1, starting transfers between devices, per_device(): from_far = lax.ppermute(to_far, space, across)  3.03 us
    ppermute x1, starting transfers between devices, per_device(): below = lax.ppermute(own_cot, space, up)  3.02 us
    ppermute x1, starting transfers between devices, per_device(): above = lax.ppermute(own_cot, space, down)  2.86 us
  transfers between devices with their start and end apart: 10, of which 6 were waited for; matrix products, arithmetic and copies ran while one was open for 2% of the time, Pallas kernels for 3%

profile of v13, /device:TPU:1, one launch (start us, length us, event | category | flops | bytes accessed | tf_op | source)
XLA Modules:
  0.0 79.3 jit_solution(14065452769118755606)
XLA Ops:
  0.6 2.1 %shard_map.58 = (bf16[16,16,1792]{2,1,0:T(8,128)(2,1)}, bf16[16,1024]{1,0:T(8,128)(2,1)}) custom-call(s32[1]{0:T(128)} %bitcast.core_at.core, s32[1]{0:T(128)} %bitcast.1.side_at, bf16[16,2,4,128]{3,2,1,0:T(4,128)(2,1)} %field_far.1, bf16[16,2,4,128]{3,2,1,0:T(4,128)(2,1)} %cot_far.1, bf16[27,16,256]{2,1,0:T(8,128)(2,1)} %filters.1), custom_call_target="tpu_custom_call" | custom-call | bytes 1048576 | tf_op jit(solution)/shard_map/pallas_call | solution.py:255
  2.7 0.0 copy-start.1
  2.7 12.0 %all-to-all-start = ((bf16[16,16,1792]{2,1,0:T(8,128)(2,1)}), bf16[16,16,1792]{2,1,0:T(8,128)(2,1)S(1)}, u32[]{:S(2)}, u32[]{:S(2)}) async-start(bf16[16,16,1792]{2,1,0:T(8,128)(2,1)} %get-tuple-element.12), calls=%async_computation | async-start | bytes 1835008 | tf_op jit(solution)/shard_map/all_to_all | solution.py:273
  14.7 0.0 copy-done.1
  14.8 2.9 %collective-permute-start.1 = (bf16[16,1024]{1,0:T(8,128)(2,1)S(1)}, bf16[16,1024]{1,0:T(8,128)(2,1)S(1)}, u32[]{:S(2)}, u32[]{:S(2)}) collective-permute-start(bf16[16,1024]{1,0:T(8,128)(2,1)S(1)} %copy-done.1), channel_id=1, source_target_pairs={{16,0},{32,16},{48,32},{64,48},{80,64},{96,80},{112,96},{128,112},... | collective-permute-start | bytes 98312 | tf_op jit(solution)/shard_map/ppermute | solution.py:275
  17.6 3.0 %collective-permute-start = (bf16[16,1024]{1,0:T(8,128)(2,1)S(1)}, bf16[16,1024]{1,0:T(8,128)(2,1)S(1)}, u32[]{:S(2)}, u32[]{:S(2)}) collective-permute-start(bf16[16,1024]{1,0:T(8,128)(2,1)S(1)} %copy-done.1), channel_id=1, source_target_pairs={{0,16},{16,32},{32,48},{48,64},{64,80},{80,96},{96,112},{112,128},... | collective-permute-start | bytes 98312 | tf_op jit(solution)/shard_map/ppermute | solution.py:274
  20.7 0.0 collective-permute-done.1.above
  20.7 1.0 %collective-permute-done.below = bf16[16,1024]{1,0:T(8,128)(2,1)S(1)} collective-permute-done((bf16[16,1024]{1,0:T(8,128)(2,1)S(1)}, bf16[16,1024]{1,0:T(8,128)(2,1)S(1)}, u32[]{:S(2)}, u32[]{:S(2)}) %collective-permute-start) | collective-permute-done | bytes 32800 | tf_op jit(solution)/shard_map/ppermute | solution.py:274
  21.7 0.1 shard_map.59.shifted
  21.8 15.2 %all-to-all-done = bf16[16,16,1792]{2,1,0:T(8,128)(2,1)S(1)} async-done(((bf16[16,16,1792]{2,1,0:T(8,128)(2,1)}), bf16[16,16,1792]{2,1,0:T(8,128)(2,1)S(1)}, u32[]{:S(2)}, u32[]{:S(2)}) %all-to-all-start) | async-done | bytes 917536 | tf_op jit(solution)/shard_map/all_to_all | solution.py:273
  37.0 0.6 shard_map.60._after
  37.6 0.7 convert_element_type.18
  38.3 6.9 %all-to-all-start.1 = ((f16[8,56,256]{2,1,0:T(8,128)(2,1)}), f16[8,56,256]{2,1,0:T(8,128)(2,1)S(1)}, u32[]{:S(2)}, u32[]{:S(2)}) async-start(f16[8,56,256]{2,1,0:T(8,128)(2,1)} %convert_element_type.18), calls=%async_computation.1 | async-start | bytes 458752 | tf_op jit(solution)/shard_map/all_to_all | solution.py:292
  45.3 2.8 %collective-permute-start.3 = (bf16[256,512]{1,0:T(8,128)(2,1)S(1)}, bf16[256,512]{1,0:T(8,128)(2,1)S(1)}, u32[]{:S(2)}, u32[]{:S(2)}) collective-permute-start(bf16[256,512]{1,0:T(8,128)(2,1)S(1)} %get-tuple-element.15), channel_id=1, source_target_pairs={{0,8},{8,0},{1,9},{9,1},{2,10},{10,2},{3,11},{11,3},{4,12},{12,4},... | collective-permute-start | bytes 786440 | tf_op jit(solution)/shard_map/ppermute | solution.py:290
  48.1 2.2 %collective-permute-start.2 = (bf16[256,256]{1,0:T(8,128)(2,1)S(1)}, bf16[256,256]{1,0:T(8,128)(2,1)S(1)}, u32[]{:S(2)}, u32[]{:S(2)}) collective-permute-start(bf16[256,256]{1,0:T(8,128)(2,1)S(1)} %get-tuple-element.14), channel_id=1, source_target_pairs={{0,16},{16,0},{1,17},{17,1},{2,18},{18,2},{3,19},{19,3},{4,20},{20... | collective-permute-start | bytes 393224 | tf_op jit(solution)/shard_map/ppermute | solution.py:291
  50.3 1.1 %all-to-all-done.1 = f16[8,56,256]{2,1,0:T(8,128)(2,1)S(1)} async-done(((f16[8,56,256]{2,1,0:T(8,128)(2,1)}), f16[8,56,256]{2,1,0:T(8,128)(2,1)S(1)}, u32[]{:S(2)}, u32[]{:S(2)}) %all-to-all-start.1) | async-done | bytes 229408 | tf_op jit(solution)/shard_map/all_to_all | solution.py:292
  51.5 0.2 shard_map.65
  51.7 0.0 copy-start
  51.7 0.7 broadcast_in_dim.4
  52.3 5.9 %all-to-all-start.2 = ((f16[4,56,256]{2,1,0:T(8,128)(2,1)}), f16[4,56,256]{2,1,0:T(8,128)(2,1)S(1)}, u32[]{:S(2)}, u32[]{:S(2)}) async-start(f16[4,56,256]{2,1,0:T(8,128)(2,1)} %broadcast_in_dim.4), calls=%async_computation.2 | async-start | bytes 229376 | tf_op jit(solution)/shard_map/all_to_all | solution.py:311
  58.3 0.0 collective-permute-done.2.swapped
  58.3 0.0 collective-permute-done.3.halves
  58.3 0.0 copy-done
  58.3 0.7 shard_map.62
  59.0 3.0 %collective-permute-start.4 = (f32[32,1024]{1,0:T(8,128)S(1)}, f32[32,1024]{1,0:T(8,128)S(1)}, u32[]{:S(2)}, u32[]{:S(2)}) collective-permute-start(f32[32,1024]{1,0:T(8,128)S(1)} %get-tuple-element.17), channel_id=1, source_target_pairs={{16,32},{32,16},{48,64},{64,48},{80,96},{96,80},{112,128},{128,112... | collective-permute-start | bytes 393224 | tf_op jit(solution)/shard_map/ppermute | solution.py:301
  62.1 3.4 %all-to-all-done.2 = f16[4,56,256]{2,1,0:T(8,128)(2,1)S(1)} async-done(((f16[4,56,256]{2,1,0:T(8,128)(2,1)}), f16[4,56,256]{2,1,0:T(8,128)(2,1)S(1)}, u32[]{:S(2)}, u32[]{:S(2)}) %all-to-all-start.2) | async-done | bytes 114720 | tf_op jit(solution)/shard_map/all_to_all | solution.py:311
  65.5 0.2 shard_map.66
  65.6 0.7 broadcast_in_dim.5
  66.3 5.9 %all-to-all-start.3 = ((f16[8,56,256]{2,1,0:T(8,128)(2,1)}), f16[8,56,256]{2,1,0:T(8,128)(2,1)S(1)}, u32[]{:S(2)}, u32[]{:S(2)}) async-start(f16[8,56,256]{2,1,0:T(8,128)(2,1)} %broadcast_in_dim.5), calls=%async_computation.3 | async-start | bytes 458752 | tf_op jit(solution)/shard_map/all_to_all | solution.py:311
  72.3 2.0 %collective-permute-start.5 = (f32[32,1024]{1,0:T(8,128)S(1)}, f32[32,1024]{1,0:T(8,128)S(1)}, u32[]{:S(2)}, u32[]{:S(2)}) collective-permute-start(f32[32,1024]{1,0:T(8,128)S(1)} %get-tuple-element.18), channel_id=1, source_target_pairs={{0,16},{16,0},{1,17},{17,1},{2,18},{18,2},{3,19},{19,3},{4,20},{20... | collective-permute-start | bytes 393224 | tf_op jit(solution)/shard_map/ppermute | solution.py:315
  74.3 0.0 collective-permute-done.4.far
  74.3 1.2 %collective-permute-done.5.near = f32[32,1024]{1,0:T(8,128)S(1)} collective-permute-done((f32[32,1024]{1,0:T(8,128)S(1)}, f32[32,1024]{1,0:T(8,128)S(1)}, u32[]{:S(2)}, u32[]{:S(2)}) %collective-permute-start.5) | collective-permute-done | bytes 131104 | tf_op jit(solution)/shard_map/ppermute | solution.py:315
  75.5 0.8 %shard_map.64 = (bf16[16,2,4,128]{3,2,1,0:T(4,128)(2,1)}, bf16[16,2,4,128]{3,2,1,0:T(4,128)(2,1)}) custom-call(f32[32,1024]{1,0:T(8,128)S(1)} %shard_map.63.own, f32[32,1024]{1,0:T(8,128)S(1)} %collective-permute-done.5.near), custom_call_target="tpu_custom_call" | custom-call | bytes 262144 | tf_op jit(solution)/shard_map/pallas_call | solution.py:328
  76.3 2.2 %all-to-all-done.3 = f16[8,56,256]{2,1,0:T(8,128)(2,1)S(1)} async-done(((f16[8,56,256]{2,1,0:T(8,128)(2,1)}), f16[8,56,256]{2,1,0:T(8,128)(2,1)S(1)}, u32[]{:S(2)}, u32[]{:S(2)}) %all-to-all-start.3) | async-done | bytes 229408 | tf_op jit(solution)/shard_map/all_to_all | solution.py:311
  78.5 0.8 %shard_map.67 = f32[432,256]{1,0:T(8,128)} custom-call(f32[8,56,256]{2,1,0:T(8,128)S(1)} %convert_element_type.23.full), custom_call_target="tpu_custom_call" | custom-call | bytes 1048576 | tf_op jit(solution)/shard_map/pallas_call | solution.py:317
  (7 shorter events, 0.1 us)
Async XLA Ops:
  2.7 12.0 %copy-start.1 = (bf16[16,1024]{1,0:T(8,128)(2,1)S(1)}, bf16[16,1024]{1,0:T(8,128)(2,1)}, u32[]{:S(2)}) copy-start(bf16[16,1024]{1,0:T(8,128)(2,1)} %get-tuple-element.13.own) | copy-start | bytes 98308
  2.7 34.2 %all-to-all-start = ((bf16[16,16,1792]{2,1,0:T(8,128)(2,1)}), bf16[16,16,1792]{2,1,0:T(8,128)(2,1)S(1)}, u32[]{:S(2)}, u32[]{:S(2)}) async-start(bf16[16,16,1792]{2,1,0:T(8,128)(2,1)} %get-tuple-element.12), calls=%async_computation | async-start | bytes 1835008 | tf_op jit(solution)/shard_map/all_to_all | solution.py:273
  14.8 5.9 %collective-permute-start.1 = (bf16[16,1024]{1,0:T(8,128)(2,1)S(1)}, bf16[16,1024]{1,0:T(8,128)(2,1)S(1)}, u32[]{:S(2)}, u32[]{:S(2)}) collective-permute-start(bf16[16,1024]{1,0:T(8,128)(2,1)S(1)} %copy-done.1), channel_id=1, source_target_pairs={{16,0},{32,16},{48,32},{64,48},{80,64},{96,80},{112,96},{128,112},... | collective-permute-start | bytes 98312 | tf_op jit(solution)/shard_map/ppermute | solution.py:275
  17.6 4.0 %collective-permute-start = (bf16[16,1024]{1,0:T(8,128)(2,1)S(1)}, bf16[16,1024]{1,0:T(8,128)(2,1)S(1)}, u32[]{:S(2)}, u32[]{:S(2)}) collective-permute-start(bf16[16,1024]{1,0:T(8,128)(2,1)S(1)} %copy-done.1), channel_id=1, source_target_pairs={{0,16},{16,32},{32,48},{48,64},{64,80},{80,96},{96,112},{112,128},... | collective-permute-start | bytes 98312 | tf_op jit(solution)/shard_map/ppermute | solution.py:274
  38.3 13.1 %all-to-all-start.1 = ((f16[8,56,256]{2,1,0:T(8,128)(2,1)}), f16[8,56,256]{2,1,0:T(8,128)(2,1)S(1)}, u32[]{:S(2)}, u32[]{:S(2)}) async-start(f16[8,56,256]{2,1,0:T(8,128)(2,1)} %convert_element_type.18), calls=%async_computation.1 | async-start | bytes 458752 | tf_op jit(solution)/shard_map/all_to_all | solution.py:292
  45.3 13.0 %collective-permute-start.3 = (bf16[256,512]{1,0:T(8,128)(2,1)S(1)}, bf16[256,512]{1,0:T(8,128)(2,1)S(1)}, u32[]{:S(2)}, u32[]{:S(2)}) collective-permute-start(bf16[256,512]{1,0:T(8,128)(2,1)S(1)} %get-tuple-element.15), channel_id=1, source_target_pairs={{0,8},{8,0},{1,9},{9,1},{2,10},{10,2},{3,11},{11,3},{4,12},{12,4},... | collective-permute-start | bytes 786440 | tf_op jit(solution)/shard_map/ppermute | solution.py:290
  48.1 10.2 %collective-permute-start.2 = (bf16[256,256]{1,0:T(8,128)(2,1)S(1)}, bf16[256,256]{1,0:T(8,128)(2,1)S(1)}, u32[]{:S(2)}, u32[]{:S(2)}) collective-permute-start(bf16[256,256]{1,0:T(8,128)(2,1)S(1)} %get-tuple-element.14), channel_id=1, source_target_pairs={{0,16},{16,0},{1,17},{17,1},{2,18},{18,2},{3,19},{19,3},{4,20},{20... | collective-permute-start | bytes 393224 | tf_op jit(solution)/shard_map/ppermute | solution.py:291
  51.7 6.6 %copy-start = (bf16[27,16,256]{2,1,0:T(8,128)(2,1)S(1)}, bf16[27,16,256]{2,1,0:T(8,128)(2,1)}, u32[]{:S(2)}) copy-start(bf16[27,16,256]{2,1,0:T(8,128)(2,1)} %filters.1) | copy-start | bytes 663556
  52.3 13.1 %all-to-all-start.2 = ((f16[4,56,256]{2,1,0:T(8,128)(2,1)}), f16[4,56,256]{2,1,0:T(8,128)(2,1)S(1)}, u32[]{:S(2)}, u32[]{:S(2)}) async-start(f16[4,56,256]{2,1,0:T(8,128)(2,1)} %broadcast_in_dim.4), calls=%async_computation.2 | async-start | bytes 229376 | tf_op jit(solution)/shard_map/all_to_all | solution.py:311
  59.0 15.3 %collective-permute-start.4 = (f32[32,1024]{1,0:T(8,128)S(1)}, f32[32,1024]{1,0:T(8,128)S(1)}, u32[]{:S(2)}, u32[]{:S(2)}) collective-permute-start(f32[32,1024]{1,0:T(8,128)S(1)} %get-tuple-element.17), channel_id=1, source_target_pairs={{16,32},{32,16},{48,64},{64,48},{80,96},{96,80},{112,128},{128,112... | collective-permute-start | bytes 393224 | tf_op jit(solution)/shard_map/ppermute | solution.py:301
  66.3 12.1 %all-to-all-start.3 = ((f16[8,56,256]{2,1,0:T(8,128)(2,1)}), f16[8,56,256]{2,1,0:T(8,128)(2,1)S(1)}, u32[]{:S(2)}, u32[]{:S(2)}) async-start(f16[8,56,256]{2,1,0:T(8,128)(2,1)} %broadcast_in_dim.5), calls=%async_computation.3 | async-start | bytes 458752 | tf_op jit(solution)/shard_map/all_to_all | solution.py:311
  72.3 3.2 %collective-permute-start.5 = (f32[32,1024]{1,0:T(8,128)S(1)}, f32[32,1024]{1,0:T(8,128)S(1)}, u32[]{:S(2)}, u32[]{:S(2)}) collective-permute-start(f32[32,1024]{1,0:T(8,128)S(1)} %get-tuple-element.18), channel_id=1, source_target_pairs={{0,16},{16,0},{1,17},{17,1},{2,18},{18,2},{3,19},{19,3},{4,20},{20... | collective-permute-start | bytes 393224 | tf_op jit(solution)/shard_map/ppermute | solution.py:315

commit v14 on v12

--- a/solution.py
+++ b/solution.py
@@ -102,12 +102,12 @@
                     turned = block if step == 0 else pltpu.roll(block, step, 1)
                     parts[8 * h + q] = jnp.where(here, turned, parts[8 * h + q])
         for c in range(16):
-            taps[c, :, 128 * g : 128 * g + 128] = parts[c].astype(BF)
-    last = pltpu.make_async_copy(taps, out.at[:, :, pl.ds(TAPS_AT, 256)], sent.at[16])
-    last.start()
+            taps[g, c] = parts[c].astype(BF)
+        there = out.at[:, :, pl.ds(TAPS_AT + 128 * g, 128)]
+        sends.append(pltpu.make_async_copy(taps.at[g], there, sent.at[18 if g else 16]))
+        sends[-1].start()
     for send in sends:
         send.wait()
-    last.wait()
 
 
 def taps_sum(products, a, sign):
@@ -263,9 +263,9 @@
             pltpu.VMEM((16, OWN, 256), BF),
             pltpu.VMEM((OWN, CELLS), BF),
             pltpu.VMEM((2, OWN, TAPS_AT), BF),
-            pltpu.VMEM((16, OWN, 256), BF),
+            pltpu.VMEM((2, 16, OWN, 128), BF),
             pltpu.SemaphoreType.DMA((3,)),
-            pltpu.SemaphoreType.DMA((18,)),
+            pltpu.SemaphoreType.DMA((19,)),
         ],
         moved=1 << 20,
         limit=PACK_LIMIT,

time: 80.1 us -> 80.1 us (level)
  no operation moved by 1% of the time
where the time goes in v14:
time: 80.1 us; the launch traced here: 79.4 us
  starting transfers between devices  46.7 us (58%)
  waiting for transfers between devices  24.1 us (30%)
  Pallas kernels  5.59 us (7%)
  other arithmetic  2.17 us (3%)
  between operations  0.81 us (1%)
    all_to_all x1, waiting for transfers between devices, per_device(): gathered = lax.all_to_all(packed, chan, 0, 0).reshape(256, WIDE)  15.2 us
    all_to_all x1, starting transfers between devices, per_device(): gathered = lax.all_to_all(packed, chan, 0, 0).reshape(256, WIDE)  12 us
    all_to_all x2, starting transfers between devices, spread(): return lax.all_to_all(many.astype(HALF), axes, 0, 0).astype(F32)  11.8 us
    all_to_all x1, starting transfers between devices, per_device(): lax.all_to_all(own_grad.astype(HALF), ('core', 'near'), 0, 0).astype(F32)  6.91 us
    all_to_all x2, waiting for transfers between devices, spread(): return lax.all_to_all(many.astype(HALF), axes, 0, 0).astype(F32)  5.55 us
    ppermute x1, starting transfers between devices, per_device(): from_far = lax.ppermute(to_far, space, across)  3.03 us
    ppermute x1, starting transfers between devices, per_device(): below = lax.ppermute(own_cot, space, up)  3.02 us
    ppermute x1, starting transfers between devices, per_device(): above = lax.ppermute(own_cot, space, down)  2.86 us
  transfers between devices with their start and end apart: 10, of which 6 were waited for; matrix products, arithmetic and copies ran while one was open for 2% of the time, Pallas kernels for 3%

profile of v14, /device:TPU:1, one launch (start us, length us, event | category | flops | bytes accessed | tf_op | source)
XLA Modules:
  0.0 79.4 jit_solution(422684126326175250)
XLA Ops:
  0.6 2.1 %shard_map.58 = (bf16[16,16,1792]{2,1,0:T(8,128)(2,1)}, bf16[16,1024]{1,0:T(8,128)(2,1)}) custom-call(s32[1]{0:T(128)} %bitcast.core_at.core, s32[1]{0:T(128)} %bitcast.1.side_at, bf16[16,2,4,128]{3,2,1,0:T(4,128)(2,1)} %field_far.1, bf16[16,2,4,128]{3,2,1,0:T(4,128)(2,1)} %cot_far.1, bf16[27,16,256]{2,1,0:T(8,128)(2,1)} %filters.1), custom_call_target="tpu_custom_call" | custom-call | bytes 1048576 | tf_op jit(solution)/shard_map/pallas_call | solution.py:256
  2.7 0.0 copy-start.1
  2.7 12.0 %all-to-all-start = ((bf16[16,16,1792]{2,1,0:T(8,128)(2,1)}), bf16[16,16,1792]{2,1,0:T(8,128)(2,1)S(1)}, u32[]{:S(2)}, u32[]{:S(2)}) async-start(bf16[16,16,1792]{2,1,0:T(8,128)(2,1)} %get-tuple-element.12), calls=%async_computation | async-start | bytes 1835008 | tf_op jit(solution)/shard_map/all_to_all | solution.py:274
  14.7 0.0 copy-done.1
  14.8 2.9 %collective-permute-start.1 = (bf16[16,1024]{1,0:T(8,128)(2,1)S(1)}, bf16[16,1024]{1,0:T(8,128)(2,1)S(1)}, u32[]{:S(2)}, u32[]{:S(2)}) collective-permute-start(bf16[16,1024]{1,0:T(8,128)(2,1)S(1)} %copy-done.1), channel_id=1, source_target_pairs={{16,0},{32,16},{48,32},{64,48},{80,64},{96,80},{112,96},{128,112},... | collective-permute-start | bytes 98312 | tf_op jit(solution)/shard_map/ppermute | solution.py:276
  17.6 3.0 %collective-permute-start = (bf16[16,1024]{1,0:T(8,128)(2,1)S(1)}, bf16[16,1024]{1,0:T(8,128)(2,1)S(1)}, u32[]{:S(2)}, u32[]{:S(2)}) collective-permute-start(bf16[16,1024]{1,0:T(8,128)(2,1)S(1)} %copy-done.1), channel_id=1, source_target_pairs={{0,16},{16,32},{32,48},{48,64},{64,80},{80,96},{96,112},{112,128},... | collective-permute-start | bytes 98312 | tf_op jit(solution)/shard_map/ppermute | solution.py:275
  20.7 0.0 collective-permute-done.1.above
  20.7 1.0 %collective-permute-done.below = bf16[16,1024]{1,0:T(8,128)(2,1)S(1)} collective-permute-done((bf16[16,1024]{1,0:T(8,128)(2,1)S(1)}, bf16[16,1024]{1,0:T(8,128)(2,1)S(1)}, u32[]{:S(2)}, u32[]{:S(2)}) %collective-permute-start) | collective-permute-done | bytes 32800 | tf_op jit(solution)/shard_map/ppermute | solution.py:275
  21.7 0.1 shard_map.59.shifted
  21.8 15.2 %all-to-all-done = bf16[16,16,1792]{2,1,0:T(8,128)(2,1)S(1)} async-done(((bf16[16,16,1792]{2,1,0:T(8,128)(2,1)}), bf16[16,16,1792]{2,1,0:T(8,128)(2,1)S(1)}, u32[]{:S(2)}, u32[]{:S(2)}) %all-to-all-start) | async-done | bytes 917536 | tf_op jit(solution)/shard_map/all_to_all | solution.py:274
  37.0 0.6 shard_map.60._after
  37.6 0.7 convert_element_type.18
  38.3 6.9 %all-to-all-start.1 = ((f16[8,56,256]{2,1,0:T(8,128)(2,1)}), f16[8,56,256]{2,1,0:T(8,128)(2,1)S(1)}, u32[]{:S(2)}, u32[]{:S(2)}) async-start(f16[8,56,256]{2,1,0:T(8,128)(2,1)} %convert_element_type.18), calls=%async_computation.1 | async-start | bytes 458752 | tf_op jit(solution)/shard_map/all_to_all | solution.py:293
  45.3 2.8 %collective-permute-start.3 = (bf16[256,512]{1,0:T(8,128)(2,1)S(1)}, bf16[256,512]{1,0:T(8,128)(2,1)S(1)}, u32[]{:S(2)}, u32[]{:S(2)}) collective-permute-start(bf16[256,512]{1,0:T(8,128)(2,1)S(1)} %get-tuple-element.15), channel_id=1, source_target_pairs={{0,8},{8,0},{1,9},{9,1},{2,10},{10,2},{3,11},{11,3},{4,12},{12,4},... | collective-permute-start | bytes 786440 | tf_op jit(solution)/shard_map/ppermute | solution.py:291
  48.1 2.2 %collective-permute-start.2 = (bf16[256,256]{1,0:T(8,128)(2,1)S(1)}, bf16[256,256]{1,0:T(8,128)(2,1)S(1)}, u32[]{:S(2)}, u32[]{:S(2)}) collective-permute-start(bf16[256,256]{1,0:T(8,128)(2,1)S(1)} %get-tuple-element.14), channel_id=1, source_target_pairs={{0,16},{16,0},{1,17},{17,1},{2,18},{18,2},{3,19},{19,3},{4,20},{20... | collective-permute-start | bytes 393224 | tf_op jit(solution)/shard_map/ppermute | solution.py:292
  50.3 1.1 %all-to-all-done.1 = f16[8,56,256]{2,1,0:T(8,128)(2,1)S(1)} async-done(((f16[8,56,256]{2,1,0:T(8,128)(2,1)}), f16[8,56,256]{2,1,0:T(8,128)(2,1)S(1)}, u32[]{:S(2)}, u32[]{:S(2)}) %all-to-all-start.1) | async-done | bytes 229408 | tf_op jit(solution)/shard_map/all_to_all | solution.py:293
  51.5 0.2 shard_map.65
  51.7 0.0 copy-start
  51.7 0.7 convert_element_type.20
  52.3 5.9 %all-to-all-start.2 = ((f16[4,56,256]{2,1,0:T(8,128)(2,1)}), f16[4,56,256]{2,1,0:T(8,128)(2,1)S(1)}, u32[]{:S(2)}, u32[]{:S(2)}) async-start(f16[4,56,256]{2,1,0:T(8,128)(2,1)} %convert_element_type.20), calls=%async_computation.2 | async-start | bytes 229376 | tf_op jit(solution)/shard_map/all_to_all | solution.py:310
  58.3 0.0 collective-permute-done.2.swapped
  58.3 0.0 collective-permute-done.3.halves
  58.3 0.0 copy-done
  58.3 0.7 shard_map.62
  59.0 3.0 %collective-permute-start.4 = (f32[32,1024]{1,0:T(8,128)S(1)}, f32[32,1024]{1,0:T(8,128)S(1)}, u32[]{:S(2)}, u32[]{:S(2)}) collective-permute-start(f32[32,1024]{1,0:T(8,128)S(1)} %get-tuple-element.17), channel_id=1, source_target_pairs={{16,32},{32,16},{48,64},{64,48},{80,96},{96,80},{112,128},{128,112... | collective-permute-start | bytes 393224 | tf_op jit(solution)/shard_map/ppermute | solution.py:302
  62.1 3.4 %all-to-all-done.2 = f16[4,56,256]{2,1,0:T(8,128)(2,1)S(1)} async-done(((f16[4,56,256]{2,1,0:T(8,128)(2,1)}), f16[4,56,256]{2,1,0:T(8,128)(2,1)S(1)}, u32[]{:S(2)}, u32[]{:S(2)}) %all-to-all-start.2) | async-done | bytes 114720 | tf_op jit(solution)/shard_map/all_to_all | solution.py:310
  65.5 0.2 shard_map.66
  65.7 0.7 convert_element_type.22
  66.4 5.9 %all-to-all-start.3 = ((f16[8,56,256]{2,1,0:T(8,128)(2,1)}), f16[8,56,256]{2,1,0:T(8,128)(2,1)S(1)}, u32[]{:S(2)}, u32[]{:S(2)}) async-start(f16[8,56,256]{2,1,0:T(8,128)(2,1)} %convert_element_type.22), calls=%async_computation.3 | async-start | bytes 458752 | tf_op jit(solution)/shard_map/all_to_all | solution.py:310
  72.3 2.0 %collective-permute-start.5 = (f32[32,1024]{1,0:T(8,128)S(1)}, f32[32,1024]{1,0:T(8,128)S(1)}, u32[]{:S(2)}, u32[]{:S(2)}) collective-permute-start(f32[32,1024]{1,0:T(8,128)S(1)} %get-tuple-element.18), channel_id=1, source_target_pairs={{0,16},{16,0},{1,17},{17,1},{2,18},{18,2},{3,19},{19,3},{4,20},{20... | collective-permute-start | bytes 393224 | tf_op jit(solution)/shard_map/ppermute | solution.py:314
  74.3 0.0 collective-permute-done.4.far
  74.3 1.2 %collective-permute-done.5.near = f32[32,1024]{1,0:T(8,128)S(1)} collective-permute-done((f32[32,1024]{1,0:T(8,128)S(1)}, f32[32,1024]{1,0:T(8,128)S(1)}, u32[]{:S(2)}, u32[]{:S(2)}) %collective-permute-start.5) | collective-permute-done | bytes 131104 | tf_op jit(solution)/shard_map/ppermute | solution.py:314
  75.5 0.8 %shard_map.64 = (bf16[16,2,4,128]{3,2,1,0:T(4,128)(2,1)}, bf16[16,2,4,128]{3,2,1,0:T(4,128)(2,1)}) custom-call(f32[32,1024]{1,0:T(8,128)S(1)} %shard_map.63.own, f32[32,1024]{1,0:T(8,128)S(1)} %collective-permute-done.5.near), custom_call_target="tpu_custom_call" | custom-call | bytes 262144 | tf_op jit(solution)/shard_map/pallas_call | solution.py:327
  76.3 2.2 %all-to-all-done.3 = f16[8,56,256]{2,1,0:T(8,128)(2,1)S(1)} async-done(((f16[8,56,256]{2,1,0:T(8,128)(2,1)}), f16[8,56,256]{2,1,0:T(8,128)(2,1)S(1)}, u32[]{:S(2)}, u32[]{:S(2)}) %all-to-all-start.3) | async-done | bytes 229408 | tf_op jit(solution)/shard_map/all_to_all | solution.py:310
  78.5 0.8 %shard_map.67 = f32[432,256]{1,0:T(8,128)} custom-call(f32[8,56,256]{2,1,0:T(8,128)S(1)} %convert_element_type.23.full), custom_call_target="tpu_custom_call" | custom-call | bytes 1048576 | tf_op jit(solution)/shard_map/pallas_call | solution.py:316
  (5 shorter events, 0.1 us)
Async XLA Ops:
  2.7 12.0 %copy-start.1 = (bf16[16,1024]{1,0:T(8,128)(2,1)S(1)}, bf16[16,1024]{1,0:T(8,128)(2,1)}, u32[]{:S(2)}) copy-start(bf16[16,1024]{1,0:T(8,128)(2,1)} %get-tuple-element.13.own) | copy-start | bytes 98308
  2.7 34.2 %all-to-all-start = ((bf16[16,16,1792]{2,1,0:T(8,128)(2,1)}), bf16[16,16,1792]{2,1,0:T(8,128)(2,1)S(1)}, u32[]{:S(2)}, u32[]{:S(2)}) async-start(bf16[16,16,1792]{2,1,0:T(8,128)(2,1)} %get-tuple-element.12), calls=%async_computation | async-start | bytes 1835008 | tf_op jit(solution)/shard_map/all_to_all | solution.py:274
  14.8 5.9 %collective-permute-start.1 = (bf16[16,1024]{1,0:T(8,128)(2,1)S(1)}, bf16[16,1024]{1,0:T(8,128)(2,1)S(1)}, u32[]{:S(2)}, u32[]{:S(2)}) collective-permute-start(bf16[16,1024]{1,0:T(8,128)(2,1)S(1)} %copy-done.1), channel_id=1, source_target_pairs={{16,0},{32,16},{48,32},{64,48},{80,64},{96,80},{112,96},{128,112},... | collective-permute-start | bytes 98312 | tf_op jit(solution)/shard_map/ppermute | solution.py:276
  17.6 4.0 %collective-permute-start = (bf16[16,1024]{1,0:T(8,128)(2,1)S(1)}, bf16[16,1024]{1,0:T(8,128)(2,1)S(1)}, u32[]{:S(2)}, u32[]{:S(2)}) collective-permute-start(bf16[16,1024]{1,0:T(8,128)(2,1)S(1)} %copy-done.1), channel_id=1, source_target_pairs={{0,16},{16,32},{32,48},{48,64},{64,80},{80,96},{96,112},{112,128},... | collective-permute-start | bytes 98312 | tf_op jit(solution)/shard_map/ppermute | solution.py:275
  38.3 13.1 %all-to-all-start.1 = ((f16[8,56,256]{2,1,0:T(8,128)(2,1)}), f16[8,56,256]{2,1,0:T(8,128)(2,1)S(1)}, u32[]{:S(2)}, u32[]{:S(2)}) async-start(f16[8,56,256]{2,1,0:T(8,128)(2,1)} %convert_element_type.18), calls=%async_computation.1 | async-start | bytes 458752 | tf_op jit(solution)/shard_map/all_to_all | solution.py:293
  45.3 13.0 %collective-permute-start.3 = (bf16[256,512]{1,0:T(8,128)(2,1)S(1)}, bf16[256,512]{1,0:T(8,128)(2,1)S(1)}, u32[]{:S(2)}, u32[]{:S(2)}) collective-permute-start(bf16[256,512]{1,0:T(8,128)(2,1)S(1)} %get-tuple-element.15), channel_id=1, source_target_pairs={{0,8},{8,0},{1,9},{9,1},{2,10},{10,2},{3,11},{11,3},{4,12},{12,4},... | collective-permute-start | bytes 786440 | tf_op jit(solution)/shard_map/ppermute | solution.py:291
  48.1 10.2 %collective-permute-start.2 = (bf16[256,256]{1,0:T(8,128)(2,1)S(1)}, bf16[256,256]{1,0:T(8,128)(2,1)S(1)}, u32[]{:S(2)}, u32[]{:S(2)}) collective-permute-start(bf16[256,256]{1,0:T(8,128)(2,1)S(1)} %get-tuple-element.14), channel_id=1, source_target_pairs={{0,16},{16,0},{1,17},{17,1},{2,18},{18,2},{3,19},{19,3},{4,20},{20... | collective-permute-start | bytes 393224 | tf_op jit(solution)/shard_map/ppermute | solution.py:292
  51.7 6.6 %copy-start = (bf16[27,16,256]{2,1,0:T(8,128)(2,1)S(1)}, bf16[27,16,256]{2,1,0:T(8,128)(2,1)}, u32[]{:S(2)}) copy-start(bf16[27,16,256]{2,1,0:T(8,128)(2,1)} %filters.1) | copy-start | bytes 663556
  52.3 13.1 %all-to-all-start.2 = ((f16[4,56,256]{2,1,0:T(8,128)(2,1)}), f16[4,56,256]{2,1,0:T(8,128)(2,1)S(1)}, u32[]{:S(2)}, u32[]{:S(2)}) async-start(f16[4,56,256]{2,1,0:T(8,128)(2,1)} %convert_element_type.20), calls=%async_computation.2 | async-start | bytes 229376 | tf_op jit(solution)/shard_map/all_to_all | solution.py:310
  59.0 15.3 %collective-permute-start.4 = (f32[32,1024]{1,0:T(8,128)S(1)}, f32[32,1024]{1,0:T(8,128)S(1)}, u32[]{:S(2)}, u32[]{:S(2)}) collective-permute-start(f32[32,1024]{1,0:T(8,128)S(1)} %get-tuple-element.17), channel_id=1, source_target_pairs={{16,32},{32,16},{48,64},{64,48},{80,96},{96,80},{112,128},{128,112... | collective-permute-start | bytes 393224 | tf_op jit(solution)/shard_map/ppermute | solution.py:302
  66.4 12.1 %all-to-all-start.3 = ((f16[8,56,256]{2,1,0:T(8,128)(2,1)}), f16[8,56,256]{2,1,0:T(8,128)(2,1)S(1)}, u32[]{:S(2)}, u32[]{:S(2)}) async-start(f16[8,56,256]{2,1,0:T(8,128)(2,1)} %convert_element_type.22), calls=%async_computation.3 | async-start | bytes 458752 | tf_op jit(solution)/shard_map/all_to_all | solution.py:310
  72.3 3.2 %collective-permute-start.5 = (f32[32,1024]{1,0:T(8,128)S(1)}, f32[32,1024]{1,0:T(8,128)S(1)}, u32[]{:S(2)}, u32[]{:S(2)}) collective-permute-start(f32[32,1024]{1,0:T(8,128)S(1)} %get-tuple-element.18), channel_id=1, source_target_pairs={{0,16},{16,0},{1,17},{17,1},{2,18},{18,2},{3,19},{19,3},{4,20},{20... | collective-permute-start | bytes 393224 | tf_op jit(solution)/shard_map/ppermute | solution.py:314
